TPU v7x, 32 devices: a whole 2x2x4 slice. The times are simulated.
32 devices in a mesh: dp: 16 (over z, y, core), tensor: 2 (over x).
Axes of the slice: x: 2, y: 2, z: 4, core: 2. Of those that a mesh axis runs over, the one named last changes fastest.
Arguments:
- residual_in: bfloat16 [4096, 2048], P(('dp', 'tensor')), may hold values from -6 to 6
- seg_ids: int32 [4096], P('dp'), may hold values from -1 to 2, as said below
- attn_gain: bfloat16 [2048], P('dp'), may hold values from 0.099609375 to 1.8984375
- w_qkv: bfloat16 [3, 2048, 2048], P(None, 'dp', 'tensor'), may hold values from -0.125 to 0.125
- w_out: bfloat16 [2048, 2048], P('tensor', 'dp'), may hold values from -2 to 2
- ffn_gain: bfloat16 [2048], P('dp'), may hold values from 0.099609375 to 1.8984375
- w_gate_up: bfloat16 [2, 2048, 8192], P(None, 'dp', 'tensor'), may hold values from -0.125 to 0.125
- w_down: bfloat16 [8192, 2048], P('tensor', 'dp'), may hold values from -0.0625 to 0.0625
- cotangent: bfloat16 [4096, 2048], P(('dp', 'tensor')), may hold values from -6 to 6
Outputs:
- block_out: bfloat16 [4096, 2048], P(('dp', 'tensor'))
- input_grad: float32 [4096, 2048], P(('dp', 'tensor'))
- attn_gain_grad: float32 [2048], P('dp')
- w_qkv_grad: float32 [3, 2048, 2048], P(None, 'dp', 'tensor')
- w_out_grad: float32 [2048, 2048], P('tensor', 'dp')
- ffn_gain_grad: float32 [2048], P('dp')
- w_gate_up_grad: float32 [2, 2048, 8192], P(None, 'dp', 'tensor')
- w_down_grad: float32 [8192, 2048], P('tensor', 'dp')
Inputs may be any that keep to these rules, and one draw needn't show every extreme that they name: `seg_ids`: each aligned group of 256 rows (the rows of one dp index) holds one to three sequences as runs of non-decreasing ids, followed by padding rows of -1 up to the group's end; a sequence always covers rows 127 and 128 of its group; in one group a single sequence fills all 256 rows.
All inputs are finite; a program needn't handle non-finite values.
Results may differ from a plain program's by a relative error of at most 0.012.
The roundings to bfloat16 on the way count: a program that leaves them out, or rounds other values in their place, can miss the bound.
Values may be sent and summed in bfloat16 or wider, within the bound.
A program may use at most 320 MiB of HBM per device.

v0:
```python
import jax
import jax.numpy as jnp
from jax import lax
from jax.sharding import PartitionSpec as P

HD = 64


EPSILON = 1e-05
ROPE_BASE = 130000.0


def positions(segments):
    row_index = jnp.arange(segments.shape[1], dtype=jnp.int32)[None, :]
    previous = jnp.concatenate([segments[:, :1] - 1, segments[:, :-1]], axis=1)
    run_start = lax.cummax(jnp.where(segments != previous, row_index, 0), axis=1)
    return row_index - run_start


def rope_tables(places, head_dim):
    half_dim = head_dim // 2
    frequency = ROPE_BASE ** (-(jnp.arange(half_dim, dtype=jnp.float32) * 2.0 / head_dim))
    angles = places.astype(jnp.float32)[:, None, None] * frequency[None, None, :]
    return (jnp.cos(angles), jnp.sin(angles))


def rotate(field, cosine, sine_table):
    half_dim = field.shape[-1] // 2
    lower_half = field[..., :half_dim]
    upper_half = field[..., half_dim:]
    return jnp.concatenate(
        [
            lower_half * cosine - upper_half * sine_table,
            upper_half * cosine + lower_half * sine_table,
        ],
        axis=-1,
    )


def unrotate(field, cosine, sine_table):
    half_dim = field.shape[-1] // 2
    lower_half = field[..., :half_dim]
    upper_half = field[..., half_dim:]
    return jnp.concatenate(
        [
            lower_half * cosine + upper_half * sine_table,
            upper_half * cosine - lower_half * sine_table,
        ],
        axis=-1,
    )


def attention_scores(queries, key_rows, allowed):
    scores = jnp.einsum(
        "qhd,khd->hqk", queries, key_rows, preferred_element_type=jnp.float32
    ) * queries.shape[-1] ** (-0.5)
    return jnp.where(allowed[None], scores, -1e30)


def shards(residual_in, seg_ids, attn_gain, w_qkv, w_out, ffn_gain, w_gate_up, w_down, cotangent):
    rows_local = residual_in.shape[0]
    group_rows = seg_ids.shape[0]
    offset = lax.axis_index("tensor") * rows_local
    live_rows = (lax.dynamic_slice_in_dim(seg_ids, offset, rows_local) >= 0).astype(jnp.float32)
    residual = residual_in.astype(jnp.float32)
    contract_rows = (((0,), (0,)), ((), ()))
    contract_cols = (((1,), (1,)), ((), ()))
    gain_attn, qkv_full, out_full = (
        lax.all_gather(attn_gain, "dp", axis=0, tiled=True),
        lax.all_gather(w_qkv, "dp", axis=1, tiled=True),
        lax.all_gather(w_out, "dp", axis=1, tiled=True),
    )
    norm_attn = lax.rsqrt(jnp.mean(residual * residual, axis=-1, keepdims=True) + EPSILON)
    unit_attn = residual * norm_attn
    normed = (unit_attn * gain_attn.astype(jnp.float32)).astype(jnp.bfloat16)
    normed_all = lax.all_gather(normed, "tensor", axis=0, tiled=True)
    projected = jnp.einsum("rd,cde->cre", normed_all, qkv_full, preferred_element_type=jnp.float32)
    head_count = qkv_full.shape[2] // HD
    head_shape = (group_rows, head_count, HD)
    cosine, sine_table = rope_tables(positions(seg_ids[None, :])[0], HD)
    queries = rotate(projected[0].reshape(head_shape), cosine, sine_table).astype(jnp.bfloat16)
    key_rows = rotate(projected[1].reshape(head_shape), cosine, sine_table).astype(jnp.bfloat16)
    value_rows = projected[2].reshape(head_shape).astype(jnp.bfloat16)
    row_index = jnp.arange(group_rows)
    allowed = (seg_ids[:, None] == seg_ids[None, :]) & (row_index[:, None] >= row_index[None, :])
    scores = attention_scores(queries, key_rows, allowed)
    row_top = jnp.max(scores, axis=-1, keepdims=True)
    log_total = row_top + jnp.log(jnp.sum(jnp.exp(scores - row_top), axis=-1, keepdims=True))
    weights = jnp.exp(scores - log_total).astype(jnp.bfloat16)
    attended = jnp.einsum("hqk,khd->qhd", weights, value_rows, preferred_element_type=jnp.float32)
    attended = attended.reshape(group_rows, head_count * HD).astype(jnp.bfloat16)
    mixed = residual + lax.psum_scatter(
        jnp.dot(attended, out_full, preferred_element_type=jnp.float32),
        "tensor",
        scatter_dimension=0,
        tiled=True,
    )
    gain_ffn, gate_up_full, down_full = (
        lax.all_gather(ffn_gain, "dp", axis=0, tiled=True),
        lax.all_gather(w_gate_up, "dp", axis=1, tiled=True),
        lax.all_gather(w_down, "dp", axis=1, tiled=True),
    )
    norm_ffn = lax.rsqrt(jnp.mean(mixed * mixed, axis=-1, keepdims=True) + EPSILON)
    unit_ffn = mixed * norm_ffn
    normed_ffn = (unit_ffn * gain_ffn.astype(jnp.float32)).astype(jnp.bfloat16)
    normed_ffn_all = lax.all_gather(normed_ffn, "tensor", axis=0, tiled=True)
    gate_up = jnp.einsum(
        "rd,cde->cre", normed_ffn_all, gate_up_full, preferred_element_type=jnp.float32
    )
    gate_pre = gate_up[0]
    up_pre = gate_up[1]
    sigmoid_gate = jax.nn.sigmoid(gate_pre)
    activated = gate_pre * sigmoid_gate
    hidden = (activated * up_pre).astype(jnp.bfloat16)
    output = mixed + lax.psum_scatter(
        jnp.dot(hidden, down_full, preferred_element_type=jnp.float32).astype(jnp.bfloat16),
        "tensor",
        scatter_dimension=0,
        tiled=True,
    ).astype(jnp.float32)
    grad_out = cotangent.astype(jnp.float32) * live_rows[:, None]
    grad_all = lax.all_gather(grad_out.astype(jnp.bfloat16), "tensor", axis=0, tiled=True)
    down_grad = lax.dot_general(hidden, grad_all, contract_rows, preferred_element_type=jnp.float32)
    hidden_grad = lax.dot_general(
        grad_all, down_full, contract_cols, preferred_element_type=jnp.float32
    )
    gate_grads = jnp.stack(
        [
            hidden_grad * up_pre * sigmoid_gate * (1.0 + gate_pre * (1.0 - sigmoid_gate)),
            hidden_grad * activated,
        ]
    ).astype(jnp.bfloat16)
    gate_up_grad = jnp.einsum(
        "rd,cre->cde", normed_ffn_all, gate_grads, preferred_element_type=jnp.float32
    )
    normed_ffn_grad = lax.psum_scatter(
        jnp.einsum("cre,cde->rd", gate_grads, gate_up_full, preferred_element_type=jnp.float32),
        "tensor",
        scatter_dimension=0,
        tiled=True,
    )
    ffn_gain_part = jnp.sum(normed_ffn_grad * unit_ffn, axis=0)
    scaled_ffn = normed_ffn_grad * gain_ffn.astype(jnp.float32)
    mixed_grad = grad_out + norm_ffn * (
        scaled_ffn - unit_ffn * jnp.mean(scaled_ffn * unit_ffn, axis=-1, keepdims=True)
    )
    mixed_all = lax.all_gather(mixed_grad.astype(jnp.bfloat16), "tensor", axis=0, tiled=True)
    out_grad = lax.dot_general(
        attended, mixed_all, contract_rows, preferred_element_type=jnp.float32
    )
    attended_grad = lax.dot_general(
        mixed_all, out_full, contract_cols, preferred_element_type=jnp.float32
    )
    attended_grad = attended_grad.astype(jnp.bfloat16).reshape(head_shape)
    probabilities = jnp.exp(attention_scores(queries, key_rows, allowed) - log_total)
    value_grad = jnp.einsum(
        "hqk,qhd->khd",
        probabilities.astype(jnp.bfloat16),
        attended_grad,
        preferred_element_type=jnp.float32,
    )
    prob_grad = jnp.einsum(
        "qhd,khd->hqk", attended_grad, value_rows, preferred_element_type=jnp.float32
    )
    score_grad = (
        probabilities * (prob_grad - jnp.sum(probabilities * prob_grad, axis=-1, keepdims=True))
    ).astype(jnp.bfloat16)
    scale_factor = HD ** (-0.5)
    query_grad = (
        jnp.einsum("hqk,khd->qhd", score_grad, key_rows, preferred_element_type=jnp.float32)
        * scale_factor
    )
    key_grad = (
        jnp.einsum("hqk,qhd->khd", score_grad, queries, preferred_element_type=jnp.float32)
        * scale_factor
    )
    qkv_grads = jnp.stack(
        [
            unrotate(query_grad, cosine, sine_table),
            unrotate(key_grad, cosine, sine_table),
            value_grad,
        ]
    )
    qkv_grads = qkv_grads.reshape(3, group_rows, head_count * HD).astype(jnp.bfloat16)
    qkv_grad = jnp.einsum("rd,cre->cde", normed_all, qkv_grads, preferred_element_type=jnp.float32)
    normed_grad = lax.psum_scatter(
        jnp.einsum("cre,cde->rd", qkv_grads, qkv_full, preferred_element_type=jnp.float32),
        "tensor",
        scatter_dimension=0,
        tiled=True,
    )
    attn_gain_part = jnp.sum(normed_grad * unit_attn, axis=0)
    scaled_attn = normed_grad * gain_attn.astype(jnp.float32)
    input_grad = mixed_grad + norm_attn * (
        scaled_attn - unit_attn * jnp.mean(scaled_attn * unit_attn, axis=-1, keepdims=True)
    )
    (
        query_total,
        key_total,
        value_total,
        out_total,
        attn_gain_total,
        gate_total,
        up_total,
        down_total,
        ffn_gain_total,
    ) = (
        lax.psum_scatter(qkv_grad[0], "dp", scatter_dimension=0, tiled=True),
        lax.psum_scatter(qkv_grad[1], "dp", scatter_dimension=0, tiled=True),
        lax.psum_scatter(qkv_grad[2], "dp", scatter_dimension=0, tiled=True),
        lax.psum_scatter(out_grad, "dp", scatter_dimension=1, tiled=True),
        lax.psum_scatter(attn_gain_part, "dp", scatter_dimension=0, tiled=True),
        lax.psum_scatter(gate_up_grad[0], "dp", scatter_dimension=0, tiled=True),
        lax.psum_scatter(gate_up_grad[1], "dp", scatter_dimension=0, tiled=True),
        lax.psum_scatter(down_grad, "dp", scatter_dimension=1, tiled=True),
        lax.psum_scatter(ffn_gain_part, "dp", scatter_dimension=0, tiled=True),
    )
    gate_up_total = jnp.stack([gate_total, up_total])
    qkv_total = jnp.stack([query_total, key_total, value_total])
    attn_gain_sum, ffn_gain_sum = lax.psum((attn_gain_total, ffn_gain_total), "tensor")
    return (
        output.astype(jnp.bfloat16),
        input_grad,
        attn_gain_sum,
        qkv_total,
        out_total,
        ffn_gain_sum,
        gate_up_total,
        down_total,
    )


def solution(mesh):
    in_specs = (
        P(("dp", "tensor"), None),
        P("dp"),
        P("dp"),
        P(None, "dp", "tensor"),
        P("tensor", "dp"),
        P("dp"),
        P(None, "dp", "tensor"),
        P("tensor", "dp"),
        P(("dp", "tensor"), None),
    )
    out_specs = (
        P(("dp", "tensor"), None),
        P(("dp", "tensor"), None),
        P("dp"),
        P(None, "dp", "tensor"),
        P("tensor", "dp"),
        P("dp"),
        P(None, "dp", "tensor"),
        P("tensor", "dp"),
    )
    return jax.shard_map(shards, mesh=mesh, in_specs=in_specs, out_specs=out_specs, check_vma=False)
```

profile of v0, /device:TPU:12, one launch (start us, length us, event | category | flops | bytes accessed | tf_op | source)
XLA Modules:
  0.0 2206.8 jit_solution(18164431720716108085)
XLA Ops:
  8.5 15.2 all-gather
  32.3 19.1 all-gather.11.cloned.1.call-done
  51.4 100.8 %all-gather.13.cloned.1.call-done = bf16[3,2048,1024]{2,1,0:T(8,128)(2,1)} async-done(((bf16[3,128,1024]{2,1,0:T(8,128)(2,1)}), bf16[3,2048,1024]{2,1,0:T(8,128)(2,1)}) %all-gather.13.cloned.1.call-update) | async-done | bytes 12582928 | tf_op jit(solution)/shard_map/all_gather | solution.py:70
  167.2 38.1 %all-gather.15.cloned.1.call-done = bf16[1024,2048]{1,0:T(8,128)(2,1)} async-done(((bf16[1024,128]{1,0:T(8,128)(2,1)}), bf16[1024,2048]{1,0:T(8,128)(2,1)}) %all-gather.15.cloned.1.call-update) | async-done | bytes 4194320 | tf_op jit(solution)/shard_map/all_gather | solution.py:71
  210.2 17.7 all-gather.1
  227.9 15.1 reduce-scatter.12.cloned.1.call-done
  248.1 18.8 all-gather.17.cloned.1.call-done
  266.9 169.3 %all-gather.19.cloned.1.call-done = bf16[2,2048,4096]{2,1,0:T(8,128)(2,1)} async-done(((bf16[2,128,4096]{2,1,0:T(8,128)(2,1)}), bf16[2,2048,4096]{2,1,0:T(8,128)(2,1)}) %all-gather.19.cloned.1.call-update) | async-done | bytes 33554448 | tf_op jit(solution)/shard_map/all_gather | solution.py:100
  436.2 17.7 convolution_bitcast_fusion.2
  460.0 129.9 %all-gather.21.cloned.1.call-done = bf16[4096,2048]{1,0:T(8,128)(2,1)} async-done(((bf16[4096,128]{1,0:T(8,128)(2,1)}), bf16[4096,2048]{1,0:T(8,128)(2,1)}) %all-gather.21.cloned.1.call-update) | async-done | bytes 16777232 | tf_op jit(solution)/shard_map/all_gather | solution.py:101
  602.9 17.7 convolution_bitcast_fusion.4
  629.9 23.7 %reduce-scatter.16.cloned.1.call-done = f32[128,2048]{1,0:T(8,128)} async-done(((f32[256,2048]{1,0:T(8,128)}), f32[128,2048]{1,0:T(8,128)}) %reduce-scatter.16.cloned.1.call-update) | async-done | bytes 1048592 | tf_op jit(solution)/shard_map/reduce_scatter | solution.py:136
  655.8 20.8 reduce-scatter.14.cloned.1.call-done
  680.2 21.2 all-gather.25.cloned.1.call-done
  735.9 17.8 slice_bitcast_fusion.4
  756.3 29.1 %convolution_bitcast_fusion = f32[2,2048,4096]{1,2,0:T(8,128)} fusion(bf16[1,256,4096]{2,1,0:T(8,128)(2,1)} %get-tuple-element.50, bf16[1,256,4096]{2,1,0:T(8,128)(2,1)S(1)} %copy-done.9, bf16[256,2048]{1,0:T(8,128)(2,1)S(1)} %copy-done.5), kind=kOutput, calls=%fused_computation.2 | convolution fusion | flops 8592031744 | bytes 72351744 | tf_op jit(solution)/shard_map/rd,cre->cde/dot_general | solution.py:133
  785.4 43.0 %slice_bitcast_fusion.1 = (f32[2048,4096]{0,1:T(8,128)}, f32[2048,4096]{0,1:T(8,128)}) fusion(f32[2,2048,4096]{1,2,0:T(8,128)} %convolution_bitcast_fusion), kind=kLoop, calls=%fused_computation.1 | loop fusion | bytes 134217728 | tf_op jit(solution)/shard_map/squeeze | solution.py:213
  853.4 49.1 %all-reduce.2 = (f32[2048]{0:T(1024)S(1)}, f32[2048]{0:T(1024)S(1)}) all-reduce(f32[2048]{0:T(1024)S(1)} %get-tuple-element.34, f32[2048]{0:T(1024)S(1)} %copy-done.26), channel_id=6, replica_groups=mesh['dp'=16,'tensor'=2] {'dp'}, use_global_device_ids=true, to_apply=%region_14.15.clone | all-reduce | flops 4096 | bytes 32768
  910.6 64.3 %reduce-scatter.24.cloned.1.call-done = f32[128,1024]{0,1:T(8,128)} async-done(((f32[2048,1024]{0,1:T(8,128)}), f32[128,1024]{0,1:T(8,128)}) %reduce-scatter.24.cloned.1.call-update) | async-done | bytes 524304 | tf_op jit(solution)/shard_map/reduce_scatter | solution.py:210
  974.9 108.5 %reduce-scatter.22.cloned.1.call-done = f32[128,1024]{0,1:T(8,128)} async-done(((f32[2048,1024]{0,1:T(8,128)}), f32[128,1024]{0,1:T(8,128)}) %reduce-scatter.22.cloned.1.call-update) | async-done | bytes 524304 | tf_op jit(solution)/shard_map/reduce_scatter | solution.py:209
  1086.5 331.7 %reduce-scatter.28.cloned.1.call-done = f32[128,4096]{0,1:T(8,128)} async-done(((f32[2048,4096]{0,1:T(8,128)}), f32[128,4096]{0,1:T(8,128)}) %reduce-scatter.28.cloned.1.call-update) | async-done | bytes 2097168 | tf_op jit(solution)/shard_map/reduce_scatter | solution.py:213
  1418.3 335.8 %reduce-scatter.30.cloned.1.call-done = f32[128,4096]{0,1:T(8,128)} async-done(((f32[2048,4096]{0,1:T(8,128)}), f32[128,4096]{0,1:T(8,128)}) %reduce-scatter.30.cloned.1.call-update) | async-done | bytes 2097168 | tf_op jit(solution)/shard_map/reduce_scatter | solution.py:214
  1764.1 100.1 %reduce-scatter.26.cloned.1.call-done = f32[1024,128]{1,0:T(8,128)} async-done(((f32[1024,2048]{1,0:T(8,128)}), f32[1024,128]{1,0:T(8,128)}) %reduce-scatter.26.cloned.1.call-update) | async-done | bytes 524304 | tf_op jit(solution)/shard_map/reduce_scatter | solution.py:211
  1864.3 335.5 %reduce-scatter.32.cloned.1.call-done = f32[4096,128]{1,0:T(8,128)} async-done(((f32[4096,2048]{1,0:T(8,128)}), f32[4096,128]{1,0:T(8,128)}) %reduce-scatter.32.cloned.1.call-update) | async-done | bytes 2097168 | tf_op jit(solution)/shard_map/reduce_scatter | solution.py:215
  (174 shorter events, 150.5 us)
Async XLA Ops:
  7.2 44.2 %all-gather.11.cloned.1.call-start = ((), (), s32[]{:S(2)}) async-start(), calls=%async_computation.11 | async-start | bytes 1572864 | tf_op jit(solution)/shard_map/all_gather | solution.py:76
  26.3 125.9 %all-gather.13.cloned.1.call-start = ((), (), s32[]{:S(2)}) async-start(), calls=%async_computation.12 | async-start | bytes 13369344 | tf_op jit(solution)/shard_map/all_gather | solution.py:70
  27.0 178.3 %all-gather.15.cloned.1.call-start = ((), (), s32[]{:S(2)}) async-start(), calls=%async_computation.13 | async-start | bytes 4456448 | tf_op jit(solution)/shard_map/all_gather | solution.py:71
  27.8 215.3 %reduce-scatter.12.cloned.1.call-start = ((), (), s32[]{:S(2)}) async-start(), calls=%async_computation.14 | async-start | bytes 3145728 | tf_op jit(solution)/shard_map/reduce_scatter | solution.py:92
  167.2 43.0 %copy-start.21 = (bf16[16,64,256]{2,1,0:T(8,128)(2,1)}, bf16[16,64,256]{2,1,0:T(8,128)(2,1)S(1)}, u32[]{:S(2)}) copy-start(bf16[16,64,256]{2,1,0:T(8,128)(2,1)S(1)} %convolution_convert_fusion.2) | copy-start | bytes 1572868
  205.3 37.7 %copy-start.2 = (bf16[128,2048]{1,0:T(8,128)(2,1)S(1)}, bf16[128,2048]{1,0:T(8,128)(2,1)}, u32[]{:S(2)}) copy-start(bf16[128,2048]{1,0:T(8,128)(2,1)} %param.9) | copy-start | bytes 1572868
  210.2 56.8 %all-gather.17.cloned.1.call-start = ((), (), s32[]{:S(2)}) async-start(), calls=%async_computation.15 | async-start | bytes 1572864 | tf_op jit(solution)/shard_map/all_gather | solution.py:106
  244.5 209.4 %copy-start.30 = (f32[128]{0:T(128)}, f32[128]{0:T(128)S(1)}, u32[]{:S(2)}) copy-start(f32[128]{0:T(128)S(1)} %add_rsqrt_fusion) | copy-start | bytes 1540
  245.5 190.7 %all-gather.19.cloned.1.call-start = ((), (), s32[]{:S(2)}) async-start(), calls=%async_computation.16 | async-start | bytes 35651584 | tf_op jit(solution)/shard_map/all_gather | solution.py:100
  246.0 214.0 %all-gather.23.cloned.1.call-start = ((), (), s32[]{:S(2)}) async-start(), calls=%async_computation.19 | async-start | bytes 1572864 | tf_op jit(solution)/shard_map/all_gather | solution.py:122
  246.2 207.7 %copy-start.31 = (f32[128]{0:T(128)}, f32[128]{0:T(128)S(1)}, u32[]{:S(2)}) copy-start(f32[128]{0:T(128)S(1)} %compare_convert_fusion) | copy-start | bytes 1540
  247.2 342.7 %all-gather.21.cloned.1.call-start = ((), (), s32[]{:S(2)}) async-start(), calls=%async_computation.17 | async-start | bytes 17825792 | tf_op jit(solution)/shard_map/all_gather | solution.py:101
  247.9 405.7 %reduce-scatter.16.cloned.1.call-start = ((), (), s32[]{:S(2)}) async-start(), calls=%async_computation.20 | async-start | bytes 3145728 | tf_op jit(solution)/shard_map/reduce_scatter | solution.py:136
  620.6 56.0 %reduce-scatter.14.cloned.1.call-start = ((), (), s32[]{:S(2)}) async-start(), calls=%async_computation.18 | async-start | bytes 1572864 | tf_op jit(solution)/shard_map/reduce_scatter | solution.py:115
  629.9 71.6 %all-gather.25.cloned.1.call-start = ((), (), s32[]{:S(2)}) async-start(), calls=%async_computation.21 | async-start | bytes 1572864 | tf_op jit(solution)/shard_map/all_gather | solution.py:147
  680.0 171.8 %reduce-scatter.18.cloned.1.call-start = ((), (), s32[]{:S(2)}) async-start(), calls=%async_computation.22 | async-start | bytes 3145728 | tf_op jit(solution)/shard_map/reduce_scatter | solution.py:186
  725.1 185.5 %reduce-scatter.20.cloned.1.call-start = ((), (), s32[]{:S(2)}) async-start(), calls=%async_computation.23 | async-start | bytes 8912896 | tf_op jit(solution)/shard_map/reduce_scatter | solution.py:208
  753.8 221.1 %reduce-scatter.24.cloned.1.call-start = ((), (), s32[]{:S(2)}) async-start(), calls=%async_computation.25 | async-start | bytes 8912896 | tf_op jit(solution)/shard_map/reduce_scatter | solution.py:210
  754.3 329.1 %reduce-scatter.22.cloned.1.call-start = ((), (), s32[]{:S(2)}) async-start(), calls=%async_computation.24 | async-start | bytes 8912896 | tf_op jit(solution)/shard_map/reduce_scatter | solution.py:209
  754.9 663.3 %reduce-scatter.28.cloned.1.call-start = ((), (), s32[]{:S(2)}) async-start(), calls=%async_computation.27 | async-start | bytes 35651584 | tf_op jit(solution)/shard_map/reduce_scatter | solution.py:213
  828.4 925.7 %reduce-scatter.30.cloned.1.call-start = ((), (), s32[]{:S(2)}) async-start(), calls=%async_computation.28 | async-start | bytes 35651584 | tf_op jit(solution)/shard_map/reduce_scatter | solution.py:214
  829.0 1035.2 %reduce-scatter.26.cloned.1.call-start = ((), (), s32[]{:S(2)}) async-start(), calls=%async_computation.26 | async-start | bytes 8912896 | tf_op jit(solution)/shard_map/reduce_scatter | solution.py:211
  834.4 1365.4 %reduce-scatter.32.cloned.1.call-start = ((), (), s32[]{:S(2)}) async-start(), calls=%async_computation.29 | async-start | bytes 35651584 | tf_op jit(solution)/shard_map/reduce_scatter | solution.py:215
  849.8 58.2 %copy-start.6 = (f32[128,2048]{1,0:T(8,128)S(1)}, f32[128,2048]{1,0:T(8,128)}, u32[]{:S(2)}) copy-start(f32[128,2048]{1,0:T(8,128)} %get-tuple-element.41) | copy-start | bytes 3145732
  (29 other events, 182.1 us)
Sparse Core Ops, SparseCore 0:
  26.4 24.9 all-gather.10
  53.6 98.5 all-gather.12
  154.3 50.9 all-gather.14
  210.3 32.7 reduce-scatter.11
  245.6 21.2 all-gather.16
  268.4 167.7 all-gather.18
  438.4 21.6 all-gather.22
  462.4 127.4 all-gather.20
  620.7 32.8 reduce-scatter.15
  656.3 20.2 reduce-scatter.13
  680.1 21.3 all-gather.24
  725.2 31.8 reduce-scatter.17
  761.2 105.1 reduce-scatter.19
  870.3 104.5 reduce-scatter.23
  978.8 104.5 reduce-scatter.21
  1087.6 330.6 reduce-scatter.27
  1422.4 331.6 reduce-scatter.29
  1758.6 105.6 reduce-scatter.25
  1869.1 330.6 reduce-scatter.31
where the time goes:
time: 2220 us; the launch traced here: 2210 us
  waiting for transfers between devices  1840 us (83%)
  matrix products  149 us (7%)
  blocking collectives  87.3 us (4%)
  local copies, waits for them, and re-layouts  82.2 us (4%)
  other arithmetic  27.5 us (1%)
    reduce_scatter x1, waiting for transfers between devices, shards(): lax.psum_scatter(gate_up_grad[1], 'dp', scatter_dimension=0, tiled=True)  336 us
    reduce_scatter x1, waiting for transfers between devices, shards(): lax.psum_scatter(down_grad, 'dp', scatter_dimension=1, tiled=True)  336 us
    reduce_scatter x1, waiting for transfers between devices, shards(): lax.psum_scatter(gate_up_grad[0], 'dp', scatter_dimension=0, tiled=True)  332 us
    all_gather x1, waiting for transfers between devices, shards(): lax.all_gather(w_gate_up, 'dp', axis=1, tiled=True)  169 us
    all_gather x1, waiting for transfers between devices, shards(): lax.all_gather(w_down, 'dp', axis=1, tiled=True)  130 us
    reduce_scatter x1, waiting for transfers between devices, shards(): lax.psum_scatter(qkv_grad[1], 'dp', scatter_dimension=0, tiled=True)  109 us
    all_gather x1, waiting for transfers between devices, shards(): lax.all_gather(w_qkv, 'dp', axis=1, tiled=True)  101 us
    reduce_scatter x1, waiting for transfers between devices, shards(): lax.psum_scatter(out_grad, 'dp', scatter_dimension=1, tiled=True)  100 us
  transfers between devices with their start and end apart: 19, of which 17 were waited for; matrix products, arithmetic and copies ran while one was open for 8% of the time, Pallas kernels for 0%

commit v1 on v0

--- a/solution.py
+++ b/solution.py
@@ -1,13 +1,850 @@
+import functools
+
 import jax
 import jax.numpy as jnp
 from jax import lax
+from jax.experimental import pallas as pl
+from jax.experimental.pallas import tpu as pltpu
 from jax.sharding import PartitionSpec as P
 
 HD = 64
-
-
 EPSILON = 1e-05
 ROPE_BASE = 130000.0
+MESH = pl.DeviceIdType.MESH
+ANY = pl.BlockSpec(memory_space=pl.ANY)
+VM = pl.BlockSpec(memory_space=pltpu.VMEM)
+F32 = jnp.float32
+BF16 = jnp.bfloat16
+LANES = 128
+NT = (((1,), (1,)), ((), ()))
+TN = (((0,), (0,)), ((), ()))
+NN = (((1,), (0,)), ((), ()))
+
+
+def dot(a, b, dims=NN):
+    return lax.dot_general(a, b, dims, preferred_element_type=F32)
+
+
+def when(cond, action):
+    if cond is None:
+        action()
+    else:
+        pl.when(cond)(action)
+
+
+class Net:
+    def __init__(self, dp, send_sems, local_sems):
+        self.n = dp // 4
+        self.dp_index = lax.axis_index("dp")
+        self.x = lax.axis_index("tensor")
+        self.z = self.dp_index // 4
+        self.y = (self.dp_index // 2) % 2
+        self.c = self.dp_index % 2
+        self.send_sems = send_sems
+        self.local_sems = local_sems
+        self.sent = 0
+        self.moved = 0
+        self.pending = []
+        self.kept = []
+
+    def place(self, z, y, c):
+        return (z * 2 + y) * 2 + c
+
+    def device(self, z=None, y=None, c=None, x=None):
+        z = self.z if z is None else z
+        y = self.y if y is None else y
+        c = self.c if c is None else c
+        x = self.x if x is None else x
+        return (self.place(z, y, c), x)
+
+    def greet(self, devices):
+        barrier = pltpu.get_barrier_semaphore()
+        for device in devices:
+            pl.semaphore_signal(barrier, inc=1, device_id=device, device_id_type=MESH)
+        pl.semaphore_wait(barrier, len(devices))
+
+    def send(self, src, dst, recv_sem, device, cond=None):
+        sem = self.send_sems.at[self.sent]
+        self.sent += 1
+        copy = pltpu.make_async_remote_copy(
+            src_ref=src, dst_ref=dst, send_sem=sem, recv_sem=recv_sem, device_id=device, device_id_type=MESH
+        )
+        when(cond, copy.start)
+        self.pending.append((cond, copy))
+
+    def recv(self, dst, recv_sem):
+        pltpu.make_async_remote_copy(
+            src_ref=dst, dst_ref=dst, send_sem=self.send_sems.at[0], recv_sem=recv_sem,
+            device_id=self.device(c=1 - self.c), device_id_type=MESH,
+        ).wait_recv()
+
+    def local(self, src, dst, cond=None):
+        sem = self.local_sems.at[self.moved]
+        self.moved += 1
+        copy = pltpu.make_async_copy(src, dst, sem)
+        when(cond, copy.start)
+        self.kept.append((cond, copy))
+        return copy
+
+    def settle(self, copy):
+        self.kept = [entry for entry in self.kept if entry[1] is not copy]
+        copy.wait()
+
+    def drain(self):
+        assert self.sent <= self.send_sems.shape[0] and self.moved <= self.local_sems.shape[0]
+        for cond, copy in self.pending:
+            when(cond, copy.wait_send)
+        for cond, copy in self.kept:
+            when(cond, copy.wait)
+
+
+class Gather:
+    def __init__(self, net, own, at, sems):
+        self.net, self.own, self.at = net, own, at
+        self.sems = sems
+
+    def spread(self, block, src, ysend=True):
+        net = self.net
+        here = net.place(block, net.y, net.c)
+        net.send(src, self.at(here), self.sems.at[1, block], net.device(y=1 - net.y))
+        net.send(src, self.at(here), self.sems.at[2 + net.y, block], net.device(c=1 - net.c))
+
+    def start(self):
+        net = self.net
+        here = self.at(net.dp_index)
+        net.send(self.own, here, self.sems.at[0, net.z], net.device(z=net.z + 1), net.z < net.n - 1)
+        net.send(self.own, here, self.sems.at[0, net.z], net.device(z=net.z - 1), net.z > 0)
+        self.spread(net.z, self.own)
+        self.kept = net.local(self.own, here)
+
+    def step(self, s):
+        net = self.net
+        for sign in (1, -1):
+            block = net.z - s * sign
+            valid = jnp.logical_and(block >= 0, block < net.n)
+            nxt = net.z + sign
+            more = jnp.logical_and(nxt >= 0, nxt < net.n)
+            here = self.at(net.place(block, net.y, net.c))
+
+            @pl.when(valid)
+            def _():
+                net.recv(here, self.sems.at[0, block])
+
+            net.send(here, here, self.sems.at[0, block], net.device(z=nxt), jnp.logical_and(valid, more))
+            net.send(here, here, self.sems.at[1, block], net.device(y=1 - net.y), valid)
+            net.send(here, here, self.sems.at[2 + net.y, block], net.device(c=1 - net.c), valid)
+
+    def cross(self, block):
+        net = self.net
+        there = self.at(net.place(block, 1 - net.y, net.c))
+        net.recv(there, self.sems.at[1, block])
+        net.send(there, there, self.sems.at[3 - net.y, block], net.device(c=1 - net.c))
+
+    def cross_step(self, s):
+        net = self.net
+        for sign in (1, -1):
+            block = net.z - s * sign
+            valid = jnp.logical_and(block >= 0, block < net.n)
+            there = self.at(net.place(block, 1 - net.y, net.c))
+
+            @pl.when(valid)
+            def _():
+                net.recv(there, self.sems.at[1, block])
+
+            net.send(there, there, self.sems.at[3 - net.y, block], net.device(c=1 - net.c), valid)
+
+    def finish(self, block):
+        net = self.net
+        for y in (0, 1):
+            net.recv(self.at(net.place(block, y, 1 - net.c)), self.sems.at[2 + y, block])
+
+
+class Exchange:
+    def __init__(self, net, part, at, sems):
+        self.net, self.part, self.at = net, part, at
+        self.sems = sems
+
+    def start(self):
+        net = self.net
+        here = self.at(net.dp_index)
+        for d in list(range(1, net.n)):
+            to = (net.z + d) % net.n
+            net.send(self.part(to), here, self.sems.at[0, net.z], net.device(z=to))
+        own = self.part(net.z)
+        net.send(own, here, self.sems.at[1, net.z], net.device(y=1 - net.y))
+        net.send(own, here, self.sems.at[2 + net.y, net.z], net.device(c=1 - net.c))
+        self.kept = net.local(own, here)
+
+    def step(self, block):
+        net = self.net
+        here = self.at(net.place(block, net.y, net.c))
+        net.recv(here, self.sems.at[0, block])
+        net.send(here, here, self.sems.at[1, block], net.device(y=1 - net.y))
+        net.send(here, here, self.sems.at[2 + net.y, block], net.device(c=1 - net.c))
+
+    cross = Gather.cross
+    finish = Gather.finish
+
+
+class Rows:
+    def __init__(self, net, own, full, sems):
+        self.net, self.own, self.full = net, own, full
+        self.sems = sems
+
+    def start(self):
+        net = self.net
+        here = self.full.at[net.z, net.x]
+        net.send(self.own, here, self.sems.at[0, net.z], net.device(z=net.z + 1), net.z < net.n - 1)
+        net.send(self.own, here, self.sems.at[0, net.z], net.device(z=net.z - 1), net.z > 0)
+        net.send(self.own, here, self.sems.at[1, net.z], net.device(x=1 - net.x))
+        self.kept = net.local(self.own, here)
+
+    def step(self, s):
+        net = self.net
+        for sign in (1, -1):
+            block = net.z - s * sign
+            valid = jnp.logical_and(block >= 0, block < net.n)
+            nxt = net.z + sign
+            more = jnp.logical_and(nxt >= 0, nxt < net.n)
+            here = self.full.at[block, net.x]
+
+            @pl.when(valid)
+            def _():
+                net.recv(here, self.sems.at[0, block])
+
+            net.send(here, here, self.sems.at[0, block], net.device(z=nxt), jnp.logical_and(valid, more))
+            net.send(here, here, self.sems.at[1, block], net.device(x=1 - net.x), valid)
+
+    def finish(self):
+        net = self.net
+        for block in range(net.n):
+            net.recv(self.full.at[block, 1 - net.x], self.sems.at[1, block])
+
+
+class Reduce:
+    def __init__(self, net, part, from_c, from_y, result, sems):
+        self.net, self.part, self.from_c, self.from_y, self.result = net, part, from_c, from_y, result
+        self.cs, self.ys, self.zs = sems
+
+    def add(self, total, term):
+        def body(r):
+            span = pl.ds(r, 16)
+            total[span] = (total[span].astype(F32) + term[span].astype(F32)).astype(BF16)
+
+        loop(total.shape[0], 16, body)
+
+    def start(self, i):
+        net = self.net
+        net.send(self.part.at[i, 1 - net.c], self.from_c.at[i], self.cs.at[i], net.device(c=1 - net.c))
+
+    def step_c(self, i):
+        net = self.net
+        net.recv(self.from_c.at[i], self.cs.at[i])
+        for y in (0, 1):
+            self.add(self.part.at[i, net.c, y], self.from_c.at[i, y])
+        net.send(self.part.at[i, net.c, 1 - net.y], self.from_y.at[i], self.ys.at[i], net.device(y=1 - net.y))
+
+    def step_y(self, i, matrix, to):
+        net = self.net
+        net.recv(self.from_y.at[i], self.ys.at[i])
+        self.add(self.part.at[i, net.c, net.y], self.from_y.at[i])
+        src = self.part.at[i, net.c, net.y]
+        dst = self.result.at[matrix, net.z]
+        away = to != net.z
+        net.send(src, dst, self.zs.at[matrix, net.z], net.device(z=to), away)
+        net.local(src, dst, jnp.logical_not(away))
+
+    def finish(self, matrix):
+        net = self.net
+        for d in range(1, net.n):
+            block = (net.z + d) % net.n
+            net.recv(self.result.at[matrix, block], self.zs.at[matrix, block])
+
+
+def loop(total, step, body):
+    @pl.loop(0, total // step)
+    def _(i):
+        body(pl.multiple_of(i * step, step))
+
+
+def turn(field, cosine, sine, lane):
+    half = HD // 2
+    partner = jnp.where(lane % HD < half, pltpu.roll(field, LANES - half, 1), pltpu.roll(field, half, 1))
+    return field * cosine + partner * sine
+
+
+def head_masks():
+    lane = lax.broadcasted_iota(jnp.int32, (1, LANES), 1)
+    return (lane < HD).astype(BF16), (lane >= HD).astype(BF16)
+
+
+def both(field, masks):
+    return jnp.concatenate([field * masks[0], field * masks[1]], axis=0)
+
+
+def pick(stacked, rows):
+    lane = lax.broadcasted_iota(jnp.int32, (1, LANES), 1)
+    return jnp.where(lane < HD, stacked[:rows], stacked[rows:])
+
+
+def softmax(queries2, key_rows, allowed):
+    scores = dot(queries2, key_rows, NT) * HD ** (-0.5)
+    scores = jnp.where(allowed > 0, scores, -1e30)
+    raised = jnp.exp(scores - jnp.max(scores, axis=-1, keepdims=True))
+    return raised / jnp.sum(raised, axis=-1, keepdims=True)
+
+
+def attention_kernel(
+    dp,
+    residual, cotangent, seg_col, seg_row, gains, freq, wa, wf,
+    wa_out, wf_out, grad_out, normed_ffn_out, normed_out, attended_out, qkv_out, mixed_out, tables_out, gains_out,
+    weights, pre, all_gains, allowed, grad_own, normed_all, ffn_own, partial, to_x, from_x,
+    send_sems, local_sems, gain_sems, q_sems, o_sems, f_sems, g_sems, n_sems, x_sems,
+):
+    net = Net(dp, send_sems, local_sems)
+    n = net.n
+    rows, width = residual.shape
+    block, cols = wa.shape[1:]
+    group = 2 * rows
+    part = wf.shape[2] // n
+    me, x = net.dp_index, net.x
+    net.greet([((me + k) % dp, x) for k in range(1, dp)] + [(me, 1 - x)])
+
+    for k in range(1, dp):
+        net.send(gains, all_gains.at[me], gain_sems.at[me], ((me + k) % dp, x))
+    all_gains[me] = gains[...]
+
+    def at_weights(first, count):
+        return lambda index: weights.at[pl.ds(first, count), pl.ds(pl.multiple_of(index * block, block), block)]
+
+    qkv = Gather(net, wa.at[pl.ds(0, 3)], at_weights(0, 3), q_sems)
+    out = Gather(net, wa.at[pl.ds(3, 1)], at_weights(3, 1), o_sems)
+    ffn = Exchange(
+        net,
+        lambda to: wf.at[:, :, pl.ds(pl.multiple_of(to * part, part), part)],
+        lambda index: wf_out.at[:, pl.ds(pl.multiple_of(index * block, block), block)],
+        f_sems,
+    )
+    grads = Rows(net, grad_own, grad_out, g_sems)
+    ffn_rows = Rows(net, ffn_own, normed_ffn_out, n_sems)
+    qkv.start()
+
+    def mask_body(r):
+        span = pl.ds(r, 16)
+        live = (seg_col[x, span] >= 0).astype(F32)
+        grad_own[span] = (cotangent[span].astype(F32) * live).astype(BF16)
+
+    loop(rows, 16, mask_body)
+
+    row_seg = jnp.concatenate([seg_col[0], seg_col[1]], axis=0)
+    row_id = lax.broadcasted_iota(jnp.int32, (group, group), 0)
+    col_id = lax.broadcasted_iota(jnp.int32, (group, group), 1)
+    mask = jnp.logical_and(row_seg == seg_row[...], row_id >= col_id).astype(F32)
+    allowed[...] = mask
+    places = jnp.sum(mask, axis=1, keepdims=True) - 1.0
+    lane = lax.broadcasted_iota(jnp.int32, (group, LANES), 1)
+    angles = places * freq[...]
+    tables_out[0] = jnp.cos(angles)
+    tables_out[1] = jnp.where(lane % HD < HD // 2, -jnp.sin(angles), jnp.sin(angles))
+
+    for k in range(1, dp):
+        source = (me + k) % dp
+        net.recv(all_gains.at[source], gain_sems.at[source])
+    for i in range(dp):
+        gains_out[:, i * block : (i + 1) * block] = all_gains[i]
+
+    def norm_body(r):
+        value = residual[pl.ds(r, 16)].astype(F32)
+        unit = value * lax.rsqrt(jnp.mean(value * value, axis=-1, keepdims=True) + EPSILON)
+        to = pl.multiple_of(x * rows + r, 16)
+        normed_all[pl.ds(to, 16)] = (unit * gains_out[0:1]).astype(BF16)
+
+    loop(rows, 16, norm_body)
+    own_rows = normed_all.at[pl.ds(pl.multiple_of(x * rows, rows), rows)]
+    other_rows = normed_all.at[pl.ds(pl.multiple_of((1 - x) * rows, rows), rows)]
+    net.send(own_rows, own_rows, x_sems.at[0], net.device(x=1 - x))
+
+    depth = width // n
+
+    def project(b, first):
+        qkv.finish(b)
+        base = pl.multiple_of(b * depth, depth)
+
+        def body(col):
+            for m in range(3):
+                term = dot(normed_all[:, pl.ds(base, depth)], weights[m, pl.ds(base, depth), pl.ds(col, 256)])
+                to = pl.ds(pl.multiple_of(m * cols + col, 256), 256)
+                pre[:, to] = term if first else pre[:, to] + term
+
+        loop(cols, 256, body)
+
+    qkv.step(1)
+    qkv.cross(net.z)
+    grads.start()
+    for s in range(2, n):
+        qkv.step(s)
+        if s == 2:
+            out.start()
+            ffn.start()
+        qkv.cross_step(s - 1)
+    qkv.cross_step(n - 1)
+    net.recv(other_rows, x_sems.at[0])
+    net.settle(qkv.kept)
+    for k in range(n):
+        project((net.z + k) % n, k == 0)
+    out.cross(net.z)
+    for s in range(1, n):
+        out.step(s)
+        out.cross_step(s)
+    masks = head_masks()
+
+    def head_body(col):
+        cosine, sine = tables_out[0], tables_out[1]
+        queries = turn(pre[:, pl.ds(col, LANES)], cosine, sine, lane).astype(BF16)
+        key_rows = turn(pre[:, pl.ds(pl.multiple_of(cols + col, LANES), LANES)], cosine, sine, lane).astype(BF16)
+        value_rows = pre[:, pl.ds(pl.multiple_of(2 * cols + col, LANES), LANES)].astype(BF16)
+        qkv_out[0, :, pl.ds(col, LANES)] = queries
+        qkv_out[1, :, pl.ds(col, LANES)] = key_rows
+        qkv_out[2, :, pl.ds(col, LANES)] = value_rows
+        may = jnp.concatenate([allowed[...], allowed[...]], axis=0)
+        probs = softmax(both(queries, masks), key_rows, may).astype(BF16)
+        attended_out[:, pl.ds(col, LANES)] = pick(dot(probs, value_rows), group).astype(BF16)
+
+    loop(cols, LANES, head_body)
+    for k in range(1, n):
+        ffn.step((net.z + k) % n)
+    for k in range(n):
+        out.finish((net.z + k) % n)
+    net.settle(out.kept)
+    kept_weights = net.local(weights, wa_out)
+
+    def out_body(col):
+        term = dot(attended_out[...], weights[3, pl.ds(col, 256), :], NT)
+        partial[0, :, pl.ds(col, 256)] = term[:rows]
+        partial[1, :, pl.ds(col, 256)] = term[rows:]
+
+    loop(width, 256, out_body)
+
+    def to_body(r):
+        to_x[pl.ds(r, 16)] = partial[1 - x, pl.ds(r, 16)].astype(BF16)
+
+    loop(rows, 16, to_body)
+    net.send(to_x, from_x, x_sems.at[1], net.device(x=1 - x))
+    for s in range(1, n):
+        grads.step(s)
+    net.recv(from_x, x_sems.at[1])
+
+    def mix_body(r):
+        span = pl.ds(r, 16)
+        value = residual[span].astype(F32) + partial[x, span] + from_x[span].astype(F32)
+        mixed_out[span] = value
+        unit = value * lax.rsqrt(jnp.mean(value * value, axis=-1, keepdims=True) + EPSILON)
+        ffn_own[span] = (unit * gains_out[8:9]).astype(BF16)
+
+    loop(rows, 16, mix_body)
+    ffn_rows.start()
+    net.local(normed_all, normed_out)
+    for s in range(1, n):
+        ffn_rows.step(s)
+    for k in range(n):
+        ffn.cross((net.z + k) % n)
+    for k in range(n):
+        ffn.finish((net.z + k) % n)
+    grads.finish()
+    ffn_rows.finish()
+    net.drain()
+
+
+class RowSum:
+    def __init__(self, net, part, from_x, from_z, sems):
+        self.net, self.part, self.from_x, self.from_z = net, part, from_x, from_z
+        self.xs, self.zs = sems
+
+    def start(self, b):
+        net = self.net
+        net.send(self.part(b, 1 - net.x), self.from_x.at[b], self.xs.at[b], net.device(x=1 - net.x))
+
+    def step(self, b, own):
+        net = self.net
+        net.recv(self.from_x.at[b], self.xs.at[b])
+        total, term = self.part(b, net.x), self.from_x.at[b]
+
+        def body(r):
+            span = pl.ds(r, 16)
+            total[span] = (total[span].astype(F32) + term[span].astype(F32)).astype(BF16)
+
+        loop(total.shape[0], 16, body)
+        if not own:
+            net.send(total, self.from_z.at[net.z], self.zs.at[net.z], net.device(z=b))
+
+    def finish(self):
+        net = self.net
+        for d in range(1, net.n):
+            b = (net.z + d) % net.n
+            net.recv(self.from_z.at[b], self.zs.at[b])
+
+    def total(self, span):
+        net = self.net
+        value = self.part(net.z, net.x)[span].astype(F32)
+        for d in range(1, net.n):
+            value = value + self.from_z[(net.z + d) % net.n, span].astype(F32)
+        return value
+
+
+def norm_back(grad, value, gain):
+    scale = lax.rsqrt(jnp.mean(value * value, axis=-1, keepdims=True) + EPSILON)
+    unit = value * scale
+    scaled = grad * gain
+    back = scale * (scaled - unit * jnp.mean(scaled * unit, axis=-1, keepdims=True))
+    return back, grad * unit
+
+
+def weight_item(red, i, left, right, base, depth, block):
+    def body(col):
+        term = dot(left[:, pl.ds(base, depth)], right[:, pl.ds(col, 256)], TN).astype(BF16)
+        for y in (0, 1):
+            for c in (0, 1):
+                at = (y * 2 + c) * block
+                red.part[i, c, y, :, pl.ds(col, 256)] = term[at : at + block]
+
+    loop(right.shape[1], 256, body)
+
+
+def ffn_kernel(
+    dp,
+    mixed, gains, normed_hbm, grad_hbm, wf,
+    result, block_out, mixed_grad, gain_part,
+    weights, normed, grad, hidden, gate_up_grad, back, back_x, back_z, add_x, add_z, part, from_c, from_y,
+    send_sems, local_sems, bx_sems, bz_sems, ax_sems, az_sems, rc_sems, ry_sems, rz_sems,
+):
+    net = Net(dp, send_sems, local_sems)
+    n = net.n
+    rows, width = mixed.shape
+    cols = wf.shape[2]
+    block = width // dp
+    depth = width // n
+    pair = 2 * rows
+    loads = [net.local(normed_hbm, normed), net.local(wf, weights), net.local(grad_hbm, grad)]
+    net.greet(
+        [net.device(z=(net.z + d) % n) for d in range(1, n)]
+        + [net.device(y=1 - net.y), net.device(c=1 - net.c), net.device(x=1 - net.x)]
+    )
+    gate_grad, up_grad = gate_up_grad.at[:, pl.ds(0, cols)], gate_up_grad.at[:, pl.ds(cols, cols)]
+    add = gate_up_grad
+    backs = RowSum(net, lambda b, half: back.at[b, half], back_x, back_z, (bx_sems, bz_sems))
+    adds = RowSum(
+        net, lambda b, half: add.at[pl.ds(pl.multiple_of((b * 2 + half) * rows, rows), rows)], add_x, add_z, (ax_sems, az_sems)
+    )
+    red = Reduce(net, part, from_c, from_y, result, (rc_sems, ry_sems, rz_sems))
+    for load in loads:
+        net.settle(load)
+
+    order = sorted(range(n), key=lambda d: -min(d, n - d))
+
+    def chunk(b):
+        here = pl.ds(pl.multiple_of(b * pair, pair), pair)
+
+        def hidden_body(col):
+            span = pl.ds(col, 256)
+            gate = dot(normed[here], weights[0, :, span])
+            up = dot(normed[here], weights[1, :, span])
+            hidden_grad = dot(grad[here], weights[2, :, span])
+            sigmoid = 1.0 / (1.0 + jnp.exp(-gate))
+            active = gate * sigmoid
+            hidden[here, span] = (active * up).astype(BF16)
+            gate_grad[here, span] = (hidden_grad * up * sigmoid * (1.0 + gate * (1.0 - sigmoid))).astype(BF16)
+            up_grad[here, span] = (hidden_grad * active).astype(BF16)
+
+        loop(cols, 256, hidden_body)
+
+        def back_body(col):
+            span = pl.ds(col, 256)
+            term = dot(gate_grad[here], weights[0, span, :], NT) + dot(up_grad[here], weights[1, span, :], NT)
+            term = term.astype(BF16)
+            back[b, 0, :, span] = term[:rows]
+            back[b, 1, :, span] = term[rows:]
+
+        loop(width, 256, back_body)
+        backs.start(b)
+
+    def add_chunk(b):
+        here = pl.ds(pl.multiple_of(b * pair, pair), pair)
+
+        def body(col):
+            span = pl.ds(col, 256)
+            term = dot(hidden[here], weights[2, span, :], NT).astype(BF16)
+            add[here, span] = term
+
+        loop(width, 256, body)
+        adds.start(b)
+
+    for k, d in enumerate(order):
+        chunk((net.z + d) % n)
+        if k > 0:
+            backs.step((net.z + order[k - 1]) % n, order[k - 1] == 0)
+    items = []
+    for d in order:
+        b = (net.z + d) % n
+        for m in (2, 0, 1):
+            i = len(items)
+            left, right = ((normed, gate_grad), (normed, up_grad), (grad, hidden))[m]
+            weight_item(red, i, left, right, pl.multiple_of(b * depth, depth), depth, block)
+            red.start(i)
+            if i > 0:
+                red.step_c(i - 1)
+            if i == 1:
+                backs.step((net.z + order[-1]) % n, order[-1] == 0)
+            items.append((m, b))
+    red.step_c(len(items) - 1)
+    for k, d in enumerate(order):
+        add_chunk((net.z + d) % n)
+        if k > 0:
+            adds.step((net.z + order[k - 1]) % n, order[k - 1] == 0)
+    backs.finish()
+    gain_part[...] = jnp.zeros_like(gain_part)
+
+    def mixed_body(r):
+        span = pl.ds(r, 16)
+        own = pl.ds(pl.multiple_of((net.z * 2 + net.x) * rows + r, 16), 16)
+        term, gain_term = norm_back(backs.total(span), mixed[span], gains[8:9])
+        mixed_grad[span] = grad[own].astype(F32) + term
+        gain_part[...] += gain_term[:8] + gain_term[8:]
+
+    loop(rows, 16, mixed_body)
+    adds.step((net.z + order[-1]) % n, order[-1] == 0)
+    for i, (m, b) in enumerate(items):
+        red.step_y(i, m, b)
+    adds.finish()
+
+    def block_body(r):
+        span = pl.ds(r, 16)
+        block_out[span] = (mixed[span] + adds.total(span)).astype(BF16)
+
+    loop(rows, 16, block_body)
+    for m in range(3):
+        red.finish(m)
+    net.drain()
+
+
+def back_kernel(
+    dp,
+    residual, seg_col, seg_row, gains, tables, normed, attended, qkv, mixed_grad, ffn_part, wa,
+    result, input_grad, gain_out,
+    weights, allowed, mixed_all, attended_grad, qkv_grad, partial, to_x, from_x, gain_to, gain_from, gain_sum, gain_x,
+    part, from_c, from_y,
+    send_sems, local_sems, x_sems, gain_sems, rc_sems, ry_sems, rz_sems,
+):
+    net = Net(dp, send_sems, local_sems)
+    n = net.n
+    me, x = net.dp_index, net.x
+    rows, width = residual.shape
+    group = 2 * rows
+    cols = wa.shape[2]
+    block = width // dp
+    depth = width // n
+    load_out = net.local(wa.at[3], weights.at[3])
+    load_qkv = net.local(wa.at[pl.ds(0, 3)], weights.at[pl.ds(0, 3)])
+    net.greet([((me + k) % dp, x) for k in range(1, dp)] + [(me, 1 - x)])
+    red = Reduce(net, part, from_c, from_y, result, (rc_sems, ry_sems, rz_sems))
+
+    def low_body(r):
+        to = pl.multiple_of(x * rows + r, 16)
+        mixed_all[pl.ds(to, 16)] = mixed_grad[pl.ds(r, 16)].astype(BF16)
+
+    loop(rows, 16, low_body)
+    own_rows = mixed_all.at[pl.ds(pl.multiple_of(x * rows, rows), rows)]
+    other_rows = mixed_all.at[pl.ds(pl.multiple_of((1 - x) * rows, rows), rows)]
+    net.send(own_rows, own_rows, x_sems.at[0], net.device(x=1 - x))
+    row_seg = jnp.concatenate([seg_col[0], seg_col[1]], axis=0)
+    row_id = lax.broadcasted_iota(jnp.int32, (group, group), 0)
+    col_id = lax.broadcasted_iota(jnp.int32, (group, group), 1)
+    allowed[...] = jnp.logical_and(row_seg == seg_row[...], row_id >= col_id).astype(F32)
+    net.settle(load_out)
+    net.recv(other_rows, x_sems.at[0])
+
+    def attended_body(col):
+        span = pl.ds(col, 256)
+        attended_grad[:, span] = dot(mixed_all[...], weights[3, :, span]).astype(BF16)
+
+    loop(cols, 256, attended_body)
+    order = sorted(range(n), key=lambda d: -min(d, n - d))
+    items = []
+
+    def emit(m, left, right):
+        for d in order:
+            b = (net.z + d) % n
+            i = len(items)
+            weight_item(red, i, left, right, pl.multiple_of(b * depth, depth), depth, block)
+            red.start(i)
+            if i > 0:
+                red.step_c(i - 1)
+            items.append((m, b))
+
+    emit(3, mixed_all, attended)
+    masks = head_masks()
+    lane = lax.broadcasted_iota(jnp.int32, (group, LANES), 1)
+
+    def head_body(col):
+        span = pl.ds(col, LANES)
+        cosine, sine = tables[0], tables[1]
+        queries, key_rows, value_rows = qkv[0, :, span], qkv[1, :, span], qkv[2, :, span]
+        out_grad = attended_grad[:, span]
+        queries2, out_grad2 = both(queries, masks), both(out_grad, masks)
+        may = jnp.concatenate([allowed[...], allowed[...]], axis=0)
+        probs = softmax(queries2, key_rows, may)
+        value_grad = dot(probs.astype(BF16), out_grad2, TN)
+        prob_grad = dot(out_grad2, value_rows, NT)
+        score_grad = probs * (prob_grad - jnp.sum(probs * prob_grad, axis=-1, keepdims=True))
+        score_grad = score_grad.astype(BF16)
+        query_grad = pick(dot(score_grad, key_rows), group) * HD ** (-0.5)
+        key_grad = dot(score_grad, queries2, TN) * HD ** (-0.5)
+        qkv_grad[0, :, span] = turn(query_grad, cosine, -sine, lane).astype(BF16)
+        qkv_grad[1, :, span] = turn(key_grad, cosine, -sine, lane).astype(BF16)
+        qkv_grad[2, :, span] = value_grad.astype(BF16)
+
+    loop(cols, LANES, head_body)
+    net.settle(load_qkv)
+
+    def normed_body(col):
+        span = pl.ds(col, 256)
+        term = dot(qkv_grad[0], weights[0, span, :], NT)
+        term += dot(qkv_grad[1], weights[1, span, :], NT)
+        term += dot(qkv_grad[2], weights[2, span, :], NT)
+        partial[0, :, span] = term[:rows]
+        partial[1, :, span] = term[rows:]
+
+    def to_body(r):
+        to_x[pl.ds(r, 16)] = partial[1 - x, pl.ds(r, 16)].astype(BF16)
+
+    for m in range(3):
+        emit(m, normed, qkv_grad.at[m])
+    red.step_c(len(items) - 1)
+    loop(width, 256, normed_body)
+    loop(rows, 16, to_body)
+    net.send(to_x, from_x, x_sems.at[1], net.device(x=1 - x))
+    half = len(items) // 2
+    for i in range(half):
+        red.step_y(i, *items[i])
+    net.recv(from_x, x_sems.at[1])
+    gain_sum[...] = jnp.zeros_like(gain_sum)
+
+    def input_body(r):
+        span = pl.ds(r, 16)
+        grad = partial[x, span] + from_x[span].astype(F32)
+        term, gain_term = norm_back(grad, residual[span].astype(F32), gains[0:1])
+        input_grad[span] = mixed_grad[span] + term
+        gain_sum[...] += gain_term[:8] + gain_term[8:]
+
+    loop(rows, 16, input_body)
+    for i in range(dp):
+        gain_to[i, 0:8] = gain_sum[:, i * block : (i + 1) * block]
+        gain_to[i, 8:16] = ffn_part[:, i * block : (i + 1) * block]
+    for k in range(1, dp):
+        to = (me + k) % dp
+        net.send(gain_to.at[to], gain_from.at[me], gain_sems.at[me], (to, x))
+    for i in range(half, len(items)):
+        red.step_y(i, *items[i])
+    total = gain_to[me]
+    for k in range(1, dp):
+        source = (me + k) % dp
+        net.recv(gain_from.at[source], gain_sems.at[source])
+        total = total + gain_from[source]
+    gain_x[0] = total
+    net.send(gain_x.at[0], gain_x.at[1], x_sems.at[2], net.device(x=1 - x))
+    for m in range(4):
+        red.finish(m)
+    net.recv(gain_x.at[1], x_sems.at[2])
+    gain_out[...] = gain_x[0] + gain_x[1]
+    net.drain()
+
+
+def call(kernel, collective_id, sends, locals_, vmem, outs, out_specs, scratch, sems):
+    def typed(entry):
+        return (entry[:-1], F32) if entry[-1] is F32 else (entry, BF16)
+
+    dma = pltpu.SemaphoreType.DMA
+    return lambda in_specs, *args: pl.pallas_call(
+        kernel,
+        out_shape=[jax.ShapeDtypeStruct(*typed(entry)) for entry in outs],
+        in_specs=in_specs,
+        out_specs=out_specs,
+        scratch_shapes=[pltpu.VMEM(*typed(entry)) for entry in scratch] + [dma((sends,)), dma((locals_,))] + [dma(entry) for entry in sems],
+        compiler_params=pltpu.CompilerParams(collective_id=collective_id, has_side_effects=True, vmem_limit_bytes=vmem),
+    )(*args)
+
+
+def shards(dp, residual, seg_ids, attn_gain, w_qkv, w_out, ffn_gain, w_gate_up, w_down, cotangent):
+    n = dp // 4
+    rows, width = residual.shape
+    group = seg_ids.shape[0]
+    block, cols = w_qkv.shape[1:]
+    part = w_gate_up.shape[2] // n
+    wa = jnp.concatenate([w_qkv, w_out.T[None]], axis=0)
+    wf = jnp.concatenate([w_gate_up, w_down.T[None]], axis=0)
+    seg_col = seg_ids.reshape(2, rows, 1)
+    seg_row = seg_ids.reshape(1, group)
+    gains = jnp.concatenate(
+        [jnp.broadcast_to(gain.astype(F32)[None], (8, block)) for gain in (attn_gain, ffn_gain)], axis=0
+    )
+    pairs = jnp.arange(LANES, dtype=jnp.int32) % (HD // 2)
+    freq = (ROPE_BASE ** (-(pairs.astype(F32) * 2.0 / HD)))[None]
+    mib = 1024 * 1024
+
+    first = call(
+        functools.partial(attention_kernel, dp), 1, 192, 8, 60 * mib,
+        [
+            (4, width, cols), (3, width, part), (n, 2, rows, width), (n, 2, rows, width), (group, width),
+            (group, cols), (3, group, cols), (rows, width, F32), (2, group, LANES, F32), (16, width, F32),
+        ],
+        [ANY] * 5 + [VM] * 5,
+        [
+            (4, width, cols), (group, 3 * cols, F32), (dp, 16, block, F32), (group, group, F32),
+            (rows, width), (group, width), (rows, width), (2, rows, width, F32), (rows, width), (rows, width),
+        ],
+        [(dp,), (4, n), (4, n), (4, n), (2, n), (2, n), (2,)],
+    )
+    (weights, ffn_weights, grad_all, normed_ffn, normed, attended, qkv, mixed, tables, all_gains) = first(
+        [VM] * 6 + [ANY] * 2, residual, cotangent, seg_col, seg_row, gains, freq, wa, wf
+    )
+    every = n * 2 * rows
+    items = 3 * n
+    second = call(
+        functools.partial(ffn_kernel, dp), 2, 128, 24, 63 * mib,
+        [(3, n, block, part), (rows, width), (rows, width, F32), (8, width, F32)],
+        [ANY] + [VM] * 3,
+        [
+            (3, width, part), (every, width), (every, width), (every, part), (every, 2 * part),
+            (n, 2, rows, width), (n, rows, width), (n, rows, width), (n, rows, width), (n, rows, width),
+            (items, 2, 2, block, part), (items, 2, block, part), (items, block, part),
+        ],
+        [(n,), (n,), (n,), (n,), (items,), (items,), (3, n)],
+    )
+    ffn_result, block_out, mixed_grad, ffn_part = second(
+        [VM] * 2 + [ANY] * 3, mixed, all_gains, normed_ffn.reshape(every, width), grad_all.reshape(every, width), ffn_weights
+    )
+    items = 4 * n
+    third = call(
+        functools.partial(back_kernel, dp), 3, 128, 24, 63 * mib,
+        [(4, n, block, cols), (rows, width, F32), (16, block, F32)],
+        [ANY, VM, VM],
+        [
+            (4, width, cols), (group, group, F32), (group, width), (group, cols), (3, group, cols),
+            (2, rows, width, F32), (rows, width), (rows, width),
+            (dp, 16, block, F32), (dp, 16, block, F32), (8, width, F32), (2, 16, block, F32),
+            (items, 2, 2, block, cols), (items, 2, block, cols), (items, block, cols),
+        ],
+        [(3,), (dp,), (items,), (items,), (4, n)],
+    )
+    result, input_grad, gain_grads = third(
+        [VM] * 10 + [ANY], residual, seg_col, seg_row, all_gains, tables, normed, attended, qkv, mixed_grad, ffn_part, weights
+    )
+    gain_grads = jnp.sum(gain_grads.reshape(2, 8, block), axis=1)
+    total = jnp.sum(result.astype(F32), axis=1)
+    gate_up_grad = ffn_result[:2].astype(F32).transpose(0, 2, 1, 3).reshape(2, block, n * part)
+    down_grad = ffn_result[2].astype(F32).transpose(0, 2, 1).reshape(n * part, block)
+    return (
+        block_out, input_grad, gain_grads[0], total[:3], total[3].T, gain_grads[1], gate_up_grad, down_grad,
+    )
 
 
 def positions(segments):
@@ -57,7 +894,7 @@
     return jnp.where(allowed[None], scores, -1e30)
 
 
-def shards(residual_in, seg_ids, attn_gain, w_qkv, w_out, ffn_gain, w_gate_up, w_down, cotangent):
+def plain_shards(residual_in, seg_ids, attn_gain, w_qkv, w_out, ffn_gain, w_gate_up, w_down, cotangent):
     rows_local = residual_in.shape[0]
     group_rows = seg_ids.shape[0]
     offset = lax.axis_index("tensor") * rows_local
@@ -252,4 +1089,6 @@
         P(None, "dp", "tensor"),
         P("tensor", "dp"),
     )
-    return jax.shard_map(shards, mesh=mesh, in_specs=in_specs, out_specs=out_specs, check_vma=False)
+    dp = mesh.shape["dp"]
+    local = functools.partial(shards, dp) if dp == 16 else plain_shards
+    return jax.shard_map(local, mesh=mesh, in_specs=in_specs, out_specs=out_specs, check_vma=False)

time: 2220 us -> 662 us (0.30)
  waiting for transfers between devices: 1840 us -> 0 us
  Pallas kernels: 0 us -> 622 us
  matrix products: 149 us -> 0 us
  blocking collectives: 87.3 us -> 0 us
  local copies, waits for them, and re-layouts: 82.2 us -> 23 us
    reduce_scatter x11 -> x0, waiting for transfers between devices: 1340 us -> none  [the longest x1 336 us: shards(): lax.psum_scatter(gate_up_grad[1], 'dp', scatter_dimension=0, tiled=True)]
    pallas_call x0 -> x3, Pallas kernels: none -> 622 us  [call(): pl.pallas_call(kernel, out_shape=[jax.ShapeDtypeStruct(*typed(entry)) for...]
    all_gather x8 -> x0, waiting for transfers between devices: 503 us -> none  [the longest x1 169 us: shards(): lax.all_gather(w_gate_up, 'dp', axis=1, tiled=True)]
    dot_general x18 -> x0, matrix products: 149 us -> none  [the longest x1 29.1 us: shards(): jnp.einsum('rd,cre->cde', normed_ffn_all, gate_grads, preferred_element_t...]
    squeeze x2 -> x1, local copies, waits for them, and re-layouts: 60.8 us -> 0.52 us  [shards(): gain_grads[1]]
    unnamed x1 -> x0, blocking collectives: 49.1 us -> none
    all_gather x2 -> x0, blocking collectives: 32.8 us -> none  [the longest x1 17.7 us: shards(): lax.all_gather(ffn_gain, 'dp', axis=0, tiled=True)]
  transfers between devices with their start and end apart: 19 -> 0, of which waited for: 17 -> 0; matrix products, arithmetic and copies ran while one was open for 8% -> 0% of each run, Pallas kernels for 0% -> 0%
where the time goes in v1:
time: 662 us; the launch traced here: 661 us
  Pallas kernels  622 us (94%)
  local copies, waits for them, and re-layouts  23 us (3%)
  other arithmetic  14.9 us (2%)
    pallas_call x3, Pallas kernels, call(): pl.pallas_call(kernel, out_shape=[jax.ShapeDtypeStruct(*typed(entry)) for...  622 us

profile of v1, /device:TPU:12, one launch (start us, length us, event | category | flops | bytes accessed | tf_op | source)
XLA Modules:
  0.0 660.6 jit_solution(9347719512337815245)
XLA Ops:
  0.6 0.5 fusion.3.freq
  1.2 0.8 broadcast_in_dim.8
  1.9 0.7 broadcast_in_dim.9
  2.6 0.6 pad_maximum_fusion.2.gains
  3.2 1.5 copy.30.seg_col
  4.7 1.1 copy.28
  5.7 2.2 pad_maximum_fusion.1.wa
  7.9 1.5 copy.29
  9.4 1.9 pad_maximum_fusion.wf
  11.4 245.0 %shard_map.152 = (bf16[4,2048,1024]{2,1,0:T(8,128)(2,1)}, bf16[3,2048,1024]{2,1,0:T(8,128)(2,1)}, bf16[4,2,128,2048]{3,2,1,0:T(8,128)(2,1)}, bf16[4,2,128,2048]{...) custom-call(bf16[128,2048]{1,0:T(8,128)(2,1)} %residual.3, ...), custom_call_target="tpu_custom_call" | custom-call | tf_op jit(solution)/shard_map/pallas_call | solution.py:766
  256.4 219.9 %shard_map.153 = (bf16[3,4,128,1024]{3,2,1,0:T(8,128)(2,1)}, bf16[128,2048]{1,0:T(8,128)(2,1)}, f32[128,2048]{1,0:T(8,128)}, f32[8,2048]{1,0:T(8,128)}) custom-call(f32[128,2048]{1,0:T(8,128)} %get-tuple-element.25.mixed, f32[16,2048]{1,0:T(8,128)} %get-tuple-element.26.gains, bf16[1024,2048]{1,0:T(8,128)(2,1)} %bitcast.32, bf16[1024,2048]{1,0:T(8,128)(2,1)} %bitcast.31, ...), custom_call_target="tpu_custom_call" | custom-call | tf_op jit(solution)/shard_map/pallas_call | solution.py:766
  476.2 157.2 %shard_map.154 = (bf16[4,4,128,1024]{3,2,1,0:T(8,128)(2,1)}, f32[128,2048]{1,0:T(8,128)}, f32[16,128]{1,0:T(8,128)}) custom-call(bf16[128,2048]{1,0:T(8,128)(2,1)} %residual.3, s32[2,128,1]{2,1,0:T(8,128)} %copy.30.seg_col, s32[1,256]{1,0:T(1,128)} %bitcast.37, f32[16,2048]{1,0:T(8,128)} %get-tuple-element.26.gains, ...), custom_call_target="tpu_custom_call" | custom-call | tf_op jit(solution)/shard_map/pallas_call | solution.py:766
  633.4 0.7 bitcast_reduce_fusion
  634.1 0.5 slice_bitcast_fusion.1
  634.7 3.4 convert_reduce_fusion
  638.1 1.3 slice.24
  639.5 1.0 copy.34
  640.5 1.5 convert_bitcast_fusion.1
  641.9 1.8 copy.33
  643.7 4.1 convert_bitcast_fusion
  647.8 5.3 copy.32
  653.1 5.7 copy.35
  658.9 0.8 copy.38
  659.7 1.0 copy.39
  (7 shorter events, 0.0 us)
Async XLA Ops:
  0.6 8.8 %copy-start = (bf16[2,128,4096]{2,1,0:T(8,128)(2,1)S(1)}, bf16[2,128,4096]{2,1,0:T(8,128)(2,1)}, u32[]{:S(2)}) copy-start(bf16[2,128,4096]{2,1,0:T(8,128)(2,1)} %param.15) | copy-start | bytes 6291460
  653.1 5.7 copy-start.2
  653.1 6.5 copy-start.1

commit v2 on v1

--- a/solution.py
+++ b/solution.py
@@ -71,6 +71,7 @@
         )
         when(cond, copy.start)
         self.pending.append((cond, copy))
+        return self.pending[-1]
 
     def recv(self, dst, recv_sem):
         pltpu.make_async_remote_copy(
@@ -84,11 +85,15 @@
         copy = pltpu.make_async_copy(src, dst, sem)
         when(cond, copy.start)
         self.kept.append((cond, copy))
-        return copy
-
-    def settle(self, copy):
-        self.kept = [entry for entry in self.kept if entry[1] is not copy]
-        copy.wait()
+        return self.kept[-1]
+
+    def settle(self, entry):
+        for entries, wait in ((self.kept, "wait"), (self.pending, "wait_send")):
+            for k, known in enumerate(entries):
+                if known is entry:
+                    when(entry[0], getattr(entry[1], wait))
+                    del entries[k]
+                    return
 
     def drain(self):
         assert self.sent <= self.send_sems.shape[0] and self.moved <= self.local_sems.shape[0]
@@ -222,9 +227,16 @@
 
 
 class Reduce:
-    def __init__(self, net, part, from_c, from_y, result, sems):
-        self.net, self.part, self.from_c, self.from_y, self.result = net, part, from_c, from_y, result
-        self.cs, self.ys, self.zs = sems
+    def __init__(self, net, part, from_c, from_y, result, line, sems, total):
+        self.net, self.part, self.from_c, self.from_y = net, part, from_c, from_y
+        self.result, self.totals = result
+        self.line = line
+        self.cs, self.ys, self.zs, self.ls, self.free = sems
+        self.slots = part.shape[0]
+        self.total = total
+        self.items = []
+        self.out = {}
+        self.done_c = self.done_y = self.done_z = 0
 
     def add(self, total, term):
         def body(r):
@@ -233,32 +245,104 @@
 
         loop(total.shape[0], 16, body)
 
-    def start(self, i):
-        net = self.net
-        net.send(self.part.at[i, 1 - net.c], self.from_c.at[i], self.cs.at[i], net.device(c=1 - net.c))
-
-    def step_c(self, i):
-        net = self.net
-        net.recv(self.from_c.at[i], self.cs.at[i])
+    def credit(self, which, device):
+        pl.semaphore_signal(self.free.at[which], inc=1, device_id=device, device_id_type=MESH)
+
+    def item(self, matrix, to, left, right, depth, block):
+        net = self.net
+        i = len(self.items)
+        slot = i % self.slots
+        self.items.append((matrix, to))
+        assert self.done_z > i - self.slots
+        for entry in self.out.pop(i - self.slots, ()):
+            net.settle(entry)
+
+        def body(col):
+            term = dot(left, right[:, pl.ds(col, 256)], TN).astype(BF16)
+            for y in (0, 1):
+                for c in (0, 1):
+                    at = (y * 2 + c) * block
+                    self.part[slot, c, y, :, pl.ds(col, 256)] = term[at : at + block]
+
+        loop(right.shape[1], 256, body)
+        if i >= self.slots:
+            pl.semaphore_wait(self.free.at[0], 1)
+        self.out[i] = [
+            net.send(self.part.at[slot, 1 - net.c], self.from_c.at[slot], self.cs.at[slot], net.device(c=1 - net.c))
+        ]
+
+    def step_c(self):
+        net = self.net
+        i = self.done_c
+        self.done_c += 1
+        slot = i % self.slots
+        net.recv(self.from_c.at[slot], self.cs.at[slot])
         for y in (0, 1):
-            self.add(self.part.at[i, net.c, y], self.from_c.at[i, y])
-        net.send(self.part.at[i, net.c, 1 - net.y], self.from_y.at[i], self.ys.at[i], net.device(y=1 - net.y))
-
-    def step_y(self, i, matrix, to):
-        net = self.net
-        net.recv(self.from_y.at[i], self.ys.at[i])
-        self.add(self.part.at[i, net.c, net.y], self.from_y.at[i])
-        src = self.part.at[i, net.c, net.y]
+            self.add(self.part.at[slot, net.c, y], self.from_c.at[slot, y])
+        if i + self.slots < self.total:
+            self.credit(0, net.device(c=1 - net.c))
+        if i >= self.slots:
+            pl.semaphore_wait(self.free.at[1], 1)
+        self.out[i].append(
+            net.send(self.part.at[slot, net.c, 1 - net.y], self.from_y.at[slot], self.ys.at[slot], net.device(y=1 - net.y))
+        )
+
+    def step_y(self):
+        net = self.net
+        i = self.done_y
+        self.done_y += 1
+        slot = i % self.slots
+        matrix, to = self.items[i]
+        net.recv(self.from_y.at[slot], self.ys.at[slot])
+        self.add(self.part.at[slot, net.c, net.y], self.from_y.at[slot])
+        if i + self.slots < self.total:
+            self.credit(1, net.device(y=1 - net.y))
+        matrices = self.result.shape[0]
+        if matrix >= matrices:
+            return
+        src = self.part.at[slot, net.c, net.y]
         dst = self.result.at[matrix, net.z]
         away = to != net.z
-        net.send(src, dst, self.zs.at[matrix, net.z], net.device(z=to), away)
-        net.local(src, dst, jnp.logical_not(away))
-
-    def finish(self, matrix):
-        net = self.net
-        for d in range(1, net.n):
-            block = (net.z + d) % net.n
-            net.recv(self.result.at[matrix, block], self.zs.at[matrix, block])
+        self.out[i].append(net.send(src, dst, self.zs.at[matrix, net.z], net.device(z=to), away))
+        self.out[i].append(net.local(src, dst, jnp.logical_not(away)))
+        self.done_z += 1
+
+    def step_z(self):
+        net = self.net
+        i = self.done_z
+        self.done_z += 1
+        assert i < self.done_y
+        matrix, to = self.items[i]
+        m = matrix - self.result.shape[0]
+        total = self.part.at[i % self.slots, net.c, net.y]
+        behind = jnp.where(to > net.z, net.z > 0, net.z < net.n - 1)
+        place = self.line(m, to)
+
+        @pl.when(jnp.logical_and(to != net.z, behind))
+        def _():
+            net.recv(place, self.ls.at[m, to])
+            self.add(total, place)
+
+        side = jnp.where(to > net.z, 0, 1)
+        nxt = jnp.where(to > net.z, net.z + 1, net.z - 1)
+        there = net.device(z=nxt)
+        last = jnp.logical_and(to != net.z, to == nxt)
+        self.out[i].append(net.send(total, place, self.ls.at[m, to], there, jnp.logical_and(to != net.z, to != nxt)))
+        self.out[i].append(net.send(total, self.totals.at[m, side], self.ls.at[m, net.n + side], there, last))
+        self.out[i].append(net.local(total, self.totals.at[m, 2], to == net.z))
+
+    def finish(self):
+        net = self.net
+        for matrix in range(self.result.shape[0]):
+            for d in range(1, net.n):
+                block = (net.z + d) % net.n
+                net.recv(self.result.at[matrix, block], self.zs.at[matrix, block])
+        for m in range(self.totals.shape[0]):
+            for side, cond in ((0, net.z > 0), (1, net.z < net.n - 1)):
+
+                @pl.when(cond)
+                def _():
+                    net.recv(self.totals.at[m, side], self.ls.at[m, net.n + side])
 
 
 def loop(total, step, body):
@@ -455,40 +539,64 @@
     net.drain()
 
 
+def far_first(net):
+    n = net.n
+    table = [sorted(range(n), key=lambda b: (-abs(b - z), -b)) for z in range(n)]
+    return [sum(jnp.where(net.z == z, table[z][k], 0) for z in range(n)) for k in range(n)]
+
+
 class RowSum:
-    def __init__(self, net, part, from_x, from_z, sems):
-        self.net, self.part, self.from_x, self.from_z = net, part, from_x, from_z
+    def __init__(self, net, order, part, from_x, from_z, sems):
+        self.net, self.order, self.part, self.from_x, self.from_z = net, order, part, from_x, from_z
         self.xs, self.zs = sems
+        self.sent = []
+        self.done_x = self.done_z = 0
 
     def start(self, b):
         net = self.net
-        net.send(self.part(b, 1 - net.x), self.from_x.at[b], self.xs.at[b], net.device(x=1 - net.x))
-
-    def step(self, b, own):
-        net = self.net
-        net.recv(self.from_x.at[b], self.xs.at[b])
-        total, term = self.part(b, net.x), self.from_x.at[b]
-
+        self.sent.append(
+            net.send(self.part(b, 1 - net.x), self.from_x.at[b], self.xs.at[b], net.device(x=1 - net.x))
+        )
+
+    def add(self, total, term):
         def body(r):
             span = pl.ds(r, 16)
             total[span] = (total[span].astype(F32) + term[span].astype(F32)).astype(BF16)
 
         loop(total.shape[0], 16, body)
-        if not own:
-            net.send(total, self.from_z.at[net.z], self.zs.at[net.z], net.device(z=b))
+
+    def step_x(self):
+        net = self.net
+        b = self.order[self.done_x]
+        self.done_x += 1
+        net.recv(self.from_x.at[b], self.xs.at[b])
+        self.add(self.part(b, net.x), self.from_x.at[b])
+
+    def step_z(self):
+        net = self.net
+        b = self.order[self.done_z]
+        self.done_z += 1
+        total = self.part(b, net.x)
+        behind = jnp.where(b > net.z, net.z > 0, net.z < net.n - 1)
+
+        @pl.when(jnp.logical_and(b != net.z, behind))
+        def _():
+            net.recv(self.from_z.at[b], self.zs.at[b])
+            self.add(total, self.from_z.at[b])
+
+        slot = jnp.where(b == net.z - 1, net.n, b)
+        to = jnp.where(b > net.z, net.z + 1, net.z - 1)
+        self.sent.append(net.send(total, self.from_z.at[slot], self.zs.at[slot], net.device(z=to), b != net.z))
 
     def finish(self):
         net = self.net
-        for d in range(1, net.n):
-            b = (net.z + d) % net.n
-            net.recv(self.from_z.at[b], self.zs.at[b])
-
-    def total(self, span):
-        net = self.net
-        value = self.part(net.z, net.x)[span].astype(F32)
-        for d in range(1, net.n):
-            value = value + self.from_z[(net.z + d) % net.n, span].astype(F32)
-        return value
+        total = self.part(net.z, net.x)
+        for slot, cond in ((net.z, net.z > 0), (net.n, net.z < net.n - 1)):
+
+            @pl.when(cond)
+            def _():
+                net.recv(self.from_z.at[slot], self.zs.at[slot])
+                self.add(total, self.from_z.at[slot])
 
 
 def norm_back(grad, value, gain):
@@ -499,55 +607,61 @@
     return back, grad * unit
 
 
-def weight_item(red, i, left, right, base, depth, block):
-    def body(col):
-        term = dot(left[:, pl.ds(base, depth)], right[:, pl.ds(col, 256)], TN).astype(BF16)
-        for y in (0, 1):
-            for c in (0, 1):
-                at = (y * 2 + c) * block
-                red.part[i, c, y, :, pl.ds(col, 256)] = term[at : at + block]
-
-    loop(right.shape[1], 256, body)
-
-
 def ffn_kernel(
     dp,
-    mixed, gains, normed_hbm, grad_hbm, wf,
-    result, block_out, mixed_grad, gain_part,
-    weights, normed, grad, hidden, gate_up_grad, back, back_x, back_z, add_x, add_z, part, from_c, from_y,
-    send_sems, local_sems, bx_sems, bz_sems, ax_sems, az_sems, rc_sems, ry_sems, rz_sems,
+    mixed, residual, gains, seg_col, seg_row, tables, normed_ffn_hbm, grad_hbm, wf, normed_hbm, attended_hbm, qkv_hbm, wa,
+    result, totals, block_out, input_grad, gain_out,
+    weights, grad, hidden, gate_up_grad, back, back_x, back_z, part, from_c, from_y,
+    mixed_all, allowed, from_x, gain_sum, ffn_sum, gain_to, gain_from, gain_x,
+    send_sems, local_sems, bx_sems, bz_sems, rc_sems, ry_sems, rz_sems, rl_sems, x_sems, gain_sems, free,
 ):
     net = Net(dp, send_sems, local_sems)
-    n = net.n
+    n, me, x = net.n, net.dp_index, net.x
     rows, width = mixed.shape
     cols = wf.shape[2]
+    every = grad.shape[0]
     block = width // dp
     depth = width // n
     pair = 2 * rows
-    loads = [net.local(normed_hbm, normed), net.local(wf, weights), net.local(grad_hbm, grad)]
+    assert width == 2 * cols and width == 2 * every and wa.shape[2] == cols
+
+    def features(half):
+        return weights.at[3, pl.ds(half * every, every)]
+
+    loads = [net.local(normed_ffn_hbm.at[:, pl.ds(half * cols, cols)], features(half)) for half in (0, 1)]
+    loads += [net.local(wf.at[m], weights.at[m]) for m in range(3)] + [net.local(grad_hbm, grad)]
     net.greet(
-        [net.device(z=(net.z + d) % n) for d in range(1, n)]
-        + [net.device(y=1 - net.y), net.device(c=1 - net.c), net.device(x=1 - net.x)]
-    )
+        [((me + k) % dp, x) for k in range(1, dp)] + [(me, 1 - x)]
+    )
+    order = far_first(net)
+    beside = jnp.where(net.z > 0, 1, 0) + jnp.where(net.z < n - 1, 1, 0)
     gate_grad, up_grad = gate_up_grad.at[:, pl.ds(0, cols)], gate_up_grad.at[:, pl.ds(cols, cols)]
     add = gate_up_grad
-    backs = RowSum(net, lambda b, half: back.at[b, half], back_x, back_z, (bx_sems, bz_sems))
+    backs = RowSum(net, order, lambda b, half: back.at[b, half], back_x, back_z, (bx_sems, bz_sems))
     adds = RowSum(
-        net, lambda b, half: add.at[pl.ds(pl.multiple_of((b * 2 + half) * rows, rows), rows)], add_x, add_z, (ax_sems, az_sems)
-    )
-    red = Reduce(net, part, from_c, from_y, result, (rc_sems, ry_sems, rz_sems))
+        net, order, lambda b, half: add.at[pl.ds(pl.multiple_of((b * 2 + half) * rows, rows), rows)],
+        back_x, back_z, (bx_sems, bz_sems),
+    )
+    red = Reduce(
+        net, part, from_c, from_y, (result, totals),
+        lambda m, to: weights.at[3, pl.ds(pl.multiple_of((m * n + to) * block, block), block)],
+        (rc_sems, ry_sems, rz_sems, rl_sems, free), 7 * n,
+    )
     for load in loads:
         net.settle(load)
 
-    order = sorted(range(n), key=lambda d: -min(d, n - d))
-
     def chunk(b):
         here = pl.ds(pl.multiple_of(b * pair, pair), pair)
 
         def hidden_body(col):
             span = pl.ds(col, 256)
-            gate = dot(normed[here], weights[0, :, span])
-            up = dot(normed[here], weights[1, :, span])
+
+            def project(m):
+                return dot(features(0)[here], weights[m, pl.ds(0, cols), span]) + dot(
+                    features(1)[here], weights[m, pl.ds(cols, cols), span]
+                )
+
+            gate, up = project(0), project(1)
             hidden_grad = dot(grad[here], weights[2, :, span])
             sigmoid = 1.0 / (1.0 + jnp.exp(-gate))
             active = gate * sigmoid
@@ -572,122 +686,119 @@
 
         def body(col):
             span = pl.ds(col, 256)
-            term = dot(hidden[here], weights[2, span, :], NT).astype(BF16)
-            add[here, span] = term
+            add[here, span] = dot(hidden[here], weights[2, span, :], NT).astype(BF16)
 
         loop(width, 256, body)
-        adds.start(b)
-
-    for k, d in enumerate(order):
-        chunk((net.z + d) % n)
+
+    def ffn_items(b):
+        base = b * depth
+        col = pl.ds(pl.multiple_of(base % cols, depth), depth)
+        row = pl.ds(pl.multiple_of(base // cols * every, every), every)
+        own = pl.ds(pl.multiple_of(base, depth), depth)
+        for m in (2, 0, 1):
+            left = grad[:, own] if m == 2 else weights[3, row, col]
+            red.item(m, b, left, (gate_grad, up_grad, hidden)[m], depth, block)
+            if len(red.items) > 1:
+                red.step_c()
+
+    for k in range(n):
+        chunk(order[k])
         if k > 0:
-            backs.step((net.z + order[k - 1]) % n, order[k - 1] == 0)
-    items = []
-    for d in order:
-        b = (net.z + d) % n
-        for m in (2, 0, 1):
-            i = len(items)
-            left, right = ((normed, gate_grad), (normed, up_grad), (grad, hidden))[m]
-            weight_item(red, i, left, right, pl.multiple_of(b * depth, depth), depth, block)
-            red.start(i)
-            if i > 0:
-                red.step_c(i - 1)
-            if i == 1:
-                backs.step((net.z + order[-1]) % n, order[-1] == 0)
-            items.append((m, b))
-    red.step_c(len(items) - 1)
-    for k, d in enumerate(order):
-        add_chunk((net.z + d) % n)
-        if k > 0:
-            adds.step((net.z + order[k - 1]) % n, order[k - 1] == 0)
+            backs.step_x()
+        if k > 1:
+            backs.step_z()
+    ffn_items(order[0])
+    backs.step_x()
+    backs.step_z()
+    ffn_items(order[1])
+    backs.step_z()
+    red.step_y()
+    for k in range(2, n):
+        ffn_items(order[k])
+        red.step_y()
+    red.step_c()
+    load_out = net.local(wa.at[3], weights.at[3])
     backs.finish()
-    gain_part[...] = jnp.zeros_like(gain_part)
+    ffn_sum[...] = jnp.zeros_like(ffn_sum)
 
     def mixed_body(r):
         span = pl.ds(r, 16)
-        own = pl.ds(pl.multiple_of((net.z * 2 + net.x) * rows + r, 16), 16)
-        term, gain_term = norm_back(backs.total(span), mixed[span], gains[8:9])
-        mixed_grad[span] = grad[own].astype(F32) + term
-        gain_part[...] += gain_term[:8] + gain_term[8:]
+        own = pl.ds(pl.multiple_of((net.z * 2 + x) * rows + r, 16), 16)
+        term, gain_term = norm_back(back[net.z, x, span].astype(F32), mixed[span], gains[8:9])
+        value = grad[own].astype(F32) + term
+        input_grad[span] = value
+        mixed_all[pl.ds(pl.multiple_of(x * rows + r, 16), 16)] = value.astype(BF16)
+        ffn_sum[...] += gain_term[:8] + gain_term[8:]
 
     loop(rows, 16, mixed_body)
-    adds.step((net.z + order[-1]) % n, order[-1] == 0)
-    for i, (m, b) in enumerate(items):
-        red.step_y(i, m, b)
-    adds.finish()
-
-    def block_body(r):
-        span = pl.ds(r, 16)
-        block_out[span] = (mixed[span] + adds.total(span)).astype(BF16)
-
-    loop(rows, 16, block_body)
-    for m in range(3):
-        red.finish(m)
-    net.drain()
-
-
-def back_kernel(
-    dp,
-    residual, seg_col, seg_row, gains, tables, normed, attended, qkv, mixed_grad, ffn_part, wa,
-    result, input_grad, gain_out,
-    weights, allowed, mixed_all, attended_grad, qkv_grad, partial, to_x, from_x, gain_to, gain_from, gain_sum, gain_x,
-    part, from_c, from_y,
-    send_sems, local_sems, x_sems, gain_sems, rc_sems, ry_sems, rz_sems,
-):
-    net = Net(dp, send_sems, local_sems)
-    n = net.n
-    me, x = net.dp_index, net.x
-    rows, width = residual.shape
-    group = 2 * rows
-    cols = wa.shape[2]
-    block = width // dp
-    depth = width // n
-    load_out = net.local(wa.at[3], weights.at[3])
-    load_qkv = net.local(wa.at[pl.ds(0, 3)], weights.at[pl.ds(0, 3)])
-    net.greet([((me + k) % dp, x) for k in range(1, dp)] + [(me, 1 - x)])
-    red = Reduce(net, part, from_c, from_y, result, (rc_sems, ry_sems, rz_sems))
-
-    def low_body(r):
-        to = pl.multiple_of(x * rows + r, 16)
-        mixed_all[pl.ds(to, 16)] = mixed_grad[pl.ds(r, 16)].astype(BF16)
-
-    loop(rows, 16, low_body)
     own_rows = mixed_all.at[pl.ds(pl.multiple_of(x * rows, rows), rows)]
     other_rows = mixed_all.at[pl.ds(pl.multiple_of((1 - x) * rows, rows), rows)]
     net.send(own_rows, own_rows, x_sems.at[0], net.device(x=1 - x))
+    pl.semaphore_signal(free.at[2], inc=1, device_id=net.device(x=1 - x), device_id_type=MESH)
+    for cond, z in ((net.z > 0, net.z - 1), (net.z < n - 1, net.z + 1)):
+
+        @pl.when(cond)
+        def _():
+            pl.semaphore_signal(free.at[3], inc=1, device_id=net.device(z=z), device_id_type=MESH)
+
+    for k in range(n):
+        add_chunk(order[k])
+        red.step_y()
+    pl.semaphore_wait(free.at[2], 1)
+    load_qkv = net.local(wa.at[pl.ds(0, 3)], weights.at[pl.ds(0, 3)])
+    load_parts = [net.local(qkv_hbm.at[m], hidden.at[pl.ds(m * pair, pair)]) for m in range(3)]
+    load_attended = net.local(attended_hbm, hidden.at[pl.ds(3 * pair, pair)])
+    load_normed = net.local(normed_hbm, grad.at[pl.ds(0, pair)])
+    queries_of, keys_of, values_of = [hidden.at[pl.ds(m * pair, pair)] for m in range(3)]
+    attended = hidden.at[pl.ds(3 * pair, pair)]
+    normed = grad.at[pl.ds(0, pair)]
+    grads_of = [
+        grad.at[pl.ds(2 * pair, pair), pl.ds(0, cols)],
+        grad.at[pl.ds(2 * pair, pair), pl.ds(cols, cols)],
+        grad.at[pl.ds(3 * pair, pair), pl.ds(0, cols)],
+    ]
+    attended_grad = grad.at[pl.ds(3 * pair, pair), pl.ds(cols, cols)]
+
     row_seg = jnp.concatenate([seg_col[0], seg_col[1]], axis=0)
-    row_id = lax.broadcasted_iota(jnp.int32, (group, group), 0)
-    col_id = lax.broadcasted_iota(jnp.int32, (group, group), 1)
+    row_id = lax.broadcasted_iota(jnp.int32, (pair, pair), 0)
+    col_id = lax.broadcasted_iota(jnp.int32, (pair, pair), 1)
     allowed[...] = jnp.logical_and(row_seg == seg_row[...], row_id >= col_id).astype(F32)
     net.settle(load_out)
     net.recv(other_rows, x_sems.at[0])
+    for k in range(n):
+        adds.start(order[k])
 
     def attended_body(col):
         span = pl.ds(col, 256)
         attended_grad[:, span] = dot(mixed_all[...], weights[3, :, span]).astype(BF16)
 
     loop(cols, 256, attended_body)
-    order = sorted(range(n), key=lambda d: -min(d, n - d))
-    items = []
-
-    def emit(m, left, right):
-        for d in order:
-            b = (net.z + d) % n
-            i = len(items)
-            weight_item(red, i, left, right, pl.multiple_of(b * depth, depth), depth, block)
-            red.start(i)
-            if i > 0:
-                red.step_c(i - 1)
-            items.append((m, b))
-
-    emit(3, mixed_all, attended)
+    for cond, z in ((net.z > 0, net.z - 1), (net.z < n - 1, net.z + 1)):
+
+        @pl.when(cond)
+        def _():
+            pl.semaphore_signal(free.at[4], inc=1, device_id=net.device(z=z), device_id_type=MESH)
+
+    net.settle(load_attended)
+
+    def attention_items(m, left, right):
+        for k in range(n):
+            base = pl.ds(pl.multiple_of(order[k] * depth, depth), depth)
+            red.item(3 + m, order[k], left[:, base], right, depth, block)
+            if red.done_c < len(red.items) - 1:
+                red.step_c()
+
+    attention_items(3, mixed_all, attended)
+    red.step_c()
+    for load in load_parts:
+        net.settle(load)
     masks = head_masks()
-    lane = lax.broadcasted_iota(jnp.int32, (group, LANES), 1)
+    lane = lax.broadcasted_iota(jnp.int32, (pair, LANES), 1)
 
     def head_body(col):
         span = pl.ds(col, LANES)
         cosine, sine = tables[0], tables[1]
-        queries, key_rows, value_rows = qkv[0, :, span], qkv[1, :, span], qkv[2, :, span]
+        queries, key_rows, value_rows = queries_of[:, span], keys_of[:, span], values_of[:, span]
         out_grad = attended_grad[:, span]
         queries2, out_grad2 = both(queries, masks), both(out_grad, masks)
         may = jnp.concatenate([allowed[...], allowed[...]], axis=0)
@@ -696,54 +807,79 @@
         prob_grad = dot(out_grad2, value_rows, NT)
         score_grad = probs * (prob_grad - jnp.sum(probs * prob_grad, axis=-1, keepdims=True))
         score_grad = score_grad.astype(BF16)
-        query_grad = pick(dot(score_grad, key_rows), group) * HD ** (-0.5)
+        query_grad = pick(dot(score_grad, key_rows), pair) * HD ** (-0.5)
         key_grad = dot(score_grad, queries2, TN) * HD ** (-0.5)
-        qkv_grad[0, :, span] = turn(query_grad, cosine, -sine, lane).astype(BF16)
-        qkv_grad[1, :, span] = turn(key_grad, cosine, -sine, lane).astype(BF16)
-        qkv_grad[2, :, span] = value_grad.astype(BF16)
+        grads_of[0][:, span] = turn(query_grad, cosine, -sine, lane).astype(BF16)
+        grads_of[1][:, span] = turn(key_grad, cosine, -sine, lane).astype(BF16)
+        grads_of[2][:, span] = value_grad.astype(BF16)
 
     loop(cols, LANES, head_body)
     net.settle(load_qkv)
+    net.settle(load_normed)
+    while red.done_y < 3 * n:
+        red.step_y()
+    attention_items(0, normed, grads_of[0])
+    pl.semaphore_wait(free.at[4], beside)
+
+    red.step_y()
+    red.step_y()
+    red.step_z()
+    attention_items(1, normed, grads_of[1])
+    red.step_y()
+    red.step_z()
+    red.step_y()
+    red.step_z()
+    red.step_z()
+    attention_items(2, normed, grads_of[2])
+    red.step_c()
+    for entry in backs.sent:
+        net.settle(entry)
 
     def normed_body(col):
         span = pl.ds(col, 256)
-        term = dot(qkv_grad[0], weights[0, span, :], NT)
-        term += dot(qkv_grad[1], weights[1, span, :], NT)
-        term += dot(qkv_grad[2], weights[2, span, :], NT)
-        partial[0, :, span] = term[:rows]
-        partial[1, :, span] = term[rows:]
-
-    def to_body(r):
-        to_x[pl.ds(r, 16)] = partial[1 - x, pl.ds(r, 16)].astype(BF16)
-
-    for m in range(3):
-        emit(m, normed, qkv_grad.at[m])
-    red.step_c(len(items) - 1)
+        term = dot(grads_of[0][...], weights[0, span, :], NT)
+        term += dot(grads_of[1][...], weights[1, span, :], NT)
+        term += dot(grads_of[2][...], weights[2, span, :], NT)
+        back[0, 0, :, span] = term[:rows].astype(BF16)
+        back[0, 1, :, span] = term[rows:].astype(BF16)
+
     loop(width, 256, normed_body)
-    loop(rows, 16, to_body)
-    net.send(to_x, from_x, x_sems.at[1], net.device(x=1 - x))
-    half = len(items) // 2
-    for i in range(half):
-        red.step_y(i, *items[i])
+    net.send(back.at[0, 1 - x], from_x, x_sems.at[1], net.device(x=1 - x))
     net.recv(from_x, x_sems.at[1])
     gain_sum[...] = jnp.zeros_like(gain_sum)
 
     def input_body(r):
         span = pl.ds(r, 16)
-        grad = partial[x, span] + from_x[span].astype(F32)
-        term, gain_term = norm_back(grad, residual[span].astype(F32), gains[0:1])
-        input_grad[span] = mixed_grad[span] + term
+        grad_rows = back[0, x, span].astype(F32) + from_x[span].astype(F32)
+        term, gain_term = norm_back(grad_rows, residual[span].astype(F32), gains[0:1])
+        input_grad[span] += term
         gain_sum[...] += gain_term[:8] + gain_term[8:]
 
     loop(rows, 16, input_body)
     for i in range(dp):
         gain_to[i, 0:8] = gain_sum[:, i * block : (i + 1) * block]
-        gain_to[i, 8:16] = ffn_part[:, i * block : (i + 1) * block]
+        gain_to[i, 8:16] = ffn_sum[:, i * block : (i + 1) * block]
     for k in range(1, dp):
         to = (me + k) % dp
         net.send(gain_to.at[to], gain_from.at[me], gain_sems.at[me], (to, x))
-    for i in range(half, len(items)):
-        red.step_y(i, *items[i])
+    pl.semaphore_wait(free.at[3], beside)
+
+    for k in range(n):
+        adds.step_x()
+        red.step_y()
+        if red.done_z < red.done_y - 1:
+            red.step_z()
+    for k in range(n):
+        red.step_y()
+        adds.step_z()
+        red.step_z()
+    adds.finish()
+
+    def block_body(r):
+        span = pl.ds(r, 16)
+        block_out[span] = (mixed[span] + adds.part(net.z, x)[span].astype(F32)).astype(BF16)
+
+    loop(rows, 16, block_body)
     total = gain_to[me]
     for k in range(1, dp):
         source = (me + k) % dp
@@ -751,14 +887,38 @@
         total = total + gain_from[source]
     gain_x[0] = total
     net.send(gain_x.at[0], gain_x.at[1], x_sems.at[2], net.device(x=1 - x))
-    for m in range(4):
-        red.finish(m)
+    while red.done_y < len(red.items):
+        red.step_y()
+        red.step_z()
+    red.step_z()
     net.recv(gain_x.at[1], x_sems.at[2])
     gain_out[...] = gain_x[0] + gain_x[1]
+    red.finish()
     net.drain()
 
 
-def call(kernel, collective_id, sends, locals_, vmem, outs, out_specs, scratch, sems):
+def finish_kernel(ffn, attention, gains, qkv_grad, out_grad, gate_up_grad, down_grad, gain_sums):
+    q, n = pl.program_id(0), pl.num_programs(0)
+    z = lax.axis_index("dp") // 4
+    gate_up_grad[...] = ffn[0:2, 0].astype(F32)
+    down_grad[...] = ffn[2, 0].astype(F32).T
+    total = attention[0, 2].astype(F32)
+    total += jnp.where(z > 0, attention[0, 0].astype(F32), 0.0)
+    total += jnp.where(z < n - 1, attention[0, 1].astype(F32), 0.0)
+
+    @pl.when(q < 3)
+    def _():
+        qkv_grad[0] = total
+
+    @pl.when(q == 3)
+    def _():
+        out_grad[...] = total.T
+
+    gain_sums[0:1] = jnp.sum(gains[0:8], axis=0, keepdims=True)
+    gain_sums[1:2] = jnp.sum(gains[8:16], axis=0, keepdims=True)
+
+
+def call(kernel, collective_id, sends, locals_, vmem, outs, out_specs, scratch, sems, flags=0):
     def typed(entry):
         return (entry[:-1], F32) if entry[-1] is F32 else (entry, BF16)
 
@@ -768,7 +928,7 @@
         out_shape=[jax.ShapeDtypeStruct(*typed(entry)) for entry in outs],
         in_specs=in_specs,
         out_specs=out_specs,
-        scratch_shapes=[pltpu.VMEM(*typed(entry)) for entry in scratch] + [dma((sends,)), dma((locals_,))] + [dma(entry) for entry in sems],
+        scratch_shapes=[pltpu.VMEM(*typed(entry)) for entry in scratch] + [dma((sends,)), dma((locals_,))] + [dma(entry) for entry in sems] + [pltpu.SemaphoreType.REGULAR((flags,))] * (flags > 0),
         compiler_params=pltpu.CompilerParams(collective_id=collective_id, has_side_effects=True, vmem_limit_bytes=vmem),
     )(*args)
 
@@ -807,44 +967,47 @@
         [VM] * 6 + [ANY] * 2, residual, cotangent, seg_col, seg_row, gains, freq, wa, wf
     )
     every = n * 2 * rows
-    items = 3 * n
+    slots = 3 * n
     second = call(
-        functools.partial(ffn_kernel, dp), 2, 128, 24, 63 * mib,
-        [(3, n, block, part), (rows, width), (rows, width, F32), (8, width, F32)],
-        [ANY] + [VM] * 3,
+        functools.partial(ffn_kernel, dp), 2, 192, 64, 63 * mib,
+        [(3, n, block, part), (4, 3, block, cols), (rows, width), (rows, width, F32), (16, block, F32)],
+        [ANY] * 2 + [VM] * 3,
         [
-            (3, width, part), (every, width), (every, width), (every, part), (every, 2 * part),
-            (n, 2, rows, width), (n, rows, width), (n, rows, width), (n, rows, width), (n, rows, width),
-            (items, 2, 2, block, part), (items, 2, block, part), (items, block, part),
+            (4, width, part), (every, width), (every, part), (every, 2 * part),
+            (n, 2, rows, width), (n, rows, width), (n + 1, rows, width),
+            (slots, 2, 2, block, part), (slots, 2, block, part), (slots, block, part),
+            (group, width), (group, group, F32), (rows, width), (8, width, F32), (8, width, F32),
+            (dp, 16, block, F32), (dp, 16, block, F32), (2, 16, block, F32),
         ],
-        [(n,), (n,), (n,), (n,), (items,), (items,), (3, n)],
-    )
-    ffn_result, block_out, mixed_grad, ffn_part = second(
-        [VM] * 2 + [ANY] * 3, mixed, all_gains, normed_ffn.reshape(every, width), grad_all.reshape(every, width), ffn_weights
-    )
-    items = 4 * n
-    third = call(
-        functools.partial(back_kernel, dp), 3, 128, 24, 63 * mib,
-        [(4, n, block, cols), (rows, width, F32), (16, block, F32)],
-        [ANY, VM, VM],
-        [
-            (4, width, cols), (group, group, F32), (group, width), (group, cols), (3, group, cols),
-            (2, rows, width, F32), (rows, width), (rows, width),
-            (dp, 16, block, F32), (dp, 16, block, F32), (8, width, F32), (2, 16, block, F32),
-            (items, 2, 2, block, cols), (items, 2, block, cols), (items, block, cols),
+        [(n,), (n + 1,), (slots,), (slots,), (3, n), (4, n + 2), (3,), (dp,)],
+        5,
+    )
+    result, totals, block_out, input_grad, gain_grads = second(
+        [VM] * 6 + [ANY] * 7, mixed, residual, all_gains, seg_col, seg_row, tables, normed_ffn.reshape(every, width),
+        grad_all.reshape(every, width), ffn_weights, normed, attended, qkv, weights,
+    )
+    qkv_grad, out_grad, gate_up_grad, down_grad, gain_sums = pl.pallas_call(
+        finish_kernel,
+        grid=(n,),
+        out_shape=[
+            jax.ShapeDtypeStruct(entry, F32)
+            for entry in ((3, block, cols), (cols, block), (2, block, n * part), (n * part, block), (2, block))
         ],
-        [(3,), (dp,), (items,), (items,), (4, n)],
-    )
-    result, input_grad, gain_grads = third(
-        [VM] * 10 + [ANY], residual, seg_col, seg_row, all_gains, tables, normed, attended, qkv, mixed_grad, ffn_part, weights
-    )
-    gain_grads = jnp.sum(gain_grads.reshape(2, 8, block), axis=1)
-    total = jnp.sum(result.astype(F32), axis=1)
-    gate_up_grad = ffn_result[:2].astype(F32).transpose(0, 2, 1, 3).reshape(2, block, n * part)
-    down_grad = ffn_result[2].astype(F32).transpose(0, 2, 1).reshape(n * part, block)
-    return (
-        block_out, input_grad, gain_grads[0], total[:3], total[3].T, gain_grads[1], gate_up_grad, down_grad,
-    )
+        in_specs=[
+            pl.BlockSpec((3, 1, block, part), lambda q: (0, q, 0, 0)),
+            pl.BlockSpec((1, 3, block, cols), lambda q: (q, 0, 0, 0)),
+            pl.BlockSpec((16, block), lambda q: (0, 0)),
+        ],
+        out_specs=[
+            pl.BlockSpec((1, block, cols), lambda q: (jnp.minimum(q, 2), 0, 0)),
+            pl.BlockSpec((cols, block), lambda q: (0, 0)),
+            pl.BlockSpec((2, block, part), lambda q: (0, 0, q)),
+            pl.BlockSpec((part, block), lambda q: (q, 0)),
+            pl.BlockSpec((2, block), lambda q: (0, 0)),
+        ],
+        compiler_params=pltpu.CompilerParams(vmem_limit_bytes=32 * mib),
+    )(result, totals, gain_grads)
+    return block_out, input_grad, gain_sums[0], qkv_grad, out_grad, gain_sums[1], gate_up_grad, down_grad
 
 
 def positions(segments):

time: 662 us -> 560 us (0.85)
  Pallas kernels: 622 us -> 539 us
  local copies, waits for them, and re-layouts: 23 us -> 12.2 us
  other arithmetic: 14.9 us -> 5.26 us
    pallas_call x3 -> x2, Pallas kernels: 622 us -> 534 us  [call(): pl.pallas_call(kernel, out_shape=[jax.ShapeDtypeStruct(*typed(entry)) for...]
    reshape x2 -> x0, local copies, waits for them, and re-layouts: 7.14 us -> none  [the longest x1 5.33 us: shards(): ffn_result[:2].astype(F32).transpose(0, 2, 1, 3).reshape(2, block, n * part)]
where the time goes in v2:
time: 560 us; the launch traced here: 557 us
  Pallas kernels  539 us (96%)
  local copies, waits for them, and re-layouts  12.2 us (2%)
    pallas_call x2, Pallas kernels, call(): pl.pallas_call(kernel, out_shape=[jax.ShapeDtypeStruct(*typed(entry)) for...  534 us

profile of v2, /device:TPU:12, one launch (start us, length us, event | category | flops | bytes accessed | tf_op | source)
XLA Modules:
  0.0 557.0 jit_solution(7920025052760369897)
XLA Ops:
  0.6 0.0 copy-start.3
  0.6 0.5 fusion.3.freq
  1.2 0.8 broadcast_in_dim.8
  1.9 0.7 broadcast_in_dim.9
  2.6 0.6 pad_maximum_fusion.2.gains
  3.2 1.5 copy.21.seg_col
  4.7 1.1 copy.19
  5.7 2.2 pad_maximum_fusion.1.wa
  7.9 1.5 copy.20
  9.4 0.0 copy-done.3
  9.4 1.9 pad_maximum_fusion.wf
  11.4 245.0 %shard_map.152 = (bf16[4,2048,1024]{2,1,0:T(8,128)(2,1)}, bf16[3,2048,1024]{2,1,0:T(8,128)(2,1)}, bf16[4,2,128,2048]{3,2,1,0:T(8,128)(2,1)}, bf16[4,2,128,2048]{...) custom-call(bf16[128,2048]{1,0:T(8,128)(2,1)} %residual.3, ...), custom_call_target="tpu_custom_call" | custom-call | tf_op jit(solution)/shard_map/pallas_call | solution.py:926
  256.4 289.3 %shard_map.153 = (bf16[3,4,128,1024]{3,2,1,0:T(8,128)(2,1)}, bf16[4,3,128,1024]{3,2,1,0:T(8,128)(2,1)}, bf16[128,2048]{1,0:T(8,128)(2,1)}, f32[128,2048]{1,0:T(8,128)}, f32[16,128]{1,0:T(8,128)}) custom-call(f32[128,2048]{1,0:T(8,128)} %get-tuple-element.28.mixed, bf16[128,2048]{1,0:T(8,128)(2,1)} %residual.3, f32[16,2048]{1,0:T(8,128)} %get-tuple-element.29.gains, ...), custom_call_target="tpu_custom_call" | custom-call | tf_op jit(solution)/shard_map/pallas_call | solution.py:926
  545.7 0.0 copy-start
  545.7 1.9 copy-done
  547.6 0.0 copy-start.1
  547.6 1.9 copy-done.1
  549.5 0.7 copy-done.2
  550.2 4.6 shard_map.154
  554.7 0.5 slice_bitcast_fusion
  555.3 0.0 copy-done.5
  555.3 0.8 copy.25
  556.1 0.0 copy-done.4
  556.1 1.0 copy.26
  (3 shorter events, 0.0 us)
Async XLA Ops:
  0.6 8.8 %copy-start.3 = (bf16[2,128,4096]{2,1,0:T(8,128)(2,1)S(1)}, bf16[2,128,4096]{2,1,0:T(8,128)(2,1)}, u32[]{:S(2)}) copy-start(bf16[2,128,4096]{2,1,0:T(8,128)(2,1)} %param.15) | copy-start | bytes 6291460
  545.7 1.9 copy-start
  547.6 1.9 copy-start.1
  549.5 0.7 copy-start.2
  550.2 5.1 copy-start.5
  550.2 5.9 %copy-start.4 = (f32[128,2048]{1,0:T(8,128)S(1)}, f32[128,2048]{1,0:T(8,128)}, u32[]{:S(2)}) copy-start(f32[128,2048]{1,0:T(8,128)} %get-tuple-element.59) | copy-start | bytes 3145732

commit v3 on v2

--- a/solution.py
+++ b/solution.py
@@ -147,6 +147,9 @@
 
     def cross_step(self, s):
         net = self.net
+        if s == 0:
+            self.cross(net.z)
+            return
         for sign in (1, -1):
             block = net.z - s * sign
             valid = jnp.logical_and(block >= 0, block < net.n)
@@ -380,77 +383,101 @@
 
 def attention_kernel(
     dp,
-    residual, cotangent, seg_col, seg_row, gains, freq, wa, wf,
-    wa_out, wf_out, grad_out, normed_ffn_out, normed_out, attended_out, qkv_out, mixed_out, tables_out, gains_out,
-    weights, pre, all_gains, allowed, grad_own, normed_all, ffn_own, partial, to_x, from_x,
+    residual, cotangent, seg, attn_gain, ffn_gain, freq, w_out, w_down, w_qkv, w_gate_up,
+    wa_out, wf_out, grad_out, normed_ffn_out, normed_out, attended_out, qkv_out, mixed_out, tables_out, gains_out, allowed,
+    weights, pre, gains, all_gains, live, grad_own, normed_all, ffn_own, partial, to_x, from_x, out_own, down_own,
     send_sems, local_sems, gain_sems, q_sems, o_sems, f_sems, g_sems, n_sems, x_sems,
 ):
     net = Net(dp, send_sems, local_sems)
     n = net.n
     rows, width = residual.shape
-    block, cols = wa.shape[1:]
+    block, cols = w_qkv.shape[1:]
     group = 2 * rows
-    part = wf.shape[2] // n
+    part = w_gate_up.shape[2] // n
+    depth = width // n
     me, x = net.dp_index, net.x
+    lane = lax.broadcasted_iota(jnp.int32, (group, LANES), 1)
     net.greet([((me + k) % dp, x) for k in range(1, dp)] + [(me, 1 - x)])
-
-    for k in range(1, dp):
-        net.send(gains, all_gains.at[me], gain_sems.at[me], ((me + k) % dp, x))
-    all_gains[me] = gains[...]
 
     def at_weights(first, count):
         return lambda index: weights.at[pl.ds(first, count), pl.ds(pl.multiple_of(index * block, block), block)]
 
-    qkv = Gather(net, wa.at[pl.ds(0, 3)], at_weights(0, 3), q_sems)
-    out = Gather(net, wa.at[pl.ds(3, 1)], at_weights(3, 1), o_sems)
-    ffn = Exchange(
-        net,
-        lambda to: wf.at[:, :, pl.ds(pl.multiple_of(to * part, part), part)],
-        lambda index: wf_out.at[:, pl.ds(pl.multiple_of(index * block, block), block)],
-        f_sems,
-    )
+    def ffn_part(m):
+        def own(to):
+            span = pl.ds(pl.multiple_of(to * part, part), part)
+            return down_own.at[:, span] if m == 2 else w_gate_up.at[m, :, span]
+
+        return own
+
+    def ffn_place(m):
+        return lambda index: wf_out.at[m, pl.ds(pl.multiple_of(index * block, block), block)]
+
+    qkv = Gather(net, w_qkv, at_weights(0, 3), q_sems)
+    out = Gather(net, out_own, at_weights(3, 1), o_sems)
+    ffn = [Exchange(net, ffn_part(m), ffn_place(m), f_sems.at[m]) for m in range(3)]
     grads = Rows(net, grad_own, grad_out, g_sems)
     ffn_rows = Rows(net, ffn_own, normed_ffn_out, n_sems)
-    qkv.start()
-
-    def mask_body(r):
-        span = pl.ds(r, 16)
-        live = (seg_col[x, span] >= 0).astype(F32)
-        grad_own[span] = (cotangent[span].astype(F32) * live).astype(BF16)
-
-    loop(rows, 16, mask_body)
-
-    row_seg = jnp.concatenate([seg_col[0], seg_col[1]], axis=0)
-    row_id = lax.broadcasted_iota(jnp.int32, (group, group), 0)
-    col_id = lax.broadcasted_iota(jnp.int32, (group, group), 1)
-    mask = jnp.logical_and(row_seg == seg_row[...], row_id >= col_id).astype(F32)
-    allowed[...] = mask
-    places = jnp.sum(mask, axis=1, keepdims=True) - 1.0
-    lane = lax.broadcasted_iota(jnp.int32, (group, LANES), 1)
-    angles = places * freq[...]
-    tables_out[0] = jnp.cos(angles)
-    tables_out[1] = jnp.where(lane % HD < HD // 2, -jnp.sin(angles), jnp.sin(angles))
-
-    for k in range(1, dp):
-        source = (me + k) % dp
-        net.recv(all_gains.at[source], gain_sems.at[source])
-    for i in range(dp):
-        gains_out[:, i * block : (i + 1) * block] = all_gains[i]
-
-    def norm_body(r):
-        value = residual[pl.ds(r, 16)].astype(F32)
-        unit = value * lax.rsqrt(jnp.mean(value * value, axis=-1, keepdims=True) + EPSILON)
-        to = pl.multiple_of(x * rows + r, 16)
-        normed_all[pl.ds(to, 16)] = (unit * gains_out[0:1]).astype(BF16)
-
-    loop(rows, 16, norm_body)
     own_rows = normed_all.at[pl.ds(pl.multiple_of(x * rows, rows), rows)]
     other_rows = normed_all.at[pl.ds(pl.multiple_of((1 - x) * rows, rows), rows)]
-    net.send(own_rows, own_rows, x_sems.at[0], net.device(x=1 - x))
-
-    depth = width // n
-
-    def project(b, first):
+
+    def send_gains():
+        gains[0:8] = jnp.broadcast_to(attn_gain[...].astype(F32), (8, block))
+        gains[8:16] = jnp.broadcast_to(ffn_gain[...].astype(F32), (8, block))
+        for k in range(1, dp):
+            net.send(gains, all_gains.at[me], gain_sems.at[me], ((me + k) % dp, x))
+        all_gains[me] = gains[...]
+
+    def turn_weights():
+        out_own[0] = w_out[...].T
+
+        def body(r):
+            down_own[:, pl.ds(r, 512)] = w_down[pl.ds(r, 512)].T
+
+        loop(w_down.shape[0], 512, body)
+
+    def mask_grads():
+        seg_rows = jnp.broadcast_to(seg[...].astype(F32), (LANES, group))
+        seg_cols = seg_rows.T
+        alive = (seg_cols >= 0).astype(F32)
+        live[0] = alive[:rows]
+        live[1] = alive[rows:]
+        row_id = lax.broadcasted_iota(jnp.int32, (group, group), 0)
+        col_id = lax.broadcasted_iota(jnp.int32, (group, group), 1)
+        same = jnp.concatenate([seg_cols] * (group // LANES), axis=1) == jnp.concatenate([seg_rows] * (group // LANES), axis=0)
+        mask = jnp.logical_and(same, row_id >= col_id).astype(F32)
+        allowed[...] = mask
+        angles = (jnp.sum(mask, axis=1, keepdims=True) - 1.0) * freq[...]
+        tables_out[0] = jnp.cos(angles)
+        tables_out[1] = jnp.where(lane % HD < HD // 2, -jnp.sin(angles), jnp.sin(angles))
+
+        def body(r):
+            span = pl.ds(r, 16)
+            grad_own[span] = (cotangent[span].astype(F32) * live[x, span, 0:1]).astype(BF16)
+
+        loop(rows, 16, body)
+
+    def norm():
+        for k in range(1, dp):
+            source = (me + k) % dp
+            net.recv(all_gains.at[source], gain_sems.at[source])
+        for i in range(dp):
+            gains_out[:, i * block : (i + 1) * block] = all_gains[i]
+
+        def body(r):
+            value = residual[pl.ds(r, 16)].astype(F32)
+            unit = value * lax.rsqrt(jnp.mean(value * value, axis=-1, keepdims=True) + EPSILON)
+            to = pl.multiple_of(x * rows + r, 16)
+            normed_all[pl.ds(to, 16)] = (unit * gains_out[0:1]).astype(BF16)
+
+        loop(rows, 16, body)
+        net.send(own_rows, own_rows, x_sems.at[0], net.device(x=1 - x))
+
+    def project(k):
+        if k == 0:
+            net.recv(other_rows, x_sems.at[0])
+            net.settle(qkv.kept)
+            net.local(normed_all, normed_out)
+        b = (net.z + k) % n
         qkv.finish(b)
         base = pl.multiple_of(b * depth, depth)
 
@@ -458,82 +485,118 @@
             for m in range(3):
                 term = dot(normed_all[:, pl.ds(base, depth)], weights[m, pl.ds(base, depth), pl.ds(col, 256)])
                 to = pl.ds(pl.multiple_of(m * cols + col, 256), 256)
-                pre[:, to] = term if first else pre[:, to] + term
+                pre[:, to] = term if k == 0 else pre[:, to] + term
 
         loop(cols, 256, body)
 
+    def heads():
+        masks = head_masks()
+
+        def body(col):
+            cosine, sine = tables_out[0], tables_out[1]
+            queries = turn(pre[:, pl.ds(col, LANES)], cosine, sine, lane).astype(BF16)
+            key_rows = turn(pre[:, pl.ds(pl.multiple_of(cols + col, LANES), LANES)], cosine, sine, lane).astype(BF16)
+            value_rows = pre[:, pl.ds(pl.multiple_of(2 * cols + col, LANES), LANES)].astype(BF16)
+            qkv_out[0, :, pl.ds(col, LANES)] = queries
+            qkv_out[1, :, pl.ds(col, LANES)] = key_rows
+            qkv_out[2, :, pl.ds(col, LANES)] = value_rows
+            may = jnp.concatenate([allowed[...], allowed[...]], axis=0)
+            probs = softmax(both(queries, masks), key_rows, may).astype(BF16)
+            attended_out[:, pl.ds(col, LANES)] = pick(dot(probs, value_rows), group).astype(BF16)
+
+        loop(cols, LANES, body)
+
+    def join():
+        for k in range(n):
+            out.finish((net.z + k) % n)
+        net.settle(out.kept)
+        net.local(weights, wa_out)
+
+        def body(col):
+            term = dot(attended_out[...], weights[3, pl.ds(col, 256), :], NT)
+            partial[0, :, pl.ds(col, 256)] = term[:rows]
+            partial[1, :, pl.ds(col, 256)] = term[rows:]
+
+        loop(width, 256, body)
+
+        def to_body(r):
+            to_x[pl.ds(r, 16)] = partial[1 - x, pl.ds(r, 16)].astype(BF16)
+
+        loop(rows, 16, to_body)
+        net.send(to_x, from_x, x_sems.at[1], net.device(x=1 - x))
+
+    def mix():
+        net.recv(from_x, x_sems.at[1])
+
+        def body(r):
+            span = pl.ds(r, 16)
+            value = residual[span].astype(F32) + partial[x, span] + from_x[span].astype(F32)
+            mixed_out[span] = value
+            unit = value * lax.rsqrt(jnp.mean(value * value, axis=-1, keepdims=True) + EPSILON)
+            ffn_own[span] = (unit * gains_out[8:9]).astype(BF16)
+
+        loop(rows, 16, body)
+
+    def ffn_step(m, k):
+        ffn[m].step((net.z + k) % n)
+
+    def ffn_cross(m):
+        for k in range(n):
+            ffn[m].cross((net.z + k) % n)
+
+    qkv.start()
+    turn_weights()
+    out.start()
     qkv.step(1)
-    qkv.cross(net.z)
+    mask_grads()
+    send_gains()
+    out.step(1)
+    qkv.step(2)
+    qkv.cross_step(0)
+    norm()
+    qkv.cross_step(1)
+    ffn[2].start()
+    out.step(2)
     grads.start()
-    for s in range(2, n):
-        qkv.step(s)
-        if s == 2:
-            out.start()
-            ffn.start()
-        qkv.cross_step(s - 1)
-    qkv.cross_step(n - 1)
-    net.recv(other_rows, x_sems.at[0])
-    net.settle(qkv.kept)
-    for k in range(n):
-        project((net.z + k) % n, k == 0)
-    out.cross(net.z)
-    for s in range(1, n):
-        out.step(s)
-        out.cross_step(s)
-    masks = head_masks()
-
-    def head_body(col):
-        cosine, sine = tables_out[0], tables_out[1]
-        queries = turn(pre[:, pl.ds(col, LANES)], cosine, sine, lane).astype(BF16)
-        key_rows = turn(pre[:, pl.ds(pl.multiple_of(cols + col, LANES), LANES)], cosine, sine, lane).astype(BF16)
-        value_rows = pre[:, pl.ds(pl.multiple_of(2 * cols + col, LANES), LANES)].astype(BF16)
-        qkv_out[0, :, pl.ds(col, LANES)] = queries
-        qkv_out[1, :, pl.ds(col, LANES)] = key_rows
-        qkv_out[2, :, pl.ds(col, LANES)] = value_rows
-        may = jnp.concatenate([allowed[...], allowed[...]], axis=0)
-        probs = softmax(both(queries, masks), key_rows, may).astype(BF16)
-        attended_out[:, pl.ds(col, LANES)] = pick(dot(probs, value_rows), group).astype(BF16)
-
-    loop(cols, LANES, head_body)
-    for k in range(1, n):
-        ffn.step((net.z + k) % n)
-    for k in range(n):
-        out.finish((net.z + k) % n)
-    net.settle(out.kept)
-    kept_weights = net.local(weights, wa_out)
-
-    def out_body(col):
-        term = dot(attended_out[...], weights[3, pl.ds(col, 256), :], NT)
-        partial[0, :, pl.ds(col, 256)] = term[:rows]
-        partial[1, :, pl.ds(col, 256)] = term[rows:]
-
-    loop(width, 256, out_body)
-
-    def to_body(r):
-        to_x[pl.ds(r, 16)] = partial[1 - x, pl.ds(r, 16)].astype(BF16)
-
-    loop(rows, 16, to_body)
-    net.send(to_x, from_x, x_sems.at[1], net.device(x=1 - x))
-    for s in range(1, n):
-        grads.step(s)
-    net.recv(from_x, x_sems.at[1])
-
-    def mix_body(r):
-        span = pl.ds(r, 16)
-        value = residual[span].astype(F32) + partial[x, span] + from_x[span].astype(F32)
-        mixed_out[span] = value
-        unit = value * lax.rsqrt(jnp.mean(value * value, axis=-1, keepdims=True) + EPSILON)
-        ffn_own[span] = (unit * gains_out[8:9]).astype(BF16)
-
-    loop(rows, 16, mix_body)
+    qkv.step(3)
+    out.cross_step(0)
+    qkv.cross_step(2)
+    ffn[0].start()
+    qkv.cross_step(3)
+    project(0)
+    project(1)
+    out.cross_step(1)
+    project(2)
+    project(3)
+    out.cross_step(2)
+    grads.step(1)
+    out.step(3)
+    out.cross_step(3)
+    ffn_step(2, 3)
+    heads()
+    ffn[1].start()
+    join()
+    grads.step(2)
+    ffn_step(0, 2)
+    ffn_step(0, 3)
+    mix()
     ffn_rows.start()
-    net.local(normed_all, normed_out)
-    for s in range(1, n):
-        ffn_rows.step(s)
-    for k in range(n):
-        ffn.cross((net.z + k) % n)
-    for k in range(n):
-        ffn.finish((net.z + k) % n)
+    ffn_step(1, 1)
+    ffn_step(2, 2)
+    ffn_step(1, 2)
+    ffn_step(0, 1)
+    grads.step(3)
+    ffn_rows.step(1)
+    ffn_cross(0)
+    ffn_step(1, 3)
+    ffn_cross(1)
+    ffn_rows.step(2)
+    ffn_rows.step(3)
+    ffn_step(2, 1)
+    ffn_cross(2)
+    for m in range(3):
+        for k in range(n):
+            ffn[m].finish((net.z + k) % n)
     grads.finish()
     ffn_rows.finish()
     net.drain()
@@ -609,10 +672,10 @@
 
 def ffn_kernel(
     dp,
-    mixed, residual, gains, seg_col, seg_row, tables, normed_ffn_hbm, grad_hbm, wf, normed_hbm, attended_hbm, qkv_hbm, wa,
+    mixed, residual, gains, allowed, tables, normed_ffn_hbm, grad_hbm, wf, normed_hbm, attended_hbm, qkv_hbm, wa,
     result, totals, block_out, input_grad, gain_out,
     weights, grad, hidden, gate_up_grad, back, back_x, back_z, part, from_c, from_y,
-    mixed_all, allowed, from_x, gain_sum, ffn_sum, gain_to, gain_from, gain_x,
+    mixed_all, from_x, gain_sum, ffn_sum, gain_to, gain_from, gain_x,
     send_sems, local_sems, bx_sems, bz_sems, rc_sems, ry_sems, rz_sems, rl_sems, x_sems, gain_sems, free,
 ):
     net = Net(dp, send_sems, local_sems)
@@ -650,10 +713,13 @@
     for load in loads:
         net.settle(load)
 
-    def chunk(b):
-        here = pl.ds(pl.multiple_of(b * pair, pair), pair)
-
-        def hidden_body(col):
+    def rows_of(b):
+        return pl.ds(pl.multiple_of(b * pair, pair), pair)
+
+    def forward(k):
+        here = rows_of(order[k])
+
+        def body(col):
             span = pl.ds(col, 256)
 
             def project(m):
@@ -669,20 +735,24 @@
             gate_grad[here, span] = (hidden_grad * up * sigmoid * (1.0 + gate * (1.0 - sigmoid))).astype(BF16)
             up_grad[here, span] = (hidden_grad * active).astype(BF16)
 
-        loop(cols, 256, hidden_body)
-
-        def back_body(col):
+        loop(cols, 256, body)
+
+    def backward(k):
+        b = order[k]
+        here = rows_of(b)
+
+        def body(col):
             span = pl.ds(col, 256)
             term = dot(gate_grad[here], weights[0, span, :], NT) + dot(up_grad[here], weights[1, span, :], NT)
             term = term.astype(BF16)
             back[b, 0, :, span] = term[:rows]
             back[b, 1, :, span] = term[rows:]
 
-        loop(width, 256, back_body)
+        loop(width, 256, body)
         backs.start(b)
 
-    def add_chunk(b):
-        here = pl.ds(pl.multiple_of(b * pair, pair), pair)
+    def add_chunk(k):
+        here = rows_of(order[k])
 
         def body(col):
             span = pl.ds(col, 256)
@@ -690,65 +760,26 @@
 
         loop(width, 256, body)
 
-    def ffn_items(b):
+    ffn_items = [(2, k) for k in range(n)] + [(m, k) for k in range(n) for m in (0, 1)]
+    attention_items = [(3, k) for k in range(n)] + [(m, k) for k in range(n) for m in range(3)]
+
+    def ffn_item():
+        m, k = ffn_items[len(red.items)]
+        b = order[k]
         base = b * depth
-        col = pl.ds(pl.multiple_of(base % cols, depth), depth)
-        row = pl.ds(pl.multiple_of(base // cols * every, every), every)
-        own = pl.ds(pl.multiple_of(base, depth), depth)
-        for m in (2, 0, 1):
-            left = grad[:, own] if m == 2 else weights[3, row, col]
-            red.item(m, b, left, (gate_grad, up_grad, hidden)[m], depth, block)
-            if len(red.items) > 1:
-                red.step_c()
-
-    for k in range(n):
-        chunk(order[k])
-        if k > 0:
-            backs.step_x()
-        if k > 1:
-            backs.step_z()
-    ffn_items(order[0])
-    backs.step_x()
-    backs.step_z()
-    ffn_items(order[1])
-    backs.step_z()
-    red.step_y()
-    for k in range(2, n):
-        ffn_items(order[k])
-        red.step_y()
-    red.step_c()
-    load_out = net.local(wa.at[3], weights.at[3])
-    backs.finish()
-    ffn_sum[...] = jnp.zeros_like(ffn_sum)
-
-    def mixed_body(r):
-        span = pl.ds(r, 16)
-        own = pl.ds(pl.multiple_of((net.z * 2 + x) * rows + r, 16), 16)
-        term, gain_term = norm_back(back[net.z, x, span].astype(F32), mixed[span], gains[8:9])
-        value = grad[own].astype(F32) + term
-        input_grad[span] = value
-        mixed_all[pl.ds(pl.multiple_of(x * rows + r, 16), 16)] = value.astype(BF16)
-        ffn_sum[...] += gain_term[:8] + gain_term[8:]
-
-    loop(rows, 16, mixed_body)
-    own_rows = mixed_all.at[pl.ds(pl.multiple_of(x * rows, rows), rows)]
-    other_rows = mixed_all.at[pl.ds(pl.multiple_of((1 - x) * rows, rows), rows)]
-    net.send(own_rows, own_rows, x_sems.at[0], net.device(x=1 - x))
-    pl.semaphore_signal(free.at[2], inc=1, device_id=net.device(x=1 - x), device_id_type=MESH)
-    for cond, z in ((net.z > 0, net.z - 1), (net.z < n - 1, net.z + 1)):
-
-        @pl.when(cond)
-        def _():
-            pl.semaphore_signal(free.at[3], inc=1, device_id=net.device(z=z), device_id_type=MESH)
-
-    for k in range(n):
-        add_chunk(order[k])
-        red.step_y()
-    pl.semaphore_wait(free.at[2], 1)
-    load_qkv = net.local(wa.at[pl.ds(0, 3)], weights.at[pl.ds(0, 3)])
-    load_parts = [net.local(qkv_hbm.at[m], hidden.at[pl.ds(m * pair, pair)]) for m in range(3)]
-    load_attended = net.local(attended_hbm, hidden.at[pl.ds(3 * pair, pair)])
-    load_normed = net.local(normed_hbm, grad.at[pl.ds(0, pair)])
+        if m == 2:
+            left = grad[:, pl.ds(pl.multiple_of(base, depth), depth)]
+        else:
+            row = pl.ds(pl.multiple_of(base // cols * every, every), every)
+            left = weights[3, row, pl.ds(pl.multiple_of(base % cols, depth), depth)]
+        red.item(m, b, left, (gate_grad, up_grad, hidden)[m], depth, block)
+
+    def attention_item():
+        m, k = attention_items[len(red.items) - len(ffn_items)]
+        base = pl.ds(pl.multiple_of(order[k] * depth, depth), depth)
+        left, right = (mixed_all, attended) if m == 3 else (normed, grads_of[m])
+        red.item(3 + m, order[k], left[:, base], right, depth, block)
+
     queries_of, keys_of, values_of = [hidden.at[pl.ds(m * pair, pair)] for m in range(3)]
     attended = hidden.at[pl.ds(3 * pair, pair)]
     normed = grad.at[pl.ds(0, pair)]
@@ -758,139 +789,279 @@
         grad.at[pl.ds(3 * pair, pair), pl.ds(0, cols)],
     ]
     attended_grad = grad.at[pl.ds(3 * pair, pair), pl.ds(cols, cols)]
-
-    row_seg = jnp.concatenate([seg_col[0], seg_col[1]], axis=0)
-    row_id = lax.broadcasted_iota(jnp.int32, (pair, pair), 0)
-    col_id = lax.broadcasted_iota(jnp.int32, (pair, pair), 1)
-    allowed[...] = jnp.logical_and(row_seg == seg_row[...], row_id >= col_id).astype(F32)
-    net.settle(load_out)
-    net.recv(other_rows, x_sems.at[0])
-    for k in range(n):
-        adds.start(order[k])
-
-    def attended_body(col):
-        span = pl.ds(col, 256)
-        attended_grad[:, span] = dot(mixed_all[...], weights[3, :, span]).astype(BF16)
-
-    loop(cols, 256, attended_body)
-    for cond, z in ((net.z > 0, net.z - 1), (net.z < n - 1, net.z + 1)):
-
-        @pl.when(cond)
-        def _():
-            pl.semaphore_signal(free.at[4], inc=1, device_id=net.device(z=z), device_id_type=MESH)
-
-    net.settle(load_attended)
-
-    def attention_items(m, left, right):
+    own_rows = mixed_all.at[pl.ds(pl.multiple_of(x * rows, rows), rows)]
+    other_rows = mixed_all.at[pl.ds(pl.multiple_of((1 - x) * rows, rows), rows)]
+    late = {}
+
+    def tell_beside(which):
+        for cond, z in ((net.z > 0, net.z - 1), (net.z < n - 1, net.z + 1)):
+
+            @pl.when(cond)
+            def _():
+                pl.semaphore_signal(free.at[which], inc=1, device_id=net.device(z=z), device_id_type=MESH)
+
+    def mix_grads():
+        backs.finish()
+        ffn_sum[...] = jnp.zeros_like(ffn_sum)
+
+        def body(r):
+            span = pl.ds(r, 16)
+            own = pl.ds(pl.multiple_of((net.z * 2 + x) * rows + r, 16), 16)
+            term, gain_term = norm_back(back[net.z, x, span].astype(F32), mixed[span], gains[8:9])
+            value = grad[own].astype(F32) + term
+            input_grad[span] = value
+            mixed_all[pl.ds(pl.multiple_of(x * rows + r, 16), 16)] = value.astype(BF16)
+            ffn_sum[...] += gain_term[:8] + gain_term[8:]
+
+        loop(rows, 16, body)
+        net.send(own_rows, own_rows, x_sems.at[0], net.device(x=1 - x))
+        pl.semaphore_signal(free.at[2], inc=1, device_id=net.device(x=1 - x), device_id_type=MESH)
+        tell_beside(3)
+
+    def load_out():
+        late["out"] = net.local(wa.at[3], weights.at[3])
+
+    def load_rest():
+        late["normed"] = net.local(normed_hbm, normed)
+        late["qkv"] = net.local(wa.at[pl.ds(0, 3)], weights.at[pl.ds(0, 3)])
+        late["parts"] = [net.local(qkv_hbm.at[m], hidden.at[pl.ds(m * pair, pair)]) for m in range(3)]
+        late["attended"] = net.local(attended_hbm, attended)
+
+    def start_adds():
+        pl.semaphore_wait(free.at[2], 1)
         for k in range(n):
-            base = pl.ds(pl.multiple_of(order[k] * depth, depth), depth)
-            red.item(3 + m, order[k], left[:, base], right, depth, block)
-            if red.done_c < len(red.items) - 1:
-                red.step_c()
-
-    attention_items(3, mixed_all, attended)
-    red.step_c()
-    for load in load_parts:
-        net.settle(load)
-    masks = head_masks()
-    lane = lax.broadcasted_iota(jnp.int32, (pair, LANES), 1)
-
-    def head_body(col):
-        span = pl.ds(col, LANES)
-        cosine, sine = tables[0], tables[1]
-        queries, key_rows, value_rows = queries_of[:, span], keys_of[:, span], values_of[:, span]
-        out_grad = attended_grad[:, span]
-        queries2, out_grad2 = both(queries, masks), both(out_grad, masks)
-        may = jnp.concatenate([allowed[...], allowed[...]], axis=0)
-        probs = softmax(queries2, key_rows, may)
-        value_grad = dot(probs.astype(BF16), out_grad2, TN)
-        prob_grad = dot(out_grad2, value_rows, NT)
-        score_grad = probs * (prob_grad - jnp.sum(probs * prob_grad, axis=-1, keepdims=True))
-        score_grad = score_grad.astype(BF16)
-        query_grad = pick(dot(score_grad, key_rows), pair) * HD ** (-0.5)
-        key_grad = dot(score_grad, queries2, TN) * HD ** (-0.5)
-        grads_of[0][:, span] = turn(query_grad, cosine, -sine, lane).astype(BF16)
-        grads_of[1][:, span] = turn(key_grad, cosine, -sine, lane).astype(BF16)
-        grads_of[2][:, span] = value_grad.astype(BF16)
-
-    loop(cols, LANES, head_body)
-    net.settle(load_qkv)
-    net.settle(load_normed)
-    while red.done_y < 3 * n:
-        red.step_y()
-    attention_items(0, normed, grads_of[0])
+            adds.start(order[k])
+
+    def attended_back():
+        net.settle(late["out"])
+        net.recv(other_rows, x_sems.at[0])
+
+        def body(col):
+            span = pl.ds(col, 256)
+            attended_grad[:, span] = dot(mixed_all[...], weights[3, :, span]).astype(BF16)
+
+        loop(cols, 256, body)
+        tell_beside(4)
+        net.settle(late["attended"])
+
+    def heads():
+        for load in late["parts"]:
+            net.settle(load)
+        masks = head_masks()
+        lane = lax.broadcasted_iota(jnp.int32, (pair, LANES), 1)
+
+        def body(col):
+            span = pl.ds(col, LANES)
+            cosine, sine = tables[0], tables[1]
+            queries, key_rows, value_rows = queries_of[:, span], keys_of[:, span], values_of[:, span]
+            out_grad = attended_grad[:, span]
+            queries2, out_grad2 = both(queries, masks), both(out_grad, masks)
+            may = jnp.concatenate([allowed[...], allowed[...]], axis=0)
+            probs = softmax(queries2, key_rows, may)
+            value_grad = dot(probs.astype(BF16), out_grad2, TN)
+            prob_grad = dot(out_grad2, value_rows, NT)
+            score_grad = probs * (prob_grad - jnp.sum(probs * prob_grad, axis=-1, keepdims=True))
+            score_grad = score_grad.astype(BF16)
+            query_grad = pick(dot(score_grad, key_rows), pair) * HD ** (-0.5)
+            key_grad = dot(score_grad, queries2, TN) * HD ** (-0.5)
+            grads_of[0][:, span] = turn(query_grad, cosine, -sine, lane).astype(BF16)
+            grads_of[1][:, span] = turn(key_grad, cosine, -sine, lane).astype(BF16)
+            grads_of[2][:, span] = value_grad.astype(BF16)
+
+        loop(cols, LANES, body)
+        net.settle(late["normed"])
+
+    def normed_back():
+        net.settle(late["qkv"])
+        for entry in backs.sent:
+            net.settle(entry)
+
+        def body(col):
+            span = pl.ds(col, 256)
+            term = dot(grads_of[0][...], weights[0, span, :], NT)
+            term += dot(grads_of[1][...], weights[1, span, :], NT)
+            term += dot(grads_of[2][...], weights[2, span, :], NT)
+            back[0, 0, :, span] = term[:rows].astype(BF16)
+            back[0, 1, :, span] = term[rows:].astype(BF16)
+
+        loop(width, 256, body)
+        net.send(back.at[0, 1 - x], from_x, x_sems.at[1], net.device(x=1 - x))
+
+    def input_back():
+        net.recv(from_x, x_sems.at[1])
+        gain_sum[...] = jnp.zeros_like(gain_sum)
+
+        def body(r):
+            span = pl.ds(r, 16)
+            grad_rows = back[0, x, span].astype(F32) + from_x[span].astype(F32)
+            term, gain_term = norm_back(grad_rows, residual[span].astype(F32), gains[0:1])
+            input_grad[span] += term
+            gain_sum[...] += gain_term[:8] + gain_term[8:]
+
+        loop(rows, 16, body)
+        for i in range(dp):
+            gain_to[i, 0:8] = gain_sum[:, i * block : (i + 1) * block]
+            gain_to[i, 8:16] = ffn_sum[:, i * block : (i + 1) * block]
+        for k in range(1, dp):
+            to = (me + k) % dp
+            net.send(gain_to.at[to], gain_from.at[me], gain_sems.at[me], (to, x))
+
+    def sum_gains():
+        total = gain_to[me]
+        for k in range(1, dp):
+            source = (me + k) % dp
+            net.recv(gain_from.at[source], gain_sems.at[source])
+            total = total + gain_from[source]
+        gain_x[0] = total
+        net.send(gain_x.at[0], gain_x.at[1], x_sems.at[2], net.device(x=1 - x))
+
+    def block_rows():
+        adds.finish()
+
+        def body(r):
+            span = pl.ds(r, 16)
+            block_out[span] = (mixed[span] + adds.part(net.z, x)[span].astype(F32)).astype(BF16)
+
+        loop(rows, 16, body)
+
+    forward(0)
+    backward(0)
+    forward(1)
+    backward(1)
+    forward(2)
+    forward(3)
+    backs.step_x()
+    backs.step_z()
+    ffn_item()
+    backward(2)
+    red.step_c()
+    ffn_item()
+    backs.step_x()
+    ffn_item()
+    backs.step_z()
+    red.step_c()
+    ffn_item()
+    red.step_y()
+    ffn_item()
+    backs.step_x()
+    red.step_c()
+    red.step_c()
+    backs.step_z()
+    backward(3)
+    ffn_item()
+    ffn_item()
+    red.step_c()
+    red.step_c()
+    ffn_item()
+    ffn_item()
+    red.step_c()
+    ffn_item()
+    backs.step_x()
+    red.step_y()
+    red.step_c()
+    red.step_y()
+    red.step_y()
+    red.step_c()
+    ffn_item()
+    backs.step_z()
+    ffn_item()
+    add_chunk(0)
+    red.step_y()
+    red.step_c()
+    load_out()
+    red.step_y()
+    red.step_c()
+    red.step_y()
+    mix_grads()
+    add_chunk(1)
+    add_chunk(2)
+    red.step_y()
+    add_chunk(3)
+    red.step_c()
+    start_adds()
+    load_rest()
+    attended_back()
+    red.step_y()
+    red.step_y()
+    pl.semaphore_wait(free.at[3], beside)
+    attention_item()
+    attention_item()
+    red.step_c()
+    attention_item()
+    red.step_c()
+    red.step_y()
+    attention_item()
+    heads()
+    adds.step_x()
+    adds.step_z()
+    red.step_y()
     pl.semaphore_wait(free.at[4], beside)
-
-    red.step_y()
-    red.step_y()
+    red.step_c()
+    adds.step_x()
+    attention_item()
+    red.step_y()
+    red.step_c()
+    red.step_y()
+    attention_item()
+    red.step_c()
+    attention_item()
     red.step_z()
-    attention_items(1, normed, grads_of[1])
+    adds.step_z()
     red.step_y()
     red.step_z()
+    red.step_y()
+    red.step_c()
+    attention_item()
+    red.step_c()
+    attention_item()
+    adds.step_x()
+    normed_back()
+    attention_item()
+    red.step_z()
+    red.step_c()
+    adds.step_z()
+    attention_item()
+    red.step_c()
+    red.step_y()
+    attention_item()
+    red.step_z()
+    red.step_y()
+    red.step_c()
+    attention_item()
+    attention_item()
+    red.step_z()
+    red.step_y()
+    adds.step_x()
+    red.step_y()
+    red.step_z()
+    red.step_c()
+    adds.step_z()
+    red.step_c()
+    red.step_c()
+    attention_item()
+    input_back()
+    red.step_y()
     red.step_y()
     red.step_z()
     red.step_z()
-    attention_items(2, normed, grads_of[2])
-    red.step_c()
-    for entry in backs.sent:
-        net.settle(entry)
-
-    def normed_body(col):
-        span = pl.ds(col, 256)
-        term = dot(grads_of[0][...], weights[0, span, :], NT)
-        term += dot(grads_of[1][...], weights[1, span, :], NT)
-        term += dot(grads_of[2][...], weights[2, span, :], NT)
-        back[0, 0, :, span] = term[:rows].astype(BF16)
-        back[0, 1, :, span] = term[rows:].astype(BF16)
-
-    loop(width, 256, normed_body)
-    net.send(back.at[0, 1 - x], from_x, x_sems.at[1], net.device(x=1 - x))
-    net.recv(from_x, x_sems.at[1])
-    gain_sum[...] = jnp.zeros_like(gain_sum)
-
-    def input_body(r):
-        span = pl.ds(r, 16)
-        grad_rows = back[0, x, span].astype(F32) + from_x[span].astype(F32)
-        term, gain_term = norm_back(grad_rows, residual[span].astype(F32), gains[0:1])
-        input_grad[span] += term
-        gain_sum[...] += gain_term[:8] + gain_term[8:]
-
-    loop(rows, 16, input_body)
-    for i in range(dp):
-        gain_to[i, 0:8] = gain_sum[:, i * block : (i + 1) * block]
-        gain_to[i, 8:16] = ffn_sum[:, i * block : (i + 1) * block]
-    for k in range(1, dp):
-        to = (me + k) % dp
-        net.send(gain_to.at[to], gain_from.at[me], gain_sems.at[me], (to, x))
-    pl.semaphore_wait(free.at[3], beside)
-
-    for k in range(n):
-        adds.step_x()
+    red.step_c()
+    red.step_y()
+    attention_item()
+    red.step_c()
+    red.step_c()
+    red.step_y()
+    for _ in range(3):
+        red.step_z()
+    red.step_y()
+    sum_gains()
+    red.step_z()
+    red.step_z()
+    for _ in range(3):
         red.step_y()
-        if red.done_z < red.done_y - 1:
-            red.step_z()
-    for k in range(n):
-        red.step_y()
-        adds.step_z()
+    block_rows()
+    for _ in range(3):
         red.step_z()
-    adds.finish()
-
-    def block_body(r):
-        span = pl.ds(r, 16)
-        block_out[span] = (mixed[span] + adds.part(net.z, x)[span].astype(F32)).astype(BF16)
-
-    loop(rows, 16, block_body)
-    total = gain_to[me]
-    for k in range(1, dp):
-        source = (me + k) % dp
-        net.recv(gain_from.at[source], gain_sems.at[source])
-        total = total + gain_from[source]
-    gain_x[0] = total
-    net.send(gain_x.at[0], gain_x.at[1], x_sems.at[2], net.device(x=1 - x))
-    while red.done_y < len(red.items):
-        red.step_y()
-        red.step_z()
-    red.step_z()
+    assert red.done_y == red.done_z == red.total and adds.done_z == n
     net.recv(gain_x.at[1], x_sems.at[2])
     gain_out[...] = gain_x[0] + gain_x[1]
     red.finish()
@@ -939,32 +1110,27 @@
     group = seg_ids.shape[0]
     block, cols = w_qkv.shape[1:]
     part = w_gate_up.shape[2] // n
-    wa = jnp.concatenate([w_qkv, w_out.T[None]], axis=0)
-    wf = jnp.concatenate([w_gate_up, w_down.T[None]], axis=0)
-    seg_col = seg_ids.reshape(2, rows, 1)
-    seg_row = seg_ids.reshape(1, group)
-    gains = jnp.concatenate(
-        [jnp.broadcast_to(gain.astype(F32)[None], (8, block)) for gain in (attn_gain, ffn_gain)], axis=0
-    )
     pairs = jnp.arange(LANES, dtype=jnp.int32) % (HD // 2)
     freq = (ROPE_BASE ** (-(pairs.astype(F32) * 2.0 / HD)))[None]
     mib = 1024 * 1024
 
     first = call(
-        functools.partial(attention_kernel, dp), 1, 192, 8, 60 * mib,
+        functools.partial(attention_kernel, dp), 1, 192, 12, 60 * mib,
         [
             (4, width, cols), (3, width, part), (n, 2, rows, width), (n, 2, rows, width), (group, width),
-            (group, cols), (3, group, cols), (rows, width, F32), (2, group, LANES, F32), (16, width, F32),
+            (group, cols), (3, group, cols), (rows, width, F32), (2, group, LANES, F32), (16, width, F32), (group, group, F32),
         ],
-        [ANY] * 5 + [VM] * 5,
+        [ANY] * 5 + [VM] * 6,
         [
-            (4, width, cols), (group, 3 * cols, F32), (dp, 16, block, F32), (group, group, F32),
+            (4, width, cols), (group, 3 * cols, F32), (16, block, F32), (dp, 16, block, F32), (2, rows, LANES, F32),
             (rows, width), (group, width), (rows, width), (2, rows, width, F32), (rows, width), (rows, width),
+            (1, block, cols), (block, n * part),
         ],
-        [(dp,), (4, n), (4, n), (4, n), (2, n), (2, n), (2,)],
-    )
-    (weights, ffn_weights, grad_all, normed_ffn, normed, attended, qkv, mixed, tables, all_gains) = first(
-        [VM] * 6 + [ANY] * 2, residual, cotangent, seg_col, seg_row, gains, freq, wa, wf
+        [(dp,), (4, n), (4, n), (3, 4, n), (2, n), (2, n), (2,)],
+    )
+    (weights, ffn_weights, grad_all, normed_ffn, normed, attended, qkv, mixed, tables, all_gains, allowed) = first(
+        [VM] * 8 + [ANY] * 2, residual, cotangent, seg_ids[None], attn_gain[None], ffn_gain[None], freq, w_out, w_down,
+        w_qkv, w_gate_up,
     )
     every = n * 2 * rows
     slots = 3 * n
@@ -976,14 +1142,14 @@
             (4, width, part), (every, width), (every, part), (every, 2 * part),
             (n, 2, rows, width), (n, rows, width), (n + 1, rows, width),
             (slots, 2, 2, block, part), (slots, 2, block, part), (slots, block, part),
-            (group, width), (group, group, F32), (rows, width), (8, width, F32), (8, width, F32),
+            (group, width), (rows, width), (8, width, F32), (8, width, F32),
             (dp, 16, block, F32), (dp, 16, block, F32), (2, 16, block, F32),
         ],
         [(n,), (n + 1,), (slots,), (slots,), (3, n), (4, n + 2), (3,), (dp,)],
         5,
     )
     result, totals, block_out, input_grad, gain_grads = second(
-        [VM] * 6 + [ANY] * 7, mixed, residual, all_gains, seg_col, seg_row, tables, normed_ffn.reshape(every, width),
+        [VM] * 5 + [ANY] * 7, mixed, residual, all_gains, allowed, tables, normed_ffn.reshape(every, width),
         grad_all.reshape(every, width), ffn_weights, normed, attended, qkv, weights,
     )
     qkv_grad, out_grad, gate_up_grad, down_grad, gain_sums = pl.pallas_call(

time: 560 us -> 472 us (0.84)
  Pallas kernels: 539 us -> 458 us
    pallas_call x2, Pallas kernels: 534 us -> 453 us  [call(): pl.pallas_call(kernel, out_shape=[jax.ShapeDtypeStruct(*typed(entry)) for...]
where the time goes in v3:
time: 472 us; the launch traced here: 466 us
  Pallas kernels  458 us (97%)
  local copies, waits for them, and re-layouts  6.76 us (1%)
    pallas_call x2, Pallas kernels, call(): pl.pallas_call(kernel, out_shape=[jax.ShapeDtypeStruct(*typed(entry)) for...  453 us

profile of v3, /device:TPU:12, one launch (start us, length us, event | category | flops | bytes accessed | tf_op | source)
XLA Modules:
  0.0 465.6 jit_solution(1122535144739521889)
XLA Ops:
  0.6 0.5 fusion.3.freq
  1.2 201.0 %shard_map.152 = (bf16[4,2048,1024]{2,1,0:T(8,128)(2,1)}, bf16[3,2048,1024]{2,1,0:T(8,128)(2,1)}, bf16[4,2,128,2048]{3,2,1,0:T(8,128)(2,1)}, bf16[4,2,128,2048]{...) custom-call(bf16[128,2048]{1,0:T(8,128)(2,1)} %residual.3, ...), custom_call_target="tpu_custom_call" | custom-call | tf_op jit(solution)/shard_map/pallas_call | solution.py:1097
  202.2 252.1 %shard_map.153 = (bf16[3,4,128,1024]{3,2,1,0:T(8,128)(2,1)}, bf16[4,3,128,1024]{3,2,1,0:T(8,128)(2,1)}, bf16[128,2048]{1,0:T(8,128)(2,1)}, f32[128,2048]{1,0:T(8,128)}, f32[16,128]{1,0:T(8,128)}) custom-call(f32[128,2048]{1,0:T(8,128)} %get-tuple-element.29.mixed, bf16[128,2048]{1,0:T(8,128)(2,1)} %residual.3, f32[16,2048]{1,0:T(8,128)} %get-tuple-element.30.gains, ...), custom_call_target="tpu_custom_call" | custom-call | tf_op jit(solution)/shard_map/pallas_call | solution.py:1097
  454.3 0.0 copy-start
  454.3 1.9 copy-done
  456.2 0.0 copy-start.1
  456.2 1.9 copy-done.1
  458.1 0.0 copy-start.2
  458.1 0.7 copy-done.2
  458.8 0.0 copy-start.4
  458.8 0.0 copy-start.3
  458.8 4.6 shard_map.154
  463.3 0.5 slice_bitcast_fusion
  463.8 0.0 copy-done.4
  463.8 0.8 copy.19
  464.6 0.0 copy-done.3
  464.6 1.0 copy.20
Async XLA Ops:
  454.3 1.9 copy-start
  456.2 1.9 copy-start.1
  458.1 0.7 copy-start.2
  458.8 5.1 %copy-start.4 = (bf16[128,2048]{1,0:T(8,128)(2,1)S(1)}, bf16[128,2048]{1,0:T(8,128)(2,1)}, u32[]{:S(2)}) copy-start(bf16[128,2048]{1,0:T(8,128)(2,1)} %get-tuple-element.60) | copy-start | bytes 1572868
  458.8 5.9 %copy-start.3 = (f32[128,2048]{1,0:T(8,128)S(1)}, f32[128,2048]{1,0:T(8,128)}, u32[]{:S(2)}) copy-start(f32[128,2048]{1,0:T(8,128)} %get-tuple-element.61) | copy-start | bytes 3145732

commit v4 on v3

--- a/solution.py
+++ b/solution.py
@@ -16,6 +16,8 @@
 F32 = jnp.float32
 BF16 = jnp.bfloat16
 LANES = 128
+SLOTS = 9
+LIMIT = 66977792
 NT = (((1,), (1,)), ((), ()))
 TN = (((0,), (0,)), ((), ()))
 NN = (((1,), (0,)), ((), ()))
@@ -46,6 +48,7 @@
         self.moved = 0
         self.pending = []
         self.kept = []
+        self.tags = {}
 
     def place(self, z, y, c):
         return (z * 2 + y) * 2 + c
@@ -95,6 +98,14 @@
                     del entries[k]
                     return
 
+    def tag(self, name, entries):
+        self.tags.setdefault(name, []).extend(entries)
+
+    def settle_tag(self, *names):
+        for name in names:
+            for entry in self.tags.pop(name, ()):
+                self.settle(entry)
+
     def drain(self):
         assert self.sent <= self.send_sems.shape[0] and self.moved <= self.local_sems.shape[0]
         for cond, copy in self.pending:
@@ -104,21 +115,21 @@
 
 
 class Gather:
-    def __init__(self, net, own, at, sems):
-        self.net, self.own, self.at = net, own, at
+    def __init__(self, net, own, at, sems, tag):
+        self.net, self.own, self.at, self.tag = net, own, at, tag
         self.sems = sems
 
     def spread(self, block, src, ysend=True):
         net = self.net
         here = net.place(block, net.y, net.c)
-        net.send(src, self.at(here), self.sems.at[1, block], net.device(y=1 - net.y))
-        net.send(src, self.at(here), self.sems.at[2 + net.y, block], net.device(c=1 - net.c))
+        net.tag(self.tag, [net.send(src, self.at(here), self.sems.at[1, block], net.device(y=1 - net.y))])
+        net.tag(self.tag, [net.send(src, self.at(here), self.sems.at[2 + net.y, block], net.device(c=1 - net.c))])
 
     def start(self):
         net = self.net
         here = self.at(net.dp_index)
-        net.send(self.own, here, self.sems.at[0, net.z], net.device(z=net.z + 1), net.z < net.n - 1)
-        net.send(self.own, here, self.sems.at[0, net.z], net.device(z=net.z - 1), net.z > 0)
+        net.tag(self.tag, [net.send(self.own, here, self.sems.at[0, net.z], net.device(z=net.z + 1), net.z < net.n - 1)])
+        net.tag(self.tag, [net.send(self.own, here, self.sems.at[0, net.z], net.device(z=net.z - 1), net.z > 0)])
         self.spread(net.z, self.own)
         self.kept = net.local(self.own, here)
 
@@ -135,15 +146,15 @@
             def _():
                 net.recv(here, self.sems.at[0, block])
 
-            net.send(here, here, self.sems.at[0, block], net.device(z=nxt), jnp.logical_and(valid, more))
-            net.send(here, here, self.sems.at[1, block], net.device(y=1 - net.y), valid)
-            net.send(here, here, self.sems.at[2 + net.y, block], net.device(c=1 - net.c), valid)
+            net.tag(self.tag, [net.send(here, here, self.sems.at[0, block], net.device(z=nxt), jnp.logical_and(valid, more))])
+            net.tag(self.tag, [net.send(here, here, self.sems.at[1, block], net.device(y=1 - net.y), valid)])
+            net.tag(self.tag, [net.send(here, here, self.sems.at[2 + net.y, block], net.device(c=1 - net.c), valid)])
 
     def cross(self, block):
         net = self.net
         there = self.at(net.place(block, 1 - net.y, net.c))
         net.recv(there, self.sems.at[1, block])
-        net.send(there, there, self.sems.at[3 - net.y, block], net.device(c=1 - net.c))
+        net.tag(self.tag, [net.send(there, there, self.sems.at[3 - net.y, block], net.device(c=1 - net.c))])
 
     def cross_step(self, s):
         net = self.net
@@ -159,7 +170,7 @@
             def _():
                 net.recv(there, self.sems.at[1, block])
 
-            net.send(there, there, self.sems.at[3 - net.y, block], net.device(c=1 - net.c), valid)
+            net.tag(self.tag, [net.send(there, there, self.sems.at[3 - net.y, block], net.device(c=1 - net.c), valid)])
 
     def finish(self, block):
         net = self.net
@@ -168,8 +179,8 @@
 
 
 class Exchange:
-    def __init__(self, net, part, at, sems):
-        self.net, self.part, self.at = net, part, at
+    def __init__(self, net, part, at, sems, tag):
+        self.net, self.part, self.at, self.tag = net, part, at, tag
         self.sems = sems
 
     def start(self):
@@ -177,10 +188,10 @@
         here = self.at(net.dp_index)
         for d in list(range(1, net.n)):
             to = (net.z + d) % net.n
-            net.send(self.part(to), here, self.sems.at[0, net.z], net.device(z=to))
+            net.tag(self.tag, [net.send(self.part(to), here, self.sems.at[0, net.z], net.device(z=to))])
         own = self.part(net.z)
-        net.send(own, here, self.sems.at[1, net.z], net.device(y=1 - net.y))
-        net.send(own, here, self.sems.at[2 + net.y, net.z], net.device(c=1 - net.c))
+        net.tag(self.tag, [net.send(own, here, self.sems.at[1, net.z], net.device(y=1 - net.y))])
+        net.tag(self.tag, [net.send(own, here, self.sems.at[2 + net.y, net.z], net.device(c=1 - net.c))])
         self.kept = net.local(own, here)
 
     def step(self, block):
@@ -190,43 +201,52 @@
         net.send(here, here, self.sems.at[1, block], net.device(y=1 - net.y))
         net.send(here, here, self.sems.at[2 + net.y, block], net.device(c=1 - net.c))
 
-    cross = Gather.cross
+    def cross(self, block):
+        net = self.net
+        there = self.at(net.place(block, 1 - net.y, net.c))
+        net.recv(there, self.sems.at[1, block])
+        net.send(there, there, self.sems.at[3 - net.y, block], net.device(c=1 - net.c))
+
     finish = Gather.finish
 
 
 class Rows:
-    def __init__(self, net, own, full, sems):
-        self.net, self.own, self.full = net, own, full
+    def __init__(self, net, own, at, sems, tag):
+        self.net, self.own, self.at, self.tag = net, own, at, tag
         self.sems = sems
 
     def start(self):
         net = self.net
-        here = self.full.at[net.z, net.x]
-        net.send(self.own, here, self.sems.at[0, net.z], net.device(z=net.z + 1), net.z < net.n - 1)
-        net.send(self.own, here, self.sems.at[0, net.z], net.device(z=net.z - 1), net.z > 0)
-        net.send(self.own, here, self.sems.at[1, net.z], net.device(x=1 - net.x))
-        self.kept = net.local(self.own, here)
+        here = self.at(net.z, net.x)
+        own = here if self.own is None else self.own
+        net.tag(self.tag, [net.send(own, here, self.sems.at[0, net.z], net.device(z=net.z + 1), net.z < net.n - 1)])
+        net.tag(self.tag, [net.send(own, here, self.sems.at[0, net.z], net.device(z=net.z - 1), net.z > 0)])
+        net.tag(self.tag, [net.send(own, here, self.sems.at[1, net.z], net.device(x=1 - net.x))])
+        if self.own is not None:
+            net.tag(self.tag + "_kept", [net.local(own, here)])
 
     def step(self, s):
         net = self.net
+        forwarded = []
         for sign in (1, -1):
             block = net.z - s * sign
             valid = jnp.logical_and(block >= 0, block < net.n)
             nxt = net.z + sign
             more = jnp.logical_and(nxt >= 0, nxt < net.n)
-            here = self.full.at[block, net.x]
+            here = self.at(block, net.x)
 
             @pl.when(valid)
             def _():
                 net.recv(here, self.sems.at[0, block])
 
-            net.send(here, here, self.sems.at[0, block], net.device(z=nxt), jnp.logical_and(valid, more))
-            net.send(here, here, self.sems.at[1, block], net.device(x=1 - net.x), valid)
-
-    def finish(self):
-        net = self.net
-        for block in range(net.n):
-            net.recv(self.full.at[block, 1 - net.x], self.sems.at[1, block])
+            forwarded.append(net.send(here, here, self.sems.at[0, block], net.device(z=nxt), jnp.logical_and(valid, more)))
+            forwarded.append(net.send(here, here, self.sems.at[1, block], net.device(x=1 - net.x), valid))
+        if self.own is None:
+            net.tag(self.tag, forwarded)
+
+    def finish(self, block):
+        net = self.net
+        net.recv(self.at(block, 1 - net.x), self.sems.at[1, block])
 
 
 class Reduce:
@@ -381,44 +401,136 @@
     return raised / jnp.sum(raised, axis=-1, keepdims=True)
 
 
-def attention_kernel(
+def far_first(net):
+    n = net.n
+    table = [sorted(range(n), key=lambda b: (-abs(b - z), -b)) for z in range(n)]
+    return [sum(jnp.where(net.z == z, table[z][k], 0) for z in range(n)) for k in range(n)]
+
+
+class RowSum:
+    def __init__(self, net, order, part, from_x, from_z, sems):
+        self.net, self.order, self.part, self.from_x, self.from_z = net, order, part, from_x, from_z
+        self.xs, self.zs = sems
+        self.sent = []
+        self.done_x = self.done_z = 0
+
+    def start(self, b):
+        net = self.net
+        self.sent.append(
+            net.send(self.part(b, 1 - net.x), self.from_x.at[b], self.xs.at[b], net.device(x=1 - net.x))
+        )
+
+    def add(self, total, term):
+        def body(r):
+            span = pl.ds(r, 16)
+            total[span] = (total[span].astype(F32) + term[span].astype(F32)).astype(BF16)
+
+        loop(total.shape[0], 16, body)
+
+    def step_x(self, k):
+        net = self.net
+        b = self.order[k]
+        self.done_x += 1
+        net.recv(self.from_x.at[b], self.xs.at[b])
+        self.add(self.part(b, net.x), self.from_x.at[b])
+
+    def step_z(self, k):
+        net = self.net
+        b = self.order[k]
+        self.done_z += 1
+        total = self.part(b, net.x)
+        behind = jnp.where(b > net.z, net.z > 0, net.z < net.n - 1)
+
+        @pl.when(jnp.logical_and(b != net.z, behind))
+        def _():
+            net.recv(self.from_z.at[b], self.zs.at[b])
+            self.add(total, self.from_z.at[b])
+
+        slot = jnp.where(b == net.z - 1, net.n, b)
+        to = jnp.where(b > net.z, net.z + 1, net.z - 1)
+        self.sent.append(net.send(total, self.from_z.at[slot], self.zs.at[slot], net.device(z=to), b != net.z))
+
+    def finish(self):
+        net = self.net
+        total = self.part(net.z, net.x)
+        for slot, cond in ((net.z, net.z > 0), (net.n, net.z < net.n - 1)):
+
+            @pl.when(cond)
+            def _():
+                net.recv(self.from_z.at[slot], self.zs.at[slot])
+                self.add(total, self.from_z.at[slot])
+
+
+def norm_back(grad, value, gain):
+    scale = lax.rsqrt(jnp.mean(value * value, axis=-1, keepdims=True) + EPSILON)
+    unit = value * scale
+    scaled = grad * gain
+    back = scale * (scaled - unit * jnp.mean(scaled * unit, axis=-1, keepdims=True))
+    return back, grad * unit
+
+
+def layer_kernel(
     dp,
-    residual, cotangent, seg, attn_gain, ffn_gain, freq, w_out, w_down, w_qkv, w_gate_up,
-    wa_out, wf_out, grad_out, normed_ffn_out, normed_out, attended_out, qkv_out, mixed_out, tables_out, gains_out, allowed,
-    weights, pre, gains, all_gains, live, grad_own, normed_all, ffn_own, partial, to_x, from_x, out_own, down_own,
+    residual, seg, attn_gain, ffn_gain, freq, w_out, w_down, w_qkv, w_gate_up, cotangent,
+    result, totals, wa_out, wf_out, normed_ffn_out, normed_out, attended_out, qkv_out, block_out, input_grad, gain_out,
+    weights, grad, hidden, gate_up_grad, back, back_x, back_z, part, from_c, from_y,
+    mixed_all, from_x, pre, mixed, tables, allowed, gains, all_gains, gains_all, gain_sum, ffn_sum, gain_to,
+    gain_from, gain_x,
     send_sems, local_sems, gain_sems, q_sems, o_sems, f_sems, g_sems, n_sems, x_sems,
+    bx_sems, bz_sems, rc_sems, ry_sems, rz_sems, rl_sems, back_gain_sems, free,
 ):
     net = Net(dp, send_sems, local_sems)
-    n = net.n
+    n, me, x = net.n, net.dp_index, net.x
     rows, width = residual.shape
     block, cols = w_qkv.shape[1:]
-    group = 2 * rows
-    part = w_gate_up.shape[2] // n
+    group = pair = 2 * rows
+    every = grad.shape[0]
     depth = width // n
-    me, x = net.dp_index, net.x
+    assert w_gate_up.shape[2] == n * cols and width == 2 * cols and width == 2 * every and width == dp * block
     lane = lax.broadcasted_iota(jnp.int32, (group, LANES), 1)
+    live = gain_to
+    assert gain_to.shape == (group // 16, 16, LANES)
+    order = far_first(net)
+    beside = jnp.where(net.z > 0, 1, 0) + jnp.where(net.z < n - 1, 1, 0)
     net.greet([((me + k) % dp, x) for k in range(1, dp)] + [(me, 1 - x)])
+
+    def block_rows_of(z, half):
+        return pl.ds(pl.multiple_of((z * 2 + half) * rows, rows), rows)
+
+    normed_all = back.at[0]
+    ffn_own, to_x = back.at[1, 0], back.at[1, 1]
+    down_own = hidden.at[pl.ds(0, n * block)]
+    out_own = hidden.at[pl.ds(n * block, block)]
+    early_qkv = [
+        gate_up_grad.at[pl.ds(0, group), pl.ds(0, cols)],
+        gate_up_grad.at[pl.ds(0, group), pl.ds(cols, cols)],
+        gate_up_grad.at[pl.ds(group, group), pl.ds(0, cols)],
+    ]
+    early_attended = gate_up_grad.at[pl.ds(group, group), pl.ds(cols, cols)]
 
     def at_weights(first, count):
         return lambda index: weights.at[pl.ds(first, count), pl.ds(pl.multiple_of(index * block, block), block)]
 
+    def at_out(index):
+        return weights.at[3, pl.ds(pl.multiple_of(index * block, block), block)]
+
     def ffn_part(m):
         def own(to):
-            span = pl.ds(pl.multiple_of(to * part, part), part)
-            return down_own.at[:, span] if m == 2 else w_gate_up.at[m, :, span]
+            if m == 2:
+                return down_own.at[pl.ds(pl.multiple_of(to * block, block), block)]
+            return w_gate_up.at[m, :, pl.ds(pl.multiple_of(to * cols, cols), cols)]
 
         return own
 
     def ffn_place(m):
         return lambda index: wf_out.at[m, pl.ds(pl.multiple_of(index * block, block), block)]
 
-    qkv = Gather(net, w_qkv, at_weights(0, 3), q_sems)
-    out = Gather(net, out_own, at_weights(3, 1), o_sems)
-    ffn = [Exchange(net, ffn_part(m), ffn_place(m), f_sems.at[m]) for m in range(3)]
-    grads = Rows(net, grad_own, grad_out, g_sems)
-    ffn_rows = Rows(net, ffn_own, normed_ffn_out, n_sems)
-    own_rows = normed_all.at[pl.ds(pl.multiple_of(x * rows, rows), rows)]
-    other_rows = normed_all.at[pl.ds(pl.multiple_of((1 - x) * rows, rows), rows)]
+    qkv = Gather(net, w_qkv, at_weights(0, 3), q_sems, "qkv")
+    out = Gather(net, out_own, at_out, o_sems, "out")
+    ffn = [Exchange(net, ffn_part(m), ffn_place(m), f_sems.at[m], "ffn") for m in range(3)]
+    grads = Rows(net, None, lambda z, half: grad.at[block_rows_of(z, half)], g_sems, "grads")
+    ffn_rows = Rows(net, ffn_own, lambda z, half: normed_ffn_out.at[z, half], n_sems, "rows")
+    load_grad = net.local(cotangent, grad.at[block_rows_of(net.z, x)])
 
     def send_gains():
         gains[0:8] = jnp.broadcast_to(attn_gain[...].astype(F32), (8, block))
@@ -428,31 +540,30 @@
         all_gains[me] = gains[...]
 
     def turn_weights():
-        out_own[0] = w_out[...].T
-
-        def body(r):
-            down_own[:, pl.ds(r, 512)] = w_down[pl.ds(r, 512)].T
-
-        loop(w_down.shape[0], 512, body)
+        out_own[...] = w_out[...].T
+        for q in range(n):
+            down_own[q * block : (q + 1) * block] = w_down[q * cols : (q + 1) * cols].T
 
     def mask_grads():
         seg_rows = jnp.broadcast_to(seg[...].astype(F32), (LANES, group))
         seg_cols = seg_rows.T
         alive = (seg_cols >= 0).astype(F32)
-        live[0] = alive[:rows]
-        live[1] = alive[rows:]
+        for i in range(group // 16):
+            live[i] = alive[i * 16 : (i + 1) * 16]
         row_id = lax.broadcasted_iota(jnp.int32, (group, group), 0)
         col_id = lax.broadcasted_iota(jnp.int32, (group, group), 1)
         same = jnp.concatenate([seg_cols] * (group // LANES), axis=1) == jnp.concatenate([seg_rows] * (group // LANES), axis=0)
         mask = jnp.logical_and(same, row_id >= col_id).astype(F32)
         allowed[...] = mask
         angles = (jnp.sum(mask, axis=1, keepdims=True) - 1.0) * freq[...]
-        tables_out[0] = jnp.cos(angles)
-        tables_out[1] = jnp.where(lane % HD < HD // 2, -jnp.sin(angles), jnp.sin(angles))
+        tables[0] = jnp.cos(angles)
+        tables[1] = jnp.where(lane % HD < HD // 2, -jnp.sin(angles), jnp.sin(angles))
+
+        net.settle(load_grad)
 
         def body(r):
-            span = pl.ds(r, 16)
-            grad_own[span] = (cotangent[span].astype(F32) * live[x, span, 0:1]).astype(BF16)
+            span = pl.ds(pl.multiple_of((net.z * 2 + x) * rows + r, 16), 16)
+            grad[span] = (grad[span].astype(F32) * live[(x * rows + r) // 16, :, 0:1]).astype(BF16)
 
         loop(rows, 16, body)
 
@@ -461,81 +572,99 @@
             source = (me + k) % dp
             net.recv(all_gains.at[source], gain_sems.at[source])
         for i in range(dp):
-            gains_out[:, i * block : (i + 1) * block] = all_gains[i]
+            gains_all[:, i * block : (i + 1) * block] = all_gains[i]
 
         def body(r):
             value = residual[pl.ds(r, 16)].astype(F32)
             unit = value * lax.rsqrt(jnp.mean(value * value, axis=-1, keepdims=True) + EPSILON)
-            to = pl.multiple_of(x * rows + r, 16)
-            normed_all[pl.ds(to, 16)] = (unit * gains_out[0:1]).astype(BF16)
+            normed_all[x, pl.ds(r, 16)] = (unit * gains_all[0:1]).astype(BF16)
 
         loop(rows, 16, body)
-        net.send(own_rows, own_rows, x_sems.at[0], net.device(x=1 - x))
+        net.tag("normed", [net.send(normed_all.at[x], normed_all.at[x], x_sems.at[0], net.device(x=1 - x))])
 
     def project(k):
         if k == 0:
-            net.recv(other_rows, x_sems.at[0])
+            net.recv(normed_all.at[1 - x], x_sems.at[0])
             net.settle(qkv.kept)
-            net.local(normed_all, normed_out)
+            net.tag("normed", [net.local(normed_all.at[half], normed_out.at[pl.ds(half * rows, rows)]) for half in (0, 1)])
         b = (net.z + k) % n
         qkv.finish(b)
         base = pl.multiple_of(b * depth, depth)
 
         def body(col):
+            left = jnp.concatenate([normed_all[0, :, pl.ds(base, depth)], normed_all[1, :, pl.ds(base, depth)]], axis=0)
             for m in range(3):
-                term = dot(normed_all[:, pl.ds(base, depth)], weights[m, pl.ds(base, depth), pl.ds(col, 256)])
+                term = dot(left, weights[m, pl.ds(base, depth), pl.ds(col, 256)])
                 to = pl.ds(pl.multiple_of(m * cols + col, 256), 256)
                 pre[:, to] = term if k == 0 else pre[:, to] + term
 
         loop(cols, 256, body)
-
-    def heads():
+        if k == n - 1:
+            net.tag("save", [net.local(weights.at[pl.ds(0, 3)], wa_out.at[pl.ds(0, 3)])])
+
+    def attend():
         masks = head_masks()
 
         def body(col):
-            cosine, sine = tables_out[0], tables_out[1]
+            cosine, sine = tables[0], tables[1]
             queries = turn(pre[:, pl.ds(col, LANES)], cosine, sine, lane).astype(BF16)
             key_rows = turn(pre[:, pl.ds(pl.multiple_of(cols + col, LANES), LANES)], cosine, sine, lane).astype(BF16)
             value_rows = pre[:, pl.ds(pl.multiple_of(2 * cols + col, LANES), LANES)].astype(BF16)
-            qkv_out[0, :, pl.ds(col, LANES)] = queries
-            qkv_out[1, :, pl.ds(col, LANES)] = key_rows
-            qkv_out[2, :, pl.ds(col, LANES)] = value_rows
+            early_qkv[0][:, pl.ds(col, LANES)] = queries
+            early_qkv[1][:, pl.ds(col, LANES)] = key_rows
+            early_qkv[2][:, pl.ds(col, LANES)] = value_rows
             may = jnp.concatenate([allowed[...], allowed[...]], axis=0)
             probs = softmax(both(queries, masks), key_rows, may).astype(BF16)
-            attended_out[:, pl.ds(col, LANES)] = pick(dot(probs, value_rows), group).astype(BF16)
+            early_attended[:, pl.ds(col, LANES)] = pick(dot(probs, value_rows), group).astype(BF16)
 
         loop(cols, LANES, body)
+        net.tag("early", [net.local(early_qkv[m], qkv_out.at[m]) for m in range(3)])
+        net.tag("early", [net.local(early_attended, attended_out)])
 
     def join():
         for k in range(n):
             out.finish((net.z + k) % n)
         net.settle(out.kept)
-        net.local(weights, wa_out)
+        net.tag("save_out", [net.local(weights.at[3], wa_out.at[3])])
 
         def body(col):
-            term = dot(attended_out[...], weights[3, pl.ds(col, 256), :], NT)
-            partial[0, :, pl.ds(col, 256)] = term[:rows]
-            partial[1, :, pl.ds(col, 256)] = term[rows:]
+            span = pl.ds(col, 256)
+            term = dot(early_attended[...], weights[3, span, :], NT)
+            low, high = term[:rows], term[rows:]
+            input_grad[:, span] = jnp.where(x == 0, low, high)
+            to_x[:, span] = jnp.where(x == 0, high, low).astype(BF16)
 
         loop(width, 256, body)
-
-        def to_body(r):
-            to_x[pl.ds(r, 16)] = partial[1 - x, pl.ds(r, 16)].astype(BF16)
-
-        loop(rows, 16, to_body)
-        net.send(to_x, from_x, x_sems.at[1], net.device(x=1 - x))
+        net.tag("to_x", [net.send(to_x, from_x, x_sems.at[1], net.device(x=1 - x))])
 
     def mix():
         net.recv(from_x, x_sems.at[1])
 
         def body(r):
             span = pl.ds(r, 16)
-            value = residual[span].astype(F32) + partial[x, span] + from_x[span].astype(F32)
-            mixed_out[span] = value
+            value = residual[span].astype(F32) + input_grad[span] + from_x[span].astype(F32)
+            mixed[span] = value
             unit = value * lax.rsqrt(jnp.mean(value * value, axis=-1, keepdims=True) + EPSILON)
-            ffn_own[span] = (unit * gains_out[8:9]).astype(BF16)
+            ffn_own[span] = (unit * gains_all[8:9]).astype(BF16)
 
         loop(rows, 16, body)
+
+    def load_ffn(m):
+        for k in range(n):
+            ffn[m].finish((net.z + k) % n)
+        net.settle(ffn[m].kept)
+        net.settle_tag("qkv", "save")
+        net.tag("weights", [net.local(wf_out.at[m], weights.at[m])])
+
+    def load_rows(k):
+        net.settle_tag("out", "save_out", "rows_kept")
+        b = order[k]
+        ffn_rows.finish(b)
+        for x_half in (0, 1):
+            for half in (0, 1):
+                there = pl.ds(pl.multiple_of(half * every + (b * 2 + x_half) * rows, rows), rows)
+                src = normed_ffn_out.at[b, x_half, :, pl.ds(half * cols, cols)]
+                net.tag("load%d" % k, [net.local(src, weights.at[3, there])])
 
     def ffn_step(m, k):
         ffn[m].step((net.z + k) % n)
@@ -544,160 +673,10 @@
         for k in range(n):
             ffn[m].cross((net.z + k) % n)
 
-    qkv.start()
-    turn_weights()
-    out.start()
-    qkv.step(1)
-    mask_grads()
-    send_gains()
-    out.step(1)
-    qkv.step(2)
-    qkv.cross_step(0)
-    norm()
-    qkv.cross_step(1)
-    ffn[2].start()
-    out.step(2)
-    grads.start()
-    qkv.step(3)
-    out.cross_step(0)
-    qkv.cross_step(2)
-    ffn[0].start()
-    qkv.cross_step(3)
-    project(0)
-    project(1)
-    out.cross_step(1)
-    project(2)
-    project(3)
-    out.cross_step(2)
-    grads.step(1)
-    out.step(3)
-    out.cross_step(3)
-    ffn_step(2, 3)
-    heads()
-    ffn[1].start()
-    join()
-    grads.step(2)
-    ffn_step(0, 2)
-    ffn_step(0, 3)
-    mix()
-    ffn_rows.start()
-    ffn_step(1, 1)
-    ffn_step(2, 2)
-    ffn_step(1, 2)
-    ffn_step(0, 1)
-    grads.step(3)
-    ffn_rows.step(1)
-    ffn_cross(0)
-    ffn_step(1, 3)
-    ffn_cross(1)
-    ffn_rows.step(2)
-    ffn_rows.step(3)
-    ffn_step(2, 1)
-    ffn_cross(2)
-    for m in range(3):
-        for k in range(n):
-            ffn[m].finish((net.z + k) % n)
-    grads.finish()
-    ffn_rows.finish()
-    net.drain()
-
-
-def far_first(net):
-    n = net.n
-    table = [sorted(range(n), key=lambda b: (-abs(b - z), -b)) for z in range(n)]
-    return [sum(jnp.where(net.z == z, table[z][k], 0) for z in range(n)) for k in range(n)]
-
-
-class RowSum:
-    def __init__(self, net, order, part, from_x, from_z, sems):
-        self.net, self.order, self.part, self.from_x, self.from_z = net, order, part, from_x, from_z
-        self.xs, self.zs = sems
-        self.sent = []
-        self.done_x = self.done_z = 0
-
-    def start(self, b):
-        net = self.net
-        self.sent.append(
-            net.send(self.part(b, 1 - net.x), self.from_x.at[b], self.xs.at[b], net.device(x=1 - net.x))
-        )
-
-    def add(self, total, term):
-        def body(r):
-            span = pl.ds(r, 16)
-            total[span] = (total[span].astype(F32) + term[span].astype(F32)).astype(BF16)
-
-        loop(total.shape[0], 16, body)
-
-    def step_x(self):
-        net = self.net
-        b = self.order[self.done_x]
-        self.done_x += 1
-        net.recv(self.from_x.at[b], self.xs.at[b])
-        self.add(self.part(b, net.x), self.from_x.at[b])
-
-    def step_z(self):
-        net = self.net
-        b = self.order[self.done_z]
-        self.done_z += 1
-        total = self.part(b, net.x)
-        behind = jnp.where(b > net.z, net.z > 0, net.z < net.n - 1)
-
-        @pl.when(jnp.logical_and(b != net.z, behind))
-        def _():
-            net.recv(self.from_z.at[b], self.zs.at[b])
-            self.add(total, self.from_z.at[b])
-
-        slot = jnp.where(b == net.z - 1, net.n, b)
-        to = jnp.where(b > net.z, net.z + 1, net.z - 1)
-        self.sent.append(net.send(total, self.from_z.at[slot], self.zs.at[slot], net.device(z=to), b != net.z))
-
-    def finish(self):
-        net = self.net
-        total = self.part(net.z, net.x)
-        for slot, cond in ((net.z, net.z > 0), (net.n, net.z < net.n - 1)):
-
-            @pl.when(cond)
-            def _():
-                net.recv(self.from_z.at[slot], self.zs.at[slot])
-                self.add(total, self.from_z.at[slot])
-
-
-def norm_back(grad, value, gain):
-    scale = lax.rsqrt(jnp.mean(value * value, axis=-1, keepdims=True) + EPSILON)
-    unit = value * scale
-    scaled = grad * gain
-    back = scale * (scaled - unit * jnp.mean(scaled * unit, axis=-1, keepdims=True))
-    return back, grad * unit
-
-
-def ffn_kernel(
-    dp,
-    mixed, residual, gains, allowed, tables, normed_ffn_hbm, grad_hbm, wf, normed_hbm, attended_hbm, qkv_hbm, wa,
-    result, totals, block_out, input_grad, gain_out,
-    weights, grad, hidden, gate_up_grad, back, back_x, back_z, part, from_c, from_y,
-    mixed_all, from_x, gain_sum, ffn_sum, gain_to, gain_from, gain_x,
-    send_sems, local_sems, bx_sems, bz_sems, rc_sems, ry_sems, rz_sems, rl_sems, x_sems, gain_sems, free,
-):
-    net = Net(dp, send_sems, local_sems)
-    n, me, x = net.n, net.dp_index, net.x
-    rows, width = mixed.shape
-    cols = wf.shape[2]
-    every = grad.shape[0]
-    block = width // dp
-    depth = width // n
-    pair = 2 * rows
-    assert width == 2 * cols and width == 2 * every and wa.shape[2] == cols
 
     def features(half):
         return weights.at[3, pl.ds(half * every, every)]
 
-    loads = [net.local(normed_ffn_hbm.at[:, pl.ds(half * cols, cols)], features(half)) for half in (0, 1)]
-    loads += [net.local(wf.at[m], weights.at[m]) for m in range(3)] + [net.local(grad_hbm, grad)]
-    net.greet(
-        [((me + k) % dp, x) for k in range(1, dp)] + [(me, 1 - x)]
-    )
-    order = far_first(net)
-    beside = jnp.where(net.z > 0, 1, 0) + jnp.where(net.z < n - 1, 1, 0)
     gate_grad, up_grad = gate_up_grad.at[:, pl.ds(0, cols)], gate_up_grad.at[:, pl.ds(cols, cols)]
     add = gate_up_grad
     backs = RowSum(net, order, lambda b, half: back.at[b, half], back_x, back_z, (bx_sems, bz_sems))
@@ -710,13 +689,12 @@
         lambda m, to: weights.at[3, pl.ds(pl.multiple_of((m * n + to) * block, block), block)],
         (rc_sems, ry_sems, rz_sems, rl_sems, free), 7 * n,
     )
-    for load in loads:
-        net.settle(load)
-
     def rows_of(b):
         return pl.ds(pl.multiple_of(b * pair, pair), pair)
 
     def forward(k):
+        net.settle_tag("load%d" % k, "weights", "ffn", "early")
+        grads.finish(order[k])
         here = rows_of(order[k])
 
         def body(col):
@@ -738,6 +716,7 @@
         loop(cols, 256, body)
 
     def backward(k):
+        net.settle_tag("normed", "to_x", "rows")
         b = order[k]
         here = rows_of(b)
 
@@ -759,6 +738,9 @@
             add[here, span] = dot(hidden[here], weights[2, span, :], NT).astype(BF16)
 
         loop(width, 256, body)
+        if k == 0:
+            pl.semaphore_wait(free.at[2], 1)
+        adds.start(order[k])
 
     ffn_items = [(2, k) for k in range(n)] + [(m, k) for k in range(n) for m in (0, 1)]
     attention_items = [(3, k) for k in range(n)] + [(m, k) for k in range(n) for m in range(3)]
@@ -807,34 +789,35 @@
         def body(r):
             span = pl.ds(r, 16)
             own = pl.ds(pl.multiple_of((net.z * 2 + x) * rows + r, 16), 16)
-            term, gain_term = norm_back(back[net.z, x, span].astype(F32), mixed[span], gains[8:9])
+            term, gain_term = norm_back(back[net.z, x, span].astype(F32), mixed[span], gains_all[8:9])
             value = grad[own].astype(F32) + term
             input_grad[span] = value
             mixed_all[pl.ds(pl.multiple_of(x * rows + r, 16), 16)] = value.astype(BF16)
             ffn_sum[...] += gain_term[:8] + gain_term[8:]
 
         loop(rows, 16, body)
-        net.send(own_rows, own_rows, x_sems.at[0], net.device(x=1 - x))
+        net.send(own_rows, own_rows, x_sems.at[2], net.device(x=1 - x))
         pl.semaphore_signal(free.at[2], inc=1, device_id=net.device(x=1 - x), device_id_type=MESH)
         tell_beside(3)
 
     def load_out():
-        late["out"] = net.local(wa.at[3], weights.at[3])
+        late["out"] = net.local(wa_out.at[3], weights.at[3])
 
     def load_rest():
-        late["normed"] = net.local(normed_hbm, normed)
-        late["qkv"] = net.local(wa.at[pl.ds(0, 3)], weights.at[pl.ds(0, 3)])
-        late["parts"] = [net.local(qkv_hbm.at[m], hidden.at[pl.ds(m * pair, pair)]) for m in range(3)]
-        late["attended"] = net.local(attended_hbm, attended)
-
-    def start_adds():
-        pl.semaphore_wait(free.at[2], 1)
-        for k in range(n):
-            adds.start(order[k])
+        net.settle_tag("grads")
+        late["normed"] = net.local(normed_out, normed)
+        late["qkv"] = net.local(wa_out.at[pl.ds(0, 3)], weights.at[pl.ds(0, 3)])
+        late["parts"] = [net.local(qkv_out.at[m], hidden.at[pl.ds(m * pair, pair)]) for m in range(3)]
+        late["attended"] = net.local(attended_out, attended)
+
+    def step_adds():
+        if adds.done_z == 0:
+            pl.semaphore_wait(free.at[3], beside)
+        adds.step_z(adds.done_z)
 
     def attended_back():
         net.settle(late["out"])
-        net.recv(other_rows, x_sems.at[0])
+        net.recv(other_rows, x_sems.at[2])
 
         def body(col):
             span = pl.ds(col, 256)
@@ -848,7 +831,6 @@
         for load in late["parts"]:
             net.settle(load)
         masks = head_masks()
-        lane = lax.broadcasted_iota(jnp.int32, (pair, LANES), 1)
 
         def body(col):
             span = pl.ds(col, LANES)
@@ -885,16 +867,16 @@
             back[0, 1, :, span] = term[rows:].astype(BF16)
 
         loop(width, 256, body)
-        net.send(back.at[0, 1 - x], from_x, x_sems.at[1], net.device(x=1 - x))
+        net.send(back.at[0, 1 - x], from_x, x_sems.at[3], net.device(x=1 - x))
 
     def input_back():
-        net.recv(from_x, x_sems.at[1])
+        net.recv(from_x, x_sems.at[3])
         gain_sum[...] = jnp.zeros_like(gain_sum)
 
         def body(r):
             span = pl.ds(r, 16)
             grad_rows = back[0, x, span].astype(F32) + from_x[span].astype(F32)
-            term, gain_term = norm_back(grad_rows, residual[span].astype(F32), gains[0:1])
+            term, gain_term = norm_back(grad_rows, residual[span].astype(F32), gains_all[0:1])
             input_grad[span] += term
             gain_sum[...] += gain_term[:8] + gain_term[8:]
 
@@ -904,16 +886,16 @@
             gain_to[i, 8:16] = ffn_sum[:, i * block : (i + 1) * block]
         for k in range(1, dp):
             to = (me + k) % dp
-            net.send(gain_to.at[to], gain_from.at[me], gain_sems.at[me], (to, x))
+            net.send(gain_to.at[to], gain_from.at[me], back_gain_sems.at[me], (to, x))
 
     def sum_gains():
         total = gain_to[me]
         for k in range(1, dp):
             source = (me + k) % dp
-            net.recv(gain_from.at[source], gain_sems.at[source])
+            net.recv(gain_from.at[source], back_gain_sems.at[source])
             total = total + gain_from[source]
         gain_x[0] = total
-        net.send(gain_x.at[0], gain_x.at[1], x_sems.at[2], net.device(x=1 - x))
+        net.send(gain_x.at[0], gain_x.at[1], x_sems.at[4], net.device(x=1 - x))
 
     def block_rows():
         adds.finish()
@@ -924,145 +906,200 @@
 
         loop(rows, 16, body)
 
+    qkv.start()
+    turn_weights()
+    out.start()
+    send_gains()
+    qkv.step(1)
+    out.step(1)
+    qkv.step(2)
+    qkv.cross_step(0)
+    out.cross_step(0)
+    ffn[0].start()
+    mask_grads()
+    out.step(2)
+    norm()
+    grads.start()
+    ffn[2].start()
+    qkv.cross_step(1)
+    qkv.step(3)
+    qkv.cross_step(2)
+    ffn_step(0, 3)
+    out.cross_step(1)
+    out.step(3)
+    ffn_step(0, 2)
+    qkv.cross_step(3)
+    project(0)
+    ffn_step(0, 1)
+    grads.step(1)
+    project(1)
+    project(2)
+    out.cross_step(2)
+    project(3)
+    ffn[1].start()
+    attend()
+    out.cross_step(3)
+    join()
+    mix()
+    ffn_rows.start()
+    grads.step(2)
+    ffn_step(2, 1)
+    ffn_step(2, 3)
+    ffn_step(1, 1)
+    ffn_step(1, 3)
+    ffn_step(1, 2)
+    ffn_step(2, 2)
+    ffn_rows.step(1)
+    load_rows(3)
+    ffn_cross(1)
+    ffn_cross(0)
+    grads.step(3)
+    ffn_cross(2)
+    load_ffn(0)
+    load_ffn(2)
+    load_rows(2)
+    ffn_rows.step(2)
+    load_ffn(1)
+    forward(3)
+    forward(2)
+    ffn_rows.step(3)
+    load_rows(1)
+    forward(1)
+    backward(2)
+    load_rows(0)
     forward(0)
+    ffn_item()
     backward(0)
-    forward(1)
+    red.step_c()
     backward(1)
-    forward(2)
-    forward(3)
-    backs.step_x()
-    backs.step_z()
     ffn_item()
-    backward(2)
-    red.step_c()
+    red.step_y()
+    backs.step_x(2)
     ffn_item()
-    backs.step_x()
-    ffn_item()
-    backs.step_z()
-    red.step_c()
-    ffn_item()
-    red.step_y()
-    ffn_item()
-    backs.step_x()
-    red.step_c()
-    red.step_c()
-    backs.step_z()
-    backward(3)
+    red.step_c()
+    backs.step_x(0)
+    backs.step_z(0)
+    red.step_c()
     ffn_item()
     ffn_item()
-    red.step_c()
+    backward(3)
+    red.step_c()
+    backs.step_x(1)
+    backs.step_z(1)
+    backs.step_z(2)
     red.step_c()
     ffn_item()
     ffn_item()
+    red.step_y()
+    red.step_y()
+    red.step_c()
     red.step_c()
     ffn_item()
-    backs.step_x()
-    red.step_y()
-    red.step_c()
-    red.step_y()
-    red.step_y()
-    red.step_c()
     ffn_item()
-    backs.step_z()
+    red.step_c()
+    backs.step_x(3)
+    red.step_y()
     ffn_item()
-    add_chunk(0)
-    red.step_y()
-    red.step_c()
-    load_out()
-    red.step_y()
-    red.step_c()
     red.step_y()
     mix_grads()
-    add_chunk(1)
-    add_chunk(2)
-    red.step_y()
-    add_chunk(3)
-    red.step_c()
-    start_adds()
-    load_rest()
-    attended_back()
-    red.step_y()
-    red.step_y()
-    pl.semaphore_wait(free.at[3], beside)
-    attention_item()
-    attention_item()
-    red.step_c()
-    attention_item()
-    red.step_c()
-    red.step_y()
-    attention_item()
-    heads()
-    adds.step_x()
-    adds.step_z()
-    red.step_y()
-    pl.semaphore_wait(free.at[4], beside)
-    red.step_c()
-    adds.step_x()
-    attention_item()
-    red.step_y()
-    red.step_c()
-    red.step_y()
-    attention_item()
-    red.step_c()
-    attention_item()
-    red.step_z()
-    adds.step_z()
-    red.step_y()
-    red.step_z()
-    red.step_y()
-    red.step_c()
-    attention_item()
-    red.step_c()
-    attention_item()
-    adds.step_x()
-    normed_back()
-    attention_item()
-    red.step_z()
-    red.step_c()
-    adds.step_z()
-    attention_item()
-    red.step_c()
-    red.step_y()
-    attention_item()
-    red.step_z()
-    red.step_y()
-    red.step_c()
-    attention_item()
-    attention_item()
-    red.step_z()
-    red.step_y()
-    adds.step_x()
-    red.step_y()
-    red.step_z()
-    red.step_c()
-    adds.step_z()
-    red.step_c()
-    red.step_c()
-    attention_item()
-    input_back()
-    red.step_y()
-    red.step_y()
-    red.step_z()
-    red.step_z()
-    red.step_c()
-    red.step_y()
-    attention_item()
-    red.step_c()
-    red.step_c()
-    red.step_y()
-    for _ in range(3):
-        red.step_z()
-    red.step_y()
-    sum_gains()
-    red.step_z()
-    red.step_z()
+    red.step_c()
+    red.step_c()
     for _ in range(3):
         red.step_y()
+    ffn_item()
+    ffn_item()
+    red.step_y()
+    add_chunk(0)
+    add_chunk(1)
+    red.step_c()
+    add_chunk(2)
+    load_out()
+    add_chunk(3)
+    load_rest()
+    red.step_y()
+    attended_back()
+    heads()
+    red.step_c()
+    attention_item()
+    adds.step_x(adds.done_x)
+    red.step_y()
+    red.step_c()
+    step_adds()
+    attention_item()
+    red.step_c()
+    attention_item()
+    adds.step_x(adds.done_x)
+    for _ in range(3):
+        attention_item()
+    red.step_c()
+    red.step_y()
+    attention_item()
+    red.step_c()
+    attention_item()
+    pl.semaphore_wait(free.at[4], beside)
+    step_adds()
+    red.step_c()
+    red.step_y()
+    red.step_z()
+    red.step_c()
+    red.step_c()
+    attention_item()
+    normed_back()
+    red.step_y()
+    red.step_z()
+    red.step_c()
+    red.step_y()
+    adds.step_x(adds.done_x)
+    attention_item()
+    step_adds()
+    red.step_y()
+    red.step_z()
+    red.step_c()
+    red.step_y()
+    attention_item()
+    red.step_y()
+    red.step_y()
+    red.step_z()
+    input_back()
+    red.step_y()
+    red.step_z()
+    red.step_c()
+    attention_item()
+    red.step_c()
+    red.step_z()
+    red.step_y()
+    adds.step_x(adds.done_x)
+    red.step_z()
+    red.step_y()
+    red.step_c()
+    attention_item()
+    red.step_c()
+    red.step_z()
+    red.step_y()
+    sum_gains()
+    red.step_z()
+    attention_item()
+    red.step_c()
+    attention_item()
+    red.step_z()
+    red.step_z()
+    red.step_y()
+    attention_item()
+    red.step_z()
+    red.step_y()
+    red.step_c()
+    red.step_z()
+    step_adds()
+    red.step_c()
+    red.step_y()
+    red.step_y()
+    red.step_z()
+    red.step_z()
+    red.step_y()
     block_rows()
-    for _ in range(3):
-        red.step_z()
-    assert red.done_y == red.done_z == red.total and adds.done_z == n
-    net.recv(gain_x.at[1], x_sems.at[2])
+    red.step_z()
+    assert red.done_y == red.done_z == red.total and adds.done_z == n and backs.done_x == n
+    net.recv(gain_x.at[1], x_sems.at[4])
     gain_out[...] = gain_x[0] + gain_x[1]
     red.finish()
     net.drain()
@@ -1112,46 +1149,35 @@
     part = w_gate_up.shape[2] // n
     pairs = jnp.arange(LANES, dtype=jnp.int32) % (HD // 2)
     freq = (ROPE_BASE ** (-(pairs.astype(F32) * 2.0 / HD)))[None]
-    mib = 1024 * 1024
-
-    first = call(
-        functools.partial(attention_kernel, dp), 1, 192, 12, 60 * mib,
+
+    every = n * 2 * rows
+    slots = SLOTS
+    layer = call(
+        functools.partial(layer_kernel, dp), 1, 320, 112, LIMIT,
         [
-            (4, width, cols), (3, width, part), (n, 2, rows, width), (n, 2, rows, width), (group, width),
-            (group, cols), (3, group, cols), (rows, width, F32), (2, group, LANES, F32), (16, width, F32), (group, group, F32),
+            (3, n, block, part), (4, 3, block, cols), (4, width, cols), (3, width, part), (n, 2, rows, width),
+            (group, width), (group, cols), (3, group, cols), (rows, width), (rows, width, F32), (16, block, F32),
         ],
-        [ANY] * 5 + [VM] * 6,
+        [ANY] * 8 + [VM] * 3,
         [
-            (4, width, cols), (group, 3 * cols, F32), (16, block, F32), (dp, 16, block, F32), (2, rows, LANES, F32),
-            (rows, width), (group, width), (rows, width), (2, rows, width, F32), (rows, width), (rows, width),
-            (1, block, cols), (block, n * part),
-        ],
-        [(dp,), (4, n), (4, n), (3, 4, n), (2, n), (2, n), (2,)],
-    )
-    (weights, ffn_weights, grad_all, normed_ffn, normed, attended, qkv, mixed, tables, all_gains, allowed) = first(
-        [VM] * 8 + [ANY] * 2, residual, cotangent, seg_ids[None], attn_gain[None], ffn_gain[None], freq, w_out, w_down,
-        w_qkv, w_gate_up,
-    )
-    every = n * 2 * rows
-    slots = 3 * n
-    second = call(
-        functools.partial(ffn_kernel, dp), 2, 192, 64, 63 * mib,
-        [(3, n, block, part), (4, 3, block, cols), (rows, width), (rows, width, F32), (16, block, F32)],
-        [ANY] * 2 + [VM] * 3,
-        [
-            (4, width, part), (every, width), (every, part), (every, 2 * part),
+            (4, width, cols), (every, width), (every, part), (every, 2 * part),
             (n, 2, rows, width), (n, rows, width), (n + 1, rows, width),
             (slots, 2, 2, block, part), (slots, 2, block, part), (slots, block, part),
-            (group, width), (rows, width), (8, width, F32), (8, width, F32),
-            (dp, 16, block, F32), (dp, 16, block, F32), (2, 16, block, F32),
+            (group, width), (rows, width), (group, 3 * cols, F32), (rows, width, F32), (2, group, LANES, F32),
+            (group, group, F32), (16, block, F32), (dp, 16, block, F32), (16, width, F32),
+            (8, width, F32), (8, width, F32), (dp, 16, block, F32), (dp, 16, block, F32), (2, 16, block, F32),
         ],
-        [(n,), (n + 1,), (slots,), (slots,), (3, n), (4, n + 2), (3,), (dp,)],
+        [
+            (dp,), (4, n), (4, n), (3, 4, n), (2, n), (2, n), (5,),
+            (n,), (n + 1,), (slots,), (slots,), (3, n), (4, n + 2), (dp,),
+        ],
         5,
     )
-    result, totals, block_out, input_grad, gain_grads = second(
-        [VM] * 5 + [ANY] * 7, mixed, residual, all_gains, allowed, tables, normed_ffn.reshape(every, width),
-        grad_all.reshape(every, width), ffn_weights, normed, attended, qkv, weights,
-    )
+    outputs = layer(
+        [VM] * 7 + [ANY] * 3, residual, seg_ids[None], attn_gain[None], ffn_gain[None], freq, w_out, w_down, w_qkv,
+        w_gate_up, cotangent,
+    )
+    result, totals, block_out, input_grad, gain_grads = outputs[0], outputs[1], outputs[8], outputs[9], outputs[10]
     qkv_grad, out_grad, gate_up_grad, down_grad, gain_sums = pl.pallas_call(
         finish_kernel,
         grid=(n,),
@@ -1171,7 +1197,7 @@
             pl.BlockSpec((part, block), lambda q: (q, 0)),
             pl.BlockSpec((2, block), lambda q: (0, 0)),
         ],
-        compiler_params=pltpu.CompilerParams(vmem_limit_bytes=32 * mib),
+        compiler_params=pltpu.CompilerParams(vmem_limit_bytes=LIMIT),
     )(result, totals, gain_grads)
     return block_out, input_grad, gain_sums[0], qkv_grad, out_grad, gain_sums[1], gate_up_grad, down_grad
 

time: 472 us -> 462 us (0.979); the launches traced: 466 us -> 461 us
    pallas_call x2 -> x1, Pallas kernels: 453 us -> 447 us  [call(): pl.pallas_call(kernel, out_shape=[jax.ShapeDtypeStruct(*typed(entry)) for...]
where the time goes in v4:
time: 462 us; the launch traced here: 461 us
  Pallas kernels  455 us (98%)
  local copies, waits for them, and re-layouts  5.45 us (1%)
    pallas_call x1, Pallas kernels, call(): pl.pallas_call(kernel, out_shape=[jax.ShapeDtypeStruct(*typed(entry)) for...  447 us

profile of v4, /device:TPU:12, one launch (start us, length us, event | category | flops | bytes accessed | tf_op | source)
XLA Modules:
  0.0 461.3 jit_solution(16801199870261828782)
XLA Ops:
  0.6 0.5 fusion.3.freq
  1.2 447.4 %shard_map.152 = (bf16[3,4,128,1024]{3,2,1,0:T(8,128)(2,1)}, bf16[4,3,128,1024]{3,2,1,0:T(8,128)(2,1)}, bf16[4,2048,1024]{2,1,0:T(8,128)(2,1)}, bf16[3,2048,1024...) custom-call(bf16[128,2048]{1,0:T(8,128)(2,1)} %residual.1, ...), custom_call_target="tpu_custom_call" | custom-call | tf_op jit(solution)/shard_map/pallas_call | solution.py:1134
  448.5 7.4 %shard_map.153 = (f32[3,128,1024]{2,1,0:T(8,128)}, f32[1024,128]{1,0:T(8,128)}, f32[2,128,4096]{2,1,0:T(8,128)}, f32[4096,128]{1,0:T(8,128)}, f32[2,128]{1,0:T(2,128)}) custom-call(bf16[3,4,128,1024]{3,2,1,0:T(8,128)(2,1)} %get-tuple-element.20.ffn, bf16[4,3,128,1024]{3,2,1,0:T(8,128)(2,1)} %get-tuple-element.21.attention, f32[16,128]{1,0:T(8,128)} %get-tuple-element.22.gains), custom_call_target="tpu_custom_call" | custom-call | tf_op jit(solution)/shard_map/pallas_call | solution.py:1181
  455.9 1.3 slice_bitcast_fusion
  457.2 1.9 copy.19
  459.0 2.3 copy.20

commit v5 on v4

--- a/solution.py
+++ b/solution.py
@@ -266,7 +266,7 @@
             span = pl.ds(r, 16)
             total[span] = (total[span].astype(F32) + term[span].astype(F32)).astype(BF16)
 
-        loop(total.shape[0], 16, body)
+        loop(total.shape[0], 16, body, 8)
 
     def credit(self, which, device):
         pl.semaphore_signal(self.free.at[which], inc=1, device_id=device, device_id_type=MESH)
@@ -287,7 +287,7 @@
                     at = (y * 2 + c) * block
                     self.part[slot, c, y, :, pl.ds(col, 256)] = term[at : at + block]
 
-        loop(right.shape[1], 256, body)
+        loop(right.shape[1], 256, body, 4)
         if i >= self.slots:
             pl.semaphore_wait(self.free.at[0], 1)
         self.out[i] = [
@@ -368,8 +368,8 @@
                     net.recv(self.totals.at[m, side], self.ls.at[m, net.n + side])
 
 
-def loop(total, step, body):
-    @pl.loop(0, total // step)
+def loop(total, step, body, unroll):
+    @pl.loop(0, total // step, unroll=unroll)
     def _(i):
         body(pl.multiple_of(i * step, step))
 
@@ -425,7 +425,7 @@
             span = pl.ds(r, 16)
             total[span] = (total[span].astype(F32) + term[span].astype(F32)).astype(BF16)
 
-        loop(total.shape[0], 16, body)
+        loop(total.shape[0], 16, body, 8)
 
     def step_x(self, k):
         net = self.net
@@ -565,7 +565,7 @@
             span = pl.ds(pl.multiple_of((net.z * 2 + x) * rows + r, 16), 16)
             grad[span] = (grad[span].astype(F32) * live[(x * rows + r) // 16, :, 0:1]).astype(BF16)
 
-        loop(rows, 16, body)
+        loop(rows, 16, body, 4)
 
     def norm():
         for k in range(1, dp):
@@ -579,7 +579,7 @@
             unit = value * lax.rsqrt(jnp.mean(value * value, axis=-1, keepdims=True) + EPSILON)
             normed_all[x, pl.ds(r, 16)] = (unit * gains_all[0:1]).astype(BF16)
 
-        loop(rows, 16, body)
+        loop(rows, 16, body, 4)
         net.tag("normed", [net.send(normed_all.at[x], normed_all.at[x], x_sems.at[0], net.device(x=1 - x))])
 
     def project(k):
@@ -598,7 +598,7 @@
                 to = pl.ds(pl.multiple_of(m * cols + col, 256), 256)
                 pre[:, to] = term if k == 0 else pre[:, to] + term
 
-        loop(cols, 256, body)
+        loop(cols, 256, body, 4)
         if k == n - 1:
             net.tag("save", [net.local(weights.at[pl.ds(0, 3)], wa_out.at[pl.ds(0, 3)])])
 
@@ -617,7 +617,7 @@
             probs = softmax(both(queries, masks), key_rows, may).astype(BF16)
             early_attended[:, pl.ds(col, LANES)] = pick(dot(probs, value_rows), group).astype(BF16)
 
-        loop(cols, LANES, body)
+        loop(cols, LANES, body, 4)
         net.tag("early", [net.local(early_qkv[m], qkv_out.at[m]) for m in range(3)])
         net.tag("early", [net.local(early_attended, attended_out)])
 
@@ -634,7 +634,7 @@
             input_grad[:, span] = jnp.where(x == 0, low, high)
             to_x[:, span] = jnp.where(x == 0, high, low).astype(BF16)
 
-        loop(width, 256, body)
+        loop(width, 256, body, 4)
         net.tag("to_x", [net.send(to_x, from_x, x_sems.at[1], net.device(x=1 - x))])
 
     def mix():
@@ -647,7 +647,7 @@
             unit = value * lax.rsqrt(jnp.mean(value * value, axis=-1, keepdims=True) + EPSILON)
             ffn_own[span] = (unit * gains_all[8:9]).astype(BF16)
 
-        loop(rows, 16, body)
+        loop(rows, 16, body, 4)
 
     def load_ffn(m):
         for k in range(n):
@@ -713,7 +713,7 @@
             gate_grad[here, span] = (hidden_grad * up * sigmoid * (1.0 + gate * (1.0 - sigmoid))).astype(BF16)
             up_grad[here, span] = (hidden_grad * active).astype(BF16)
 
-        loop(cols, 256, body)
+        loop(cols, 256, body, 4)
 
     def backward(k):
         net.settle_tag("normed", "to_x", "rows")
@@ -727,7 +727,7 @@
             back[b, 0, :, span] = term[:rows]
             back[b, 1, :, span] = term[rows:]
 
-        loop(width, 256, body)
+        loop(width, 256, body, 4)
         backs.start(b)
 
     def add_chunk(k):
@@ -737,7 +737,7 @@
             span = pl.ds(col, 256)
             add[here, span] = dot(hidden[here], weights[2, span, :], NT).astype(BF16)
 
-        loop(width, 256, body)
+        loop(width, 256, body, 4)
         if k == 0:
             pl.semaphore_wait(free.at[2], 1)
         adds.start(order[k])
@@ -795,7 +795,7 @@
             mixed_all[pl.ds(pl.multiple_of(x * rows + r, 16), 16)] = value.astype(BF16)
             ffn_sum[...] += gain_term[:8] + gain_term[8:]
 
-        loop(rows, 16, body)
+        loop(rows, 16, body, 4)
         net.send(own_rows, own_rows, x_sems.at[2], net.device(x=1 - x))
         pl.semaphore_signal(free.at[2], inc=1, device_id=net.device(x=1 - x), device_id_type=MESH)
         tell_beside(3)
@@ -823,7 +823,7 @@
             span = pl.ds(col, 256)
             attended_grad[:, span] = dot(mixed_all[...], weights[3, :, span]).astype(BF16)
 
-        loop(cols, 256, body)
+        loop(cols, 256, body, 4)
         tell_beside(4)
         net.settle(late["attended"])
 
@@ -850,7 +850,7 @@
             grads_of[1][:, span] = turn(key_grad, cosine, -sine, lane).astype(BF16)
             grads_of[2][:, span] = value_grad.astype(BF16)
 
-        loop(cols, LANES, body)
+        loop(cols, LANES, body, 4)
         net.settle(late["normed"])
 
     def normed_back():
@@ -866,7 +866,7 @@
             back[0, 0, :, span] = term[:rows].astype(BF16)
             back[0, 1, :, span] = term[rows:].astype(BF16)
 
-        loop(width, 256, body)
+        loop(width, 256, body, 4)
         net.send(back.at[0, 1 - x], from_x, x_sems.at[3], net.device(x=1 - x))
 
     def input_back():
@@ -880,7 +880,7 @@
             input_grad[span] += term
             gain_sum[...] += gain_term[:8] + gain_term[8:]
 
-        loop(rows, 16, body)
+        loop(rows, 16, body, 4)
         for i in range(dp):
             gain_to[i, 0:8] = gain_sum[:, i * block : (i + 1) * block]
             gain_to[i, 8:16] = ffn_sum[:, i * block : (i + 1) * block]
@@ -904,7 +904,7 @@
             span = pl.ds(r, 16)
             block_out[span] = (mixed[span] + adds.part(net.z, x)[span].astype(F32)).astype(BF16)
 
-        loop(rows, 16, body)
+        loop(rows, 16, body, 4)
 
     qkv.start()
     turn_weights()

time: 462 us -> 456 us (0.987); the launches traced: 461 us -> 450 us
  Pallas kernels: 455 us -> 443 us
    pallas_call x1, Pallas kernels: 447 us -> 435 us  [call(): pl.pallas_call(kernel, out_shape=[jax.ShapeDtypeStruct(*typed(entry)) for...]
where the time goes in v5:
time: 456 us; the launch traced here: 450 us
  Pallas kernels  443 us (97%)
  local copies, waits for them, and re-layouts  5.45 us (1%)
    pallas_call x1, Pallas kernels, call(): pl.pallas_call(kernel, out_shape=[jax.ShapeDtypeStruct(*typed(entry)) for...  435 us

profile of v5, /device:TPU:12, one launch (start us, length us, event | category | flops | bytes accessed | tf_op | source)
XLA Modules:
  0.0 449.6 jit_solution(17472293111289495411)
XLA Ops:
  0.6 0.5 fusion.3.freq
  1.2 435.2 %shard_map.152 = (bf16[3,4,128,1024]{3,2,1,0:T(8,128)(2,1)}, bf16[4,3,128,1024]{3,2,1,0:T(8,128)(2,1)}, bf16[4,2048,1024]{2,1,0:T(8,128)(2,1)}, bf16[3,2048,1024...) custom-call(bf16[128,2048]{1,0:T(8,128)(2,1)} %residual.1, ...), custom_call_target="tpu_custom_call" | custom-call | tf_op jit(solution)/shard_map/pallas_call | solution.py:1134
  436.4 7.4 %shard_map.153 = (f32[3,128,1024]{2,1,0:T(8,128)}, f32[1024,128]{1,0:T(8,128)}, f32[2,128,4096]{2,1,0:T(8,128)}, f32[4096,128]{1,0:T(8,128)}, f32[2,128]{1,0:T(2,128)}) custom-call(bf16[3,4,128,1024]{3,2,1,0:T(8,128)(2,1)} %get-tuple-element.20.ffn, bf16[4,3,128,1024]{3,2,1,0:T(8,128)(2,1)} %get-tuple-element.21.attention, f32[16,128]{1,0:T(8,128)} %get-tuple-element.22.gains), custom_call_target="tpu_custom_call" | custom-call | tf_op jit(solution)/shard_map/pallas_call | solution.py:1181
  443.8 1.3 slice_bitcast_fusion
  445.0 1.9 copy.19
  446.9 2.3 copy.20

commit v6 on v5

--- a/solution.py
+++ b/solution.py
@@ -2,6 +2,7 @@
 
 import jax
 import jax.numpy as jnp
+import numpy as np
 from jax import lax
 from jax.experimental import pallas as pl
 from jax.experimental.pallas import tpu as pltpu
@@ -911,193 +912,192 @@
     out.start()
     send_gains()
     qkv.step(1)
+    mask_grads()
+    norm()
+    qkv.cross_step(0)
     out.step(1)
     qkv.step(2)
-    qkv.cross_step(0)
+    ffn[2].start()
+    out.step(2)
+    qkv.cross_step(1)
+    grads.start()
+    qkv.step(3)
+    ffn_step(2, 3)
+    qkv.cross_step(2)
+    out.step(3)
+    ffn[0].start()
+    qkv.cross_step(3)
     out.cross_step(0)
-    ffn[0].start()
-    mask_grads()
-    out.step(2)
-    norm()
-    grads.start()
-    ffn[2].start()
-    qkv.cross_step(1)
-    qkv.step(3)
-    qkv.cross_step(2)
-    ffn_step(0, 3)
-    out.cross_step(1)
-    out.step(3)
-    ffn_step(0, 2)
-    qkv.cross_step(3)
     project(0)
-    ffn_step(0, 1)
     grads.step(1)
     project(1)
     project(2)
+    out.cross_step(1)
     out.cross_step(2)
+    out.cross_step(3)
+    ffn_step(2, 2)
     project(3)
     ffn[1].start()
+    ffn_step(2, 1)
     attend()
-    out.cross_step(3)
     join()
+    ffn_step(0, 2)
+    grads.step(2)
+    ffn_step(0, 1)
+    ffn_cross(2)
     mix()
     ffn_rows.start()
-    grads.step(2)
-    ffn_step(2, 1)
-    ffn_step(2, 3)
+    load_ffn(2)
+    ffn_step(0, 3)
+    ffn_step(1, 2)
+    ffn_step(1, 3)
+    grads.step(3)
+    ffn_cross(0)
+    load_rows(3)
     ffn_step(1, 1)
-    ffn_step(1, 3)
-    ffn_step(1, 2)
-    ffn_step(2, 2)
     ffn_rows.step(1)
-    load_rows(3)
     ffn_cross(1)
-    ffn_cross(0)
-    grads.step(3)
-    ffn_cross(2)
+    ffn_rows.step(2)
+    load_rows(2)
+    load_ffn(1)
     load_ffn(0)
-    load_ffn(2)
-    load_rows(2)
-    ffn_rows.step(2)
-    load_ffn(1)
+    ffn_rows.step(3)
     forward(3)
     forward(2)
-    ffn_rows.step(3)
     load_rows(1)
+    backward(2)
     forward(1)
-    backward(2)
     load_rows(0)
     forward(0)
     ffn_item()
     backward(0)
     red.step_c()
+    ffn_item()
+    ffn_item()
+    red.step_c()
+    red.step_y()
     backward(1)
-    ffn_item()
-    red.step_y()
-    backs.step_x(2)
-    ffn_item()
     red.step_c()
     backs.step_x(0)
     backs.step_z(0)
-    red.step_c()
+    red.step_y()
     ffn_item()
     ffn_item()
-    backward(3)
-    red.step_c()
+    red.step_c()
+    red.step_c()
+    backs.step_x(2)
     backs.step_x(1)
     backs.step_z(1)
     backs.step_z(2)
+    ffn_item()
     red.step_c()
     ffn_item()
     ffn_item()
     red.step_y()
-    red.step_y()
-    red.step_c()
-    red.step_c()
+    backward(3)
+    red.step_c()
+    backs.step_x(3)
     ffn_item()
+    red.step_c()
     ffn_item()
     red.step_c()
-    backs.step_x(3)
     red.step_y()
     ffn_item()
-    red.step_y()
     mix_grads()
-    red.step_c()
+    red.step_y()
+    red.step_c()
+    ffn_item()
+    add_chunk(0)
+    load_out()
+    red.step_y()
+    red.step_y()
+    add_chunk(1)
+    add_chunk(2)
+    red.step_y()
+    red.step_c()
+    red.step_c()
+    add_chunk(3)
+    load_rest()
+    red.step_y()
+    attended_back()
+    attention_item()
+    heads()
     red.step_c()
     for _ in range(3):
         red.step_y()
-    ffn_item()
-    ffn_item()
-    red.step_y()
-    add_chunk(0)
-    add_chunk(1)
-    red.step_c()
-    add_chunk(2)
-    load_out()
-    add_chunk(3)
-    load_rest()
-    red.step_y()
-    attended_back()
-    heads()
-    red.step_c()
-    attention_item()
+    attention_item()
+    attention_item()
+    red.step_c()
+    pl.semaphore_wait(free.at[4], beside)
+    attention_item()
+    red.step_y()
+    red.step_z()
+    attention_item()
+    red.step_y()
+    red.step_c()
+    red.step_c()
     adds.step_x(adds.done_x)
-    red.step_y()
-    red.step_c()
+    red.step_c()
+    red.step_z()
+    attention_item()
     step_adds()
-    attention_item()
-    red.step_c()
-    attention_item()
+    normed_back()
+    red.step_y()
+    attention_item()
+    red.step_z()
+    attention_item()
+    attention_item()
+    red.step_c()
+    attention_item()
+    red.step_y()
+    red.step_y()
+    red.step_c()
     adds.step_x(adds.done_x)
-    for _ in range(3):
-        attention_item()
-    red.step_c()
-    red.step_y()
-    attention_item()
-    red.step_c()
-    attention_item()
-    pl.semaphore_wait(free.at[4], beside)
+    attention_item()
+    red.step_c()
+    red.step_c()
+    red.step_y()
     step_adds()
     red.step_c()
-    red.step_y()
-    red.step_z()
-    red.step_c()
-    red.step_c()
-    attention_item()
-    normed_back()
-    red.step_y()
-    red.step_z()
-    red.step_c()
-    red.step_y()
-    adds.step_x(adds.done_x)
-    attention_item()
-    step_adds()
-    red.step_y()
-    red.step_z()
-    red.step_c()
-    red.step_y()
-    attention_item()
-    red.step_y()
-    red.step_y()
-    red.step_z()
-    input_back()
-    red.step_y()
-    red.step_z()
-    red.step_c()
-    attention_item()
-    red.step_c()
-    red.step_z()
-    red.step_y()
+    attention_item()
+    red.step_c()
     adds.step_x(adds.done_x)
     red.step_z()
-    red.step_y()
-    red.step_c()
-    attention_item()
     red.step_c()
     red.step_z()
-    red.step_y()
-    sum_gains()
+    step_adds()
     red.step_z()
-    attention_item()
-    red.step_c()
-    attention_item()
+    adds.step_x(adds.done_x)
+    attention_item()
+    red.step_y()
+    red.step_y()
+    red.step_z()
+    red.step_y()
+    red.step_c()
+    attention_item()
+    red.step_y()
+    attention_item()
+    input_back()
     red.step_z()
     red.step_z()
     red.step_y()
-    attention_item()
+    red.step_c()
+    red.step_c()
+    step_adds()
+    block_rows()
+    attention_item()
+    red.step_y()
+    red.step_y()
+    for _ in range(3):
+        red.step_z()
+    red.step_c()
     red.step_z()
     red.step_y()
-    red.step_c()
-    red.step_z()
-    step_adds()
-    red.step_c()
-    red.step_y()
-    red.step_y()
-    red.step_z()
-    red.step_z()
-    red.step_y()
-    block_rows()
-    red.step_z()
+    red.step_y()
+    sum_gains()
+    red.step_y()
+    for _ in range(3):
+        red.step_z()
     assert red.done_y == red.done_z == red.total and adds.done_z == n and backs.done_x == n
     net.recv(gain_x.at[1], x_sems.at[4])
     gain_out[...] = gain_x[0] + gain_x[1]
@@ -1105,7 +1105,10 @@
     net.drain()
 
 
-def finish_kernel(ffn, attention, gains, qkv_grad, out_grad, gate_up_grad, down_grad, gain_sums):
+def finish_kernel(
+    ffn, attention, gains, block_rows, input_rows,
+    qkv_grad, out_grad, gate_up_grad, down_grad, attn_gain_grad, ffn_gain_grad, block_out, input_grad,
+):
     q, n = pl.program_id(0), pl.num_programs(0)
     z = lax.axis_index("dp") // 4
     gate_up_grad[...] = ffn[0:2, 0].astype(F32)
@@ -1122,8 +1125,10 @@
     def _():
         out_grad[...] = total.T
 
-    gain_sums[0:1] = jnp.sum(gains[0:8], axis=0, keepdims=True)
-    gain_sums[1:2] = jnp.sum(gains[8:16], axis=0, keepdims=True)
+    attn_gain_grad[...] = jnp.sum(gains[0:8], axis=0, keepdims=True)
+    ffn_gain_grad[...] = jnp.sum(gains[8:16], axis=0, keepdims=True)
+    block_out[...] = block_rows[...]
+    input_grad[...] = input_rows[...]
 
 
 def call(kernel, collective_id, sends, locals_, vmem, outs, out_specs, scratch, sems, flags=0):
@@ -1147,9 +1152,8 @@
     group = seg_ids.shape[0]
     block, cols = w_qkv.shape[1:]
     part = w_gate_up.shape[2] // n
-    pairs = jnp.arange(LANES, dtype=jnp.int32) % (HD // 2)
-    freq = (ROPE_BASE ** (-(pairs.astype(F32) * 2.0 / HD)))[None]
-
+    pairs = np.arange(LANES) % (HD // 2)
+    freq = jnp.asarray(ROPE_BASE ** (-2.0 * pairs / HD), F32)[None]
     every = n * 2 * rows
     slots = SLOTS
     layer = call(
@@ -1178,28 +1182,38 @@
         w_gate_up, cotangent,
     )
     result, totals, block_out, input_grad, gain_grads = outputs[0], outputs[1], outputs[8], outputs[9], outputs[10]
-    qkv_grad, out_grad, gate_up_grad, down_grad, gain_sums = pl.pallas_call(
+    qkv_grad, out_grad, gate_up_grad, down_grad, attn_gain_grad, ffn_gain_grad, block_out, input_grad = pl.pallas_call(
         finish_kernel,
         grid=(n,),
         out_shape=[
             jax.ShapeDtypeStruct(entry, F32)
-            for entry in ((3, block, cols), (cols, block), (2, block, n * part), (n * part, block), (2, block))
-        ],
+            for entry in (
+                (3, block, cols), (cols, block), (2, block, n * part), (n * part, block), (1, block), (1, block)
+            )
+        ] + [jax.ShapeDtypeStruct((rows, width), BF16), jax.ShapeDtypeStruct((rows, width), F32)],
         in_specs=[
             pl.BlockSpec((3, 1, block, part), lambda q: (0, q, 0, 0)),
             pl.BlockSpec((1, 3, block, cols), lambda q: (q, 0, 0, 0)),
             pl.BlockSpec((16, block), lambda q: (0, 0)),
+            pl.BlockSpec((rows // n, width), lambda q: (q, 0)),
+            pl.BlockSpec((rows // n, width), lambda q: (q, 0)),
         ],
         out_specs=[
             pl.BlockSpec((1, block, cols), lambda q: (jnp.minimum(q, 2), 0, 0)),
             pl.BlockSpec((cols, block), lambda q: (0, 0)),
             pl.BlockSpec((2, block, part), lambda q: (0, 0, q)),
             pl.BlockSpec((part, block), lambda q: (q, 0)),
-            pl.BlockSpec((2, block), lambda q: (0, 0)),
+            pl.BlockSpec((1, block), lambda q: (0, 0)),
+            pl.BlockSpec((1, block), lambda q: (0, 0)),
+            pl.BlockSpec((rows // n, width), lambda q: (q, 0)),
+            pl.BlockSpec((rows // n, width), lambda q: (q, 0)),
         ],
         compiler_params=pltpu.CompilerParams(vmem_limit_bytes=LIMIT),
-    )(result, totals, gain_grads)
-    return block_out, input_grad, gain_sums[0], qkv_grad, out_grad, gain_sums[1], gate_up_grad, down_grad
+    )(result, totals, gain_grads, block_out, input_grad)
+    return (
+        block_out, input_grad, attn_gain_grad.reshape(block), qkv_grad, out_grad, ffn_gain_grad.reshape(block),
+        gate_up_grad, down_grad,
+    )
 
 
 def positions(segments):

time: 456 us -> 447 us (0.980)
  local copies, waits for them, and re-layouts: 5.45 us -> 0 us
  Pallas kernels: 443 us -> 438 us
    pallas_call x1, Pallas kernels: 435 us -> 429 us  [call(): pl.pallas_call(kernel, out_shape=[jax.ShapeDtypeStruct(*typed(entry)) for...]
where the time goes in v6:
time: 447 us; the launch traced here: 439 us
  Pallas kernels  438 us (98%)
    pallas_call x1, Pallas kernels, call(): pl.pallas_call(kernel, out_shape=[jax.ShapeDtypeStruct(*typed(entry)) for...  429 us

profile of v6, /device:TPU:12, one launch (start us, length us, event | category | flops | bytes accessed | tf_op | source)
XLA Modules:
  0.0 438.6 jit_solution(11784948172124463957)
XLA Ops:
  0.6 429.4 %shard_map.161 = (bf16[3,4,128,1024]{3,2,1,0:T(8,128)(2,1)}, bf16[4,3,128,1024]{3,2,1,0:T(8,128)(2,1)}, bf16[4,2048,1024]{2,1,0:T(8,128)(2,1)}, bf16[3,2048,1024...) custom-call(bf16[128,2048]{1,0:T(8,128)(2,1)} %residual.1, ...), custom_call_target="tpu_custom_call" | custom-call | tf_op jit(solution)/shard_map/pallas_call | solution.py:1139
  430.0 8.1 %shard_map.162 = (f32[3,128,1024]{2,1,0:T(8,128)}, f32[1024,128]{1,0:T(8,128)}, f32[2,128,4096]{2,1,0:T(8,128)}, f32[4096,128]{1,0:T(8,128)}, f32[1,128]{1,0:T(1...) custom-call(bf16[3,4,128,1024]{3,2,1,0:T(8,128)(2,1)} %get-tuple-element.21.ffn, ...), custom_call_target="tpu_custom_call" | custom-call | tf_op jit(solution)/shard_map/pallas_call | solution.py:1185

commit v7 on v6

--- a/solution.py
+++ b/solution.py
@@ -139,8 +139,10 @@
         for sign in (1, -1):
             block = net.z - s * sign
             valid = jnp.logical_and(block >= 0, block < net.n)
+            block = jnp.where(valid, block, net.z)
             nxt = net.z + sign
             more = jnp.logical_and(nxt >= 0, nxt < net.n)
+            nxt = jnp.where(more, nxt, net.z)
             here = self.at(net.place(block, net.y, net.c))
 
             @pl.when(valid)
@@ -165,6 +167,7 @@
         for sign in (1, -1):
             block = net.z - s * sign
             valid = jnp.logical_and(block >= 0, block < net.n)
+            block = jnp.where(valid, block, net.z)
             there = self.at(net.place(block, 1 - net.y, net.c))
 
             @pl.when(valid)
@@ -232,8 +235,10 @@
         for sign in (1, -1):
             block = net.z - s * sign
             valid = jnp.logical_and(block >= 0, block < net.n)
+            block = jnp.where(valid, block, net.z)
             nxt = net.z + sign
             more = jnp.logical_and(nxt >= 0, nxt < net.n)
+            nxt = jnp.where(more, nxt, net.z)
             here = self.at(block, net.x)
 
             @pl.when(valid)

time: 447 us -> 447 us (level)
  no operation moved by 1% of the time
where the time goes in v7:
time: 447 us; the launch traced here: 439 us
  Pallas kernels  438 us (98%)
    pallas_call x1, Pallas kernels, call(): pl.pallas_call(kernel, out_shape=[jax.ShapeDtypeStruct(*typed(entry)) for...  429 us

profile of v7, /device:TPU:12, one launch (start us, length us, event | category | flops | bytes accessed | tf_op | source)
XLA Modules:
  0.0 438.6 jit_solution(10225076294503697620)
XLA Ops:
  0.6 429.4 %shard_map.161 = (bf16[3,4,128,1024]{3,2,1,0:T(8,128)(2,1)}, bf16[4,3,128,1024]{3,2,1,0:T(8,128)(2,1)}, bf16[4,2048,1024]{2,1,0:T(8,128)(2,1)}, bf16[3,2048,1024...) custom-call(bf16[128,2048]{1,0:T(8,128)(2,1)} %residual.1, ...), custom_call_target="tpu_custom_call" | custom-call | tf_op jit(solution)/shard_map/pallas_call | solution.py:1144
  430.1 8.1 %shard_map.162 = (f32[3,128,1024]{2,1,0:T(8,128)}, f32[1024,128]{1,0:T(8,128)}, f32[2,128,4096]{2,1,0:T(8,128)}, f32[4096,128]{1,0:T(8,128)}, f32[1,128]{1,0:T(1...) custom-call(bf16[3,4,128,1024]{3,2,1,0:T(8,128)(2,1)} %get-tuple-element.21.ffn, ...), custom_call_target="tpu_custom_call" | custom-call | tf_op jit(solution)/shard_map/pallas_call | solution.py:1190
